TPU v7x, 32 devices: a whole 2x2x4 slice. The times are simulated.
32 devices in a mesh: survey: 2 (over x), sub: 8 (over z, y), freq: 2 (over core).
Axes of the slice: x: 2, y: 2, z: 4, core: 2. Of those that a mesh axis runs over, the one named last changes fastest.
Arguments:
- trace_map: bfloat16 [4, 32, 2, 768, 768], P('freq', ('survey', 'sub')), parts along dimension 1, may hold values from -0.109375 to 0.109375
- interior_map: bfloat16 [4, 32, 2, 768, 768], P('freq', ('survey', 'sub')), parts along dimension 1, may hold values from -0.15625 to 0.15625
- excitation: bfloat16 [4, 32, 768, 2, 128], P('freq', ('survey', 'sub')), parts along dimension 1, may hold values from -6 to 6
- receiver_data: bfloat16 [4, 32, 768, 2, 128], P('freq', ('survey', 'sub')), parts along dimension 1, may hold values from -6 to 6
- shot_index: int32 [128], P('survey'), parts along dimension 0, may hold values from 0 to 127, as said below
Outputs:
- image: float32 [32, 768, 768], P(('survey', 'sub'), 'freq'), parts along dimension 0
There are 2 independent parts, one for each index of `survey`. A program takes and returns all parts, laid end to end along the dimension named above; each array names one. Nothing has to cross between parts.
Inputs may be any that keep to these rules, and one draw needn't show every extreme that they name: `shot_index`: 64 distinct shot numbers in shuffled order; 0 and 127 are always among them.
All inputs are finite; a program needn't handle non-finite values.
Results may differ from a plain program's by a relative error of at most 0.0094.
Values may be sent and summed in bfloat16 or wider, within the bound.
No kernel may reach another device: no remote copies, remote signals or barrier semaphores. Data moves between devices by JAX's collectives and lax.ppermute only.
A program may use at most 128 MiB of HBM per device.

v0:
```python
import jax
import jax.numpy as jnp
from jax import lax
from jax.sharding import PartitionSpec as P

GY = 4
TICKS = 6


def from_behind(x, axis, by):
    count = lax.axis_size(axis)
    return lax.ppermute(x, axis, [(i, (i + by) % count) for i in range(count)])


def forward_apply(maps, front, shots):
    product = jnp.einsum("fsckm,fsmn->fsckn", maps, front, preferred_element_type=jnp.float32)
    real_part = product[:, :, 0, :, :shots] - product[:, :, 1, :, shots:]
    imag_part = product[:, :, 0, :, shots:] + product[:, :, 1, :, :shots]
    return jnp.concatenate([real_part, imag_part], axis=-1)


def adjoint_apply(maps, front, shots):
    product = jnp.einsum("fsckm,fskn->fscmn", maps, front, preferred_element_type=jnp.float32)
    real_part = product[:, :, 0, :, :shots] + product[:, :, 1, :, shots:]
    imag_part = product[:, :, 0, :, shots:] - product[:, :, 1, :, :shots]
    return jnp.concatenate([real_part, imag_part], axis=-1)


def pick_shots(table, chooser, shape_out):
    picked = jnp.einsum("fsxcb,bn->fsxcn", table, chooser, preferred_element_type=jnp.float32)
    return picked.astype(jnp.bfloat16).reshape(shape_out)


def as_mask(flags):
    return flags.astype(jnp.bfloat16)[None, :, None, None]


def per_device(trace_map, interior_map, excitation, receiver_data, shot_index):
    freq_local = trace_map.shape[0]
    sub_local = trace_map.shape[1]
    width = trace_map.shape[3]
    shots = shot_index.shape[0]
    bank_size = excitation.shape[4]
    front_shape = (freq_local, sub_local, width, 2 * shots)
    chooser = (
        lax.broadcasted_iota(jnp.int32, (bank_size, shots), 0) == shot_index[None, :]
    ).astype(jnp.bfloat16)
    sources = pick_shots(excitation, chooser, front_shape)
    data_front = pick_shots(receiver_data, chooser, front_shape)
    device = lax.axis_index("sub")
    total_subs = sub_local * lax.axis_size("sub")
    grid_rows = total_subs // GY
    place = (device * sub_local + jnp.arange(sub_local, dtype=jnp.int32) + GY + 1) % total_subs
    column = place % GY
    grid_row = place // GY
    keep_left = as_mask(column != 0)
    keep_right = as_mask(column != GY - 1)
    keep_up = as_mask(grid_row != 0)
    keep_down = as_mask(grid_row != grid_rows - 1)
    reach = GY // sub_local
    forward = sources
    adjoint = data_front
    for sweep_step in range(TICKS):
        edge_left = from_behind(forward[:, sub_local - 1 :], "sub", 1)
        left_in = jnp.concatenate([edge_left, forward[:, : sub_local - 1]], axis=1) * keep_left
        up_in = from_behind(forward, "sub", reach) * keep_up
        forward_in = (left_in.astype(jnp.float32) + up_in.astype(jnp.float32)).astype(jnp.bfloat16)
        edge_right = from_behind(adjoint[:, :1], "sub", -1)
        right_in = jnp.concatenate([adjoint[:, 1:], edge_right], axis=1) * keep_right
        down_in = from_behind(adjoint, "sub", -reach) * keep_down
        adjoint_in = (right_in.astype(jnp.float32) + down_in.astype(jnp.float32)).astype(
            jnp.bfloat16
        )
        forward = (
            sources.astype(jnp.float32) + forward_apply(trace_map, forward_in, shots)
        ).astype(jnp.bfloat16)
        adjoint = (
            data_front.astype(jnp.float32) + adjoint_apply(trace_map, adjoint_in, shots)
        ).astype(jnp.bfloat16)
    wave = forward_apply(interior_map, forward, shots).astype(jnp.bfloat16)
    back = forward_apply(interior_map, adjoint, shots).astype(jnp.bfloat16)
    total_freqs = freq_local * lax.axis_size("freq")
    scale = (2.0 * shots * total_freqs) ** (-0.5)
    partial_image = (
        jnp.einsum("fsam,fscm->sac", wave, back, preferred_element_type=jnp.float32) * scale
    )
    image = lax.psum_scatter(partial_image, "freq", scatter_dimension=1, tiled=True)
    return image


def solution(mesh):
    placed = (
        P("freq", ("survey", "sub"), None, None, None),
        P("freq", ("survey", "sub"), None, None, None),
        P("freq", ("survey", "sub"), None, None, None),
        P("freq", ("survey", "sub"), None, None, None),
        P("survey"),
    )
    return jax.shard_map(
        per_device,
        mesh=mesh,
        in_specs=placed,
        out_specs=P(("survey", "sub"), "freq", None),
        check_vma=False,
    )
```

profile of v0, /device:TPU:21, one launch (start us, length us, event | category | flops | bytes accessed | tf_op | source)
XLA Modules:
  0.0 301.1 jit_solution(2695559698479689026)
XLA Ops:
  12.8 3.9 %collective-permute-start = (bf16[2,1,768,128]{2,3,1,0:T(8,128)(2,1)}, bf16[2,1,768,128]{2,3,1,0:T(8,128)(2,1)}, u32[]{:S(2)}, u32[]{:S(2)}) collective-permute-start(bf16[2,1,768,128]{2,3,1,0:T(8,128)(2,1)} %get-tuple-element.47), channel_id=1, source_target_pairs={{0,2},{2,4},{4,6},{6,8},{8,10},{10,12},{12,14},{14,0},{1,3},{3,5},... | collective-permute-start | bytes 1179656 | tf_op jit(solution)/shard_map/ppermute | solution.py:12
  16.8 19.5 %collective-permute-done.12 = bf16[2,1,768,128]{2,3,1,0:T(8,128)(2,1)} collective-permute-done((bf16[2,1,768,128]{2,3,1,0:T(8,128)(2,1)S(1)}, bf16[2,1,768,128]{2,3,1,0:T(8,128)(2,1)}, u32[]{:S(2)}, u32[]{:S(2)}) %collective-permute-start.12) | collective-permute-done | bytes 393248 | tf_op jit(solution)/shard_map/ppermute | solution.py:12
  36.4 5.7 %convolution_bitcast_fusion.6 = f32[2,2,2,768,128]{3,4,2,1,0:T(8,128)S(1)} fusion(bf16[2,2,2,768,768]{4,3,2,1,0:T(8,128)(2,1)} %param.5, bf16[2,1,768,128]{2,3,1,0:T(8,128)(2,1)} %collective-permute-done.12, bf16[2,1,768,128]{2,3,1,0:T(8,128)(2,1)S(1)} %get-tuple-element.35, bf16[2,2,768,128]{2,3,1,0:T(8,128)(2,1)} %collective-permute-done.13, ...), kind=kOutput, calls=%fused_computation.19 | convolution fusion | flops 1212678144 | bytes 14155784 | tf_op jit(solution)/shard_map/fsckm,fskn->fscmn/dot_general | solution.py:23
  42.8 11.3 %collective-permute-done = bf16[2,1,768,128]{2,3,1,0:T(8,128)(2,1)} collective-permute-done((bf16[2,1,768,128]{2,3,1,0:T(8,128)(2,1)}, bf16[2,1,768,128]{2,3,1,0:T(8,128)(2,1)}, u32[]{:S(2)}, u32[]{:S(2)}) %collective-permute-start) | collective-permute-done | bytes 393248 | tf_op jit(solution)/shard_map/ppermute | solution.py:12
  54.1 4.2 %convolution_bitcast_fusion.13 = f32[2,2,2,768,128]{3,4,2,1,0:T(8,128)S(1)} fusion(bf16[2,2,2,768,768]{4,3,2,1,0:T(8,128)(2,1)S(1)} %bitcast.219, bf16[2,1,768,128]{2,3,1,0:T(8,128)(2,1)S(1)} %get-tuple-element.48, bf16[2,1,768,128]{2,3,1,0:T(8,128)(2,1)} %collective-permute-done, bf16[2,2,768,128]{2,3,1,0:T(8,128)(2,1)S(1)} %collective-permute-done.1, ...), kind=kOutput, calls=%fused_computation.26 | convolution fusion | flops 1212678144 | bytes 14155784 | tf_op jit(solution)/shard_map/fsckm,fsmn->fsckn/dot_general | solution.py:16
  58.9 4.3 %collective-permute-start.2 = (bf16[2,1,768,128]{2,3,1,0:T(8,128)(2,1)S(1)}, bf16[2,1,768,128]{2,3,1,0:T(8,128)(2,1)S(1)}, u32[]{:S(2)}, u32[]{:S(2)}) collective-permute-start(bf16[2,1,768,128]{2,3,1,0:T(8,128)(2,1)S(1)} %get-tuple-element.45), channel_id=1, source_target_pairs={{0,2},{2,4},{4,6},{6,8},{8,10},{10,12},{12,14},{14,0},{1,3},{3,5},... | collective-permute-start | bytes 1179656 | tf_op jit(solution)/shard_map/ppermute | solution.py:12
  63.2 15.3 %collective-permute-done.14 = bf16[2,1,768,128]{2,3,1,0:T(8,128)(2,1)S(1)} collective-permute-done((bf16[2,1,768,128]{2,3,1,0:T(8,128)(2,1)S(1)}, bf16[2,1,768,128]{2,3,1,0:T(8,128)(2,1)S(1)}, u32[]{:S(2)}, u32[]{:S(2)}) %collective-permute-start.14) | collective-permute-done | bytes 393248 | tf_op jit(solution)/shard_map/ppermute | solution.py:12
  83.7 14.1 %collective-permute-done.2 = bf16[2,1,768,128]{2,3,1,0:T(8,128)(2,1)S(1)} collective-permute-done((bf16[2,1,768,128]{2,3,1,0:T(8,128)(2,1)S(1)}, bf16[2,1,768,128]{2,3,1,0:T(8,128)(2,1)S(1)}, u32[]{:S(2)}, u32[]{:S(2)}) %collective-permute-start.2) | collective-permute-done | bytes 393248 | tf_op jit(solution)/shard_map/ppermute | solution.py:12
  101.6 3.8 %collective-permute-start.4 = (bf16[2,1,768,128]{2,3,1,0:T(8,128)(2,1)S(1)}, bf16[2,1,768,128]{2,3,1,0:T(8,128)(2,1)S(1)}, u32[]{:S(2)}, u32[]{:S(2)}) collective-permute-start(bf16[2,1,768,128]{2,3,1,0:T(8,128)(2,1)S(1)} %get-tuple-element.43), channel_id=1, source_target_pairs={{0,2},{2,4},{4,6},{6,8},{8,10},{10,12},{12,14},{14,0},{1,3},{3,5},... | collective-permute-start | bytes 1179656 | tf_op jit(solution)/shard_map/ppermute | solution.py:12
  105.4 15.3 %collective-permute-done.16 = bf16[2,1,768,128]{2,3,1,0:T(8,128)(2,1)S(1)} collective-permute-done((bf16[2,1,768,128]{2,3,1,0:T(8,128)(2,1)S(1)}, bf16[2,1,768,128]{2,3,1,0:T(8,128)(2,1)S(1)}, u32[]{:S(2)}, u32[]{:S(2)}) %collective-permute-start.16) | collective-permute-done | bytes 393248 | tf_op jit(solution)/shard_map/ppermute | solution.py:12
  126.0 14.0 %collective-permute-done.4 = bf16[2,1,768,128]{2,3,1,0:T(8,128)(2,1)S(1)} collective-permute-done((bf16[2,1,768,128]{2,3,1,0:T(8,128)(2,1)S(1)}, bf16[2,1,768,128]{2,3,1,0:T(8,128)(2,1)S(1)}, u32[]{:S(2)}, u32[]{:S(2)}) %collective-permute-start.4) | collective-permute-done | bytes 393248 | tf_op jit(solution)/shard_map/ppermute | solution.py:12
  143.8 3.6 %collective-permute-start.6 = (bf16[2,1,768,128]{2,3,1,0:T(8,128)(2,1)S(1)}, bf16[2,1,768,128]{2,3,1,0:T(8,128)(2,1)S(1)}, u32[]{:S(2)}, u32[]{:S(2)}) collective-permute-start(bf16[2,1,768,128]{2,3,1,0:T(8,128)(2,1)S(1)} %get-tuple-element.41), channel_id=1, source_target_pairs={{0,2},{2,4},{4,6},{6,8},{8,10},{10,12},{12,14},{14,0},{1,3},{3,5},... | collective-permute-start | bytes 1179656 | tf_op jit(solution)/shard_map/ppermute | solution.py:12
  147.5 15.5 %collective-permute-done.18 = bf16[2,1,768,128]{2,3,1,0:T(8,128)(2,1)S(1)} collective-permute-done((bf16[2,1,768,128]{2,3,1,0:T(8,128)(2,1)S(1)}, bf16[2,1,768,128]{2,3,1,0:T(8,128)(2,1)S(1)}, u32[]{:S(2)}, u32[]{:S(2)}) %collective-permute-start.18) | collective-permute-done | bytes 393248 | tf_op jit(solution)/shard_map/ppermute | solution.py:12
  168.3 14.0 %collective-permute-done.6 = bf16[2,1,768,128]{2,3,1,0:T(8,128)(2,1)S(1)} collective-permute-done((bf16[2,1,768,128]{2,3,1,0:T(8,128)(2,1)S(1)}, bf16[2,1,768,128]{2,3,1,0:T(8,128)(2,1)S(1)}, u32[]{:S(2)}, u32[]{:S(2)}) %collective-permute-start.6) | collective-permute-done | bytes 393248 | tf_op jit(solution)/shard_map/ppermute | solution.py:12
  186.0 3.6 %collective-permute-start.8 = (bf16[2,1,768,128]{2,3,1,0:T(8,128)(2,1)S(1)}, bf16[2,1,768,128]{2,3,1,0:T(8,128)(2,1)S(1)}, u32[]{:S(2)}, u32[]{:S(2)}) collective-permute-start(bf16[2,1,768,128]{2,3,1,0:T(8,128)(2,1)S(1)} %get-tuple-element.39), channel_id=1, source_target_pairs={{0,2},{2,4},{4,6},{6,8},{8,10},{10,12},{12,14},{14,0},{1,3},{3,5},... | collective-permute-start | bytes 1179656 | tf_op jit(solution)/shard_map/ppermute | solution.py:12
  189.7 15.5 %collective-permute-done.20 = bf16[2,1,768,128]{2,3,1,0:T(8,128)(2,1)S(1)} collective-permute-done((bf16[2,1,768,128]{2,3,1,0:T(8,128)(2,1)S(1)}, bf16[2,1,768,128]{2,3,1,0:T(8,128)(2,1)S(1)}, u32[]{:S(2)}, u32[]{:S(2)}) %collective-permute-start.20) | collective-permute-done | bytes 393248 | tf_op jit(solution)/shard_map/ppermute | solution.py:12
  207.1 3.3 %collective-permute-start.23 = (bf16[2,2,768,128]{2,3,1,0:T(8,128)(2,1)S(1)}, bf16[2,2,768,128]{2,3,1,0:T(8,128)(2,1)}, u32[]{:S(2)}, u32[]{:S(2)}) collective-permute-start(bf16[2,2,768,128]{2,3,1,0:T(8,128)(2,1)S(1)} %fusion.10), channel_id=1, source_target_pairs={{0,12},{2,14},{4,0},{6,2},{8,4},{10,6},{12,8},{14,10},{1,13},{3,15... | collective-permute-start | bytes 2359304 | tf_op jit(solution)/shard_map/ppermute | solution.py:12
  210.7 13.8 %collective-permute-done.8 = bf16[2,1,768,128]{2,3,1,0:T(8,128)(2,1)S(1)} collective-permute-done((bf16[2,1,768,128]{2,3,1,0:T(8,128)(2,1)S(1)}, bf16[2,1,768,128]{2,3,1,0:T(8,128)(2,1)S(1)}, u32[]{:S(2)}, u32[]{:S(2)}) %collective-permute-start.8) | collective-permute-done | bytes 393248 | tf_op jit(solution)/shard_map/ppermute | solution.py:12
  228.3 3.8 %collective-permute-start.10 = (bf16[2,1,768,128]{2,3,1,0:T(8,128)(2,1)S(1)}, bf16[2,1,768,128]{2,3,1,0:T(8,128)(2,1)}, u32[]{:S(2)}, u32[]{:S(2)}) collective-permute-start(bf16[2,1,768,128]{2,3,1,0:T(8,128)(2,1)S(1)} %get-tuple-element.37), channel_id=1, source_target_pairs={{0,2},{2,4},{4,6},{6,8},{8,10},{10,12},{12,14},{14,0},{1,3},{3,5},... | collective-permute-start | bytes 1179656 | tf_op jit(solution)/shard_map/ppermute | solution.py:12
  232.0 15.4 %collective-permute-done.22 = bf16[2,1,768,128]{2,3,1,0:T(8,128)(2,1)S(1)} collective-permute-done((bf16[2,1,768,128]{2,3,1,0:T(8,128)(2,1)S(1)}, bf16[2,1,768,128]{2,3,1,0:T(8,128)(2,1)S(1)}, u32[]{:S(2)}, u32[]{:S(2)}) %collective-permute-start.22) | collective-permute-done | bytes 393248 | tf_op jit(solution)/shard_map/ppermute | solution.py:12
  247.4 5.6 %convolution_bitcast_fusion.1 = f32[2,2,2,768,128]{3,4,1,0,2:T(8,128)S(1)} fusion(bf16[2,1,768,128]{2,3,1,0:T(8,128)(2,1)S(1)} %collective-permute-done.22, bf16[2,1,768,128]{2,3,1,0:T(8,128)(2,1)S(1)} %get-tuple-element.25, bf16[2,2,768,128]{2,3,1,0:T(8,128)(2,1)} %collective-permute-done.23, bf16[2]{0:T(256)(128)(2,1)S(1)} %get-tuple-element.49, ...), kind=kOutput, calls=%fused_computation.14 | convolution fusion | flops 1212678144 | bytes 14155784 | tf_op jit(solution)/shard_map/fsckm,fskn->fscmn/dot_general | solution.py:23
  257.3 8.9 %collective-permute-done.10 = bf16[2,1,768,128]{2,3,1,0:T(8,128)(2,1)} collective-permute-done((bf16[2,1,768,128]{2,3,1,0:T(8,128)(2,1)S(1)}, bf16[2,1,768,128]{2,3,1,0:T(8,128)(2,1)}, u32[]{:S(2)}, u32[]{:S(2)}) %collective-permute-start.10) | collective-permute-done | bytes 393248 | tf_op jit(solution)/shard_map/ppermute | solution.py:12
  266.2 6.1 %convolution_bitcast_fusion.8 = f32[2,2,2,768,128]{3,4,1,0,2:T(8,128)S(1)} fusion(bf16[2,1,768,128]{2,3,1,0:T(8,128)(2,1)S(1)} %get-tuple-element.38, bf16[2,1,768,128]{2,3,1,0:T(8,128)(2,1)} %collective-permute-done.10, bf16[2,2,768,128]{2,3,1,0:T(8,128)(2,1)} %collective-permute-done.11, bf16[2]{0:T(256)(128)(2,1)S(1)} %get-tuple-element.51, ...), kind=kOutput, calls=%fused_computation.21 | convolution fusion | flops 1212678144 | bytes 14155784 | tf_op jit(solution)/shard_map/fsckm,fsmn->fsckn/dot_general | solution.py:16
  279.0 15.3 %reduce-scatter.2.cloned.1.call-done = f32[2,384,768]{2,1,0:T(8,128)} async-done(((f32[2,768,768]{2,1,0:T(8,128)}), f32[2,384,768]{2,1,0:T(8,128)}) %reduce-scatter.2.cloned.1.call-update) | async-done | bytes 2359312 | tf_op jit(solution)/shard_map/reduce_scatter | solution.py:87
  (108 shorter events, 51.4 us)
Async XLA Ops:
  6.5 287.7 %reduce-scatter.2.cloned.1.call-start = ((), (), s32[]{:S(2)}) async-start(), calls=%async_computation.1 | async-start | bytes 7077888 | tf_op jit(solution)/shard_map/reduce_scatter | solution.py:87
  9.4 26.9 %collective-permute-start.13 = (bf16[2,2,768,128]{2,3,1,0:T(8,128)(2,1)S(1)}, bf16[2,2,768,128]{2,3,1,0:T(8,128)(2,1)}, u32[]{:S(2)}, u32[]{:S(2)}) collective-permute-start(bf16[2,2,768,128]{2,3,1,0:T(8,128)(2,1)S(1)} %bitcast.213), channel_id=1, source_target_pairs={{0,12},{2,14},{4,0},{6,2},{8,4},{10,6},{12,8},{14,10},{1,13},{3,15... | collective-permute-start | bytes 2359304 | tf_op jit(solution)/shard_map/ppermute | solution.py:12
  10.7 43.4 %collective-permute-start.1 = (bf16[2,2,768,128]{2,3,1,0:T(8,128)(2,1)S(1)}, bf16[2,2,768,128]{2,3,1,0:T(8,128)(2,1)S(1)}, u32[]{:S(2)}, u32[]{:S(2)}) collective-permute-start(bf16[2,2,768,128]{2,3,1,0:T(8,128)(2,1)S(1)} %bitcast.210), channel_id=1, source_target_pairs={{0,4},{2,6},{4,8},{6,10},{8,12},{10,14},{12,0},{14,2},{1,5},{3,7},... | collective-permute-start | bytes 2359304 | tf_op jit(solution)/shard_map/ppermute | solution.py:12
  12.8 41.2 %collective-permute-start = (bf16[2,1,768,128]{2,3,1,0:T(8,128)(2,1)}, bf16[2,1,768,128]{2,3,1,0:T(8,128)(2,1)}, u32[]{:S(2)}, u32[]{:S(2)}) collective-permute-start(bf16[2,1,768,128]{2,3,1,0:T(8,128)(2,1)} %get-tuple-element.47), channel_id=1, source_target_pairs={{0,2},{2,4},{4,6},{6,8},{8,10},{10,12},{12,14},{14,0},{1,3},{3,5},... | collective-permute-start | bytes 1179656 | tf_op jit(solution)/shard_map/ppermute | solution.py:12
  42.5 36.0 %collective-permute-start.15 = (bf16[2,2,768,128]{2,3,1,0:T(8,128)(2,1)S(1)}, bf16[2,2,768,128]{2,3,1,0:T(8,128)(2,1)S(1)}, u32[]{:S(2)}, u32[]{:S(2)}) collective-permute-start(bf16[2,2,768,128]{2,3,1,0:T(8,128)(2,1)S(1)} %fusion.6), channel_id=1, source_target_pairs={{0,12},{2,14},{4,0},{6,2},{8,4},{10,6},{12,8},{14,10},{1,13},{3,15... | collective-permute-start | bytes 2359304 | tf_op jit(solution)/shard_map/ppermute | solution.py:12
  42.8 35.8 %collective-permute-start.14 = (bf16[2,1,768,128]{2,3,1,0:T(8,128)(2,1)S(1)}, bf16[2,1,768,128]{2,3,1,0:T(8,128)(2,1)S(1)}, u32[]{:S(2)}, u32[]{:S(2)}) collective-permute-start(bf16[2,1,768,128]{2,3,1,0:T(8,128)(2,1)S(1)} %get-tuple-element.34), channel_id=1, source_target_pairs={{0,14},{2,0},{4,2},{6,4},{8,6},{10,8},{12,10},{14,12},{1,15},{3,1}... | collective-permute-start | bytes 1179656 | tf_op jit(solution)/shard_map/ppermute | solution.py:12
  58.8 39.1 %collective-permute-start.3 = (bf16[2,2,768,128]{2,3,1,0:T(8,128)(2,1)S(1)}, bf16[2,2,768,128]{2,3,1,0:T(8,128)(2,1)S(1)}, u32[]{:S(2)}, u32[]{:S(2)}) collective-permute-start(bf16[2,2,768,128]{2,3,1,0:T(8,128)(2,1)S(1)} %fusion), channel_id=1, source_target_pairs={{0,4},{2,6},{4,8},{6,10},{8,12},{10,14},{12,0},{14,2},{1,5},{3,7},... | collective-permute-start | bytes 2359304 | tf_op jit(solution)/shard_map/ppermute | solution.py:12
  58.9 39.0 %collective-permute-start.2 = (bf16[2,1,768,128]{2,3,1,0:T(8,128)(2,1)S(1)}, bf16[2,1,768,128]{2,3,1,0:T(8,128)(2,1)S(1)}, u32[]{:S(2)}, u32[]{:S(2)}) collective-permute-start(bf16[2,1,768,128]{2,3,1,0:T(8,128)(2,1)S(1)} %get-tuple-element.45), channel_id=1, source_target_pairs={{0,2},{2,4},{4,6},{6,8},{8,10},{10,12},{12,14},{14,0},{1,3},{3,5},... | collective-permute-start | bytes 1179656 | tf_op jit(solution)/shard_map/ppermute | solution.py:12
  80.5 40.3 %collective-permute-start.17 = (bf16[2,2,768,128]{2,3,1,0:T(8,128)(2,1)S(1)}, bf16[2,2,768,128]{2,3,1,0:T(8,128)(2,1)S(1)}, u32[]{:S(2)}, u32[]{:S(2)}) collective-permute-start(bf16[2,2,768,128]{2,3,1,0:T(8,128)(2,1)S(1)} %fusion.7), channel_id=1, source_target_pairs={{0,12},{2,14},{4,0},{6,2},{8,4},{10,6},{12,8},{14,10},{1,13},{3,15... | collective-permute-start | bytes 2359304 | tf_op jit(solution)/shard_map/ppermute | solution.py:12
  83.7 37.1 %collective-permute-start.16 = (bf16[2,1,768,128]{2,3,1,0:T(8,128)(2,1)S(1)}, bf16[2,1,768,128]{2,3,1,0:T(8,128)(2,1)S(1)}, u32[]{:S(2)}, u32[]{:S(2)}) collective-permute-start(bf16[2,1,768,128]{2,3,1,0:T(8,128)(2,1)S(1)} %get-tuple-element.32), channel_id=1, source_target_pairs={{0,14},{2,0},{4,2},{6,4},{8,6},{10,8},{12,10},{14,12},{1,15},{3,1}... | collective-permute-start | bytes 1179656 | tf_op jit(solution)/shard_map/ppermute | solution.py:12
  101.5 38.6 %collective-permute-start.5 = (bf16[2,2,768,128]{2,3,1,0:T(8,128)(2,1)S(1)}, bf16[2,2,768,128]{2,3,1,0:T(8,128)(2,1)S(1)}, u32[]{:S(2)}, u32[]{:S(2)}) collective-permute-start(bf16[2,2,768,128]{2,3,1,0:T(8,128)(2,1)S(1)} %fusion.1), channel_id=1, source_target_pairs={{0,4},{2,6},{4,8},{6,10},{8,12},{10,14},{12,0},{14,2},{1,5},{3,7},... | collective-permute-start | bytes 2359304 | tf_op jit(solution)/shard_map/ppermute | solution.py:12
  101.6 38.5 %collective-permute-start.4 = (bf16[2,1,768,128]{2,3,1,0:T(8,128)(2,1)S(1)}, bf16[2,1,768,128]{2,3,1,0:T(8,128)(2,1)S(1)}, u32[]{:S(2)}, u32[]{:S(2)}) collective-permute-start(bf16[2,1,768,128]{2,3,1,0:T(8,128)(2,1)S(1)} %get-tuple-element.43), channel_id=1, source_target_pairs={{0,2},{2,4},{4,6},{6,8},{8,10},{10,12},{12,14},{14,0},{1,3},{3,5},... | collective-permute-start | bytes 1179656 | tf_op jit(solution)/shard_map/ppermute | solution.py:12
  122.7 40.3 %collective-permute-start.19 = (bf16[2,2,768,128]{2,3,1,0:T(8,128)(2,1)S(1)}, bf16[2,2,768,128]{2,3,1,0:T(8,128)(2,1)S(1)}, u32[]{:S(2)}, u32[]{:S(2)}) collective-permute-start(bf16[2,2,768,128]{2,3,1,0:T(8,128)(2,1)S(1)} %fusion.8), channel_id=1, source_target_pairs={{0,12},{2,14},{4,0},{6,2},{8,4},{10,6},{12,8},{14,10},{1,13},{3,15... | collective-permute-start | bytes 2359304 | tf_op jit(solution)/shard_map/ppermute | solution.py:12
  126.0 37.0 %collective-permute-start.18 = (bf16[2,1,768,128]{2,3,1,0:T(8,128)(2,1)S(1)}, bf16[2,1,768,128]{2,3,1,0:T(8,128)(2,1)S(1)}, u32[]{:S(2)}, u32[]{:S(2)}) collective-permute-start(bf16[2,1,768,128]{2,3,1,0:T(8,128)(2,1)S(1)} %get-tuple-element.30), channel_id=1, source_target_pairs={{0,14},{2,0},{4,2},{6,4},{8,6},{10,8},{12,10},{14,12},{1,15},{3,1}... | collective-permute-start | bytes 1179656 | tf_op jit(solution)/shard_map/ppermute | solution.py:12
  143.7 38.6 %collective-permute-start.7 = (bf16[2,2,768,128]{2,3,1,0:T(8,128)(2,1)S(1)}, bf16[2,2,768,128]{2,3,1,0:T(8,128)(2,1)S(1)}, u32[]{:S(2)}, u32[]{:S(2)}) collective-permute-start(bf16[2,2,768,128]{2,3,1,0:T(8,128)(2,1)S(1)} %fusion.2), channel_id=1, source_target_pairs={{0,4},{2,6},{4,8},{6,10},{8,12},{10,14},{12,0},{14,2},{1,5},{3,7},... | collective-permute-start | bytes 2359304 | tf_op jit(solution)/shard_map/ppermute | solution.py:12
  143.8 38.5 %collective-permute-start.6 = (bf16[2,1,768,128]{2,3,1,0:T(8,128)(2,1)S(1)}, bf16[2,1,768,128]{2,3,1,0:T(8,128)(2,1)S(1)}, u32[]{:S(2)}, u32[]{:S(2)}) collective-permute-start(bf16[2,1,768,128]{2,3,1,0:T(8,128)(2,1)S(1)} %get-tuple-element.41), channel_id=1, source_target_pairs={{0,2},{2,4},{4,6},{6,8},{8,10},{10,12},{12,14},{14,0},{1,3},{3,5},... | collective-permute-start | bytes 1179656 | tf_op jit(solution)/shard_map/ppermute | solution.py:12
  164.9 40.3 %collective-permute-start.21 = (bf16[2,2,768,128]{2,3,1,0:T(8,128)(2,1)S(1)}, bf16[2,2,768,128]{2,3,1,0:T(8,128)(2,1)S(1)}, u32[]{:S(2)}, u32[]{:S(2)}) collective-permute-start(bf16[2,2,768,128]{2,3,1,0:T(8,128)(2,1)S(1)} %fusion.9), channel_id=1, source_target_pairs={{0,12},{2,14},{4,0},{6,2},{8,4},{10,6},{12,8},{14,10},{1,13},{3,15... | collective-permute-start | bytes 2359304 | tf_op jit(solution)/shard_map/ppermute | solution.py:12
  168.2 37.0 %collective-permute-start.20 = (bf16[2,1,768,128]{2,3,1,0:T(8,128)(2,1)S(1)}, bf16[2,1,768,128]{2,3,1,0:T(8,128)(2,1)S(1)}, u32[]{:S(2)}, u32[]{:S(2)}) collective-permute-start(bf16[2,1,768,128]{2,3,1,0:T(8,128)(2,1)S(1)} %get-tuple-element.28), channel_id=1, source_target_pairs={{0,14},{2,0},{4,2},{6,4},{8,6},{10,8},{12,10},{14,12},{1,15},{3,1}... | collective-permute-start | bytes 1179656 | tf_op jit(solution)/shard_map/ppermute | solution.py:12
  185.9 38.6 %collective-permute-start.9 = (bf16[2,2,768,128]{2,3,1,0:T(8,128)(2,1)S(1)}, bf16[2,2,768,128]{2,3,1,0:T(8,128)(2,1)S(1)}, u32[]{:S(2)}, u32[]{:S(2)}) collective-permute-start(bf16[2,2,768,128]{2,3,1,0:T(8,128)(2,1)S(1)} %fusion.3), channel_id=1, source_target_pairs={{0,4},{2,6},{4,8},{6,10},{8,12},{10,14},{12,0},{14,2},{1,5},{3,7},... | collective-permute-start | bytes 2359304 | tf_op jit(solution)/shard_map/ppermute | solution.py:12
  186.0 38.5 %collective-permute-start.8 = (bf16[2,1,768,128]{2,3,1,0:T(8,128)(2,1)S(1)}, bf16[2,1,768,128]{2,3,1,0:T(8,128)(2,1)S(1)}, u32[]{:S(2)}, u32[]{:S(2)}) collective-permute-start(bf16[2,1,768,128]{2,3,1,0:T(8,128)(2,1)S(1)} %get-tuple-element.39), channel_id=1, source_target_pairs={{0,2},{2,4},{4,6},{6,8},{8,10},{10,12},{12,14},{14,0},{1,3},{3,5},... | collective-permute-start | bytes 1179656 | tf_op jit(solution)/shard_map/ppermute | solution.py:12
  207.1 40.3 %collective-permute-start.23 = (bf16[2,2,768,128]{2,3,1,0:T(8,128)(2,1)S(1)}, bf16[2,2,768,128]{2,3,1,0:T(8,128)(2,1)}, u32[]{:S(2)}, u32[]{:S(2)}) collective-permute-start(bf16[2,2,768,128]{2,3,1,0:T(8,128)(2,1)S(1)} %fusion.10), channel_id=1, source_target_pairs={{0,12},{2,14},{4,0},{6,2},{8,4},{10,6},{12,8},{14,10},{1,13},{3,15... | collective-permute-start | bytes 2359304 | tf_op jit(solution)/shard_map/ppermute | solution.py:12
  210.4 37.0 %collective-permute-start.22 = (bf16[2,1,768,128]{2,3,1,0:T(8,128)(2,1)S(1)}, bf16[2,1,768,128]{2,3,1,0:T(8,128)(2,1)S(1)}, u32[]{:S(2)}, u32[]{:S(2)}) collective-permute-start(bf16[2,1,768,128]{2,3,1,0:T(8,128)(2,1)S(1)} %get-tuple-element.26), channel_id=1, source_target_pairs={{0,14},{2,0},{4,2},{6,4},{8,6},{10,8},{12,10},{14,12},{1,15},{3,1}... | collective-permute-start | bytes 1179656 | tf_op jit(solution)/shard_map/ppermute | solution.py:12
  228.2 38.1 %collective-permute-start.11 = (bf16[2,2,768,128]{2,3,1,0:T(8,128)(2,1)S(1)}, bf16[2,2,768,128]{2,3,1,0:T(8,128)(2,1)}, u32[]{:S(2)}, u32[]{:S(2)}) collective-permute-start(bf16[2,2,768,128]{2,3,1,0:T(8,128)(2,1)S(1)} %fusion.4), channel_id=1, source_target_pairs={{0,4},{2,6},{4,8},{6,10},{8,12},{10,14},{12,0},{14,2},{1,5},{3,7},... | collective-permute-start | bytes 2359304 | tf_op jit(solution)/shard_map/ppermute | solution.py:12
  228.3 37.9 %collective-permute-start.10 = (bf16[2,1,768,128]{2,3,1,0:T(8,128)(2,1)S(1)}, bf16[2,1,768,128]{2,3,1,0:T(8,128)(2,1)}, u32[]{:S(2)}, u32[]{:S(2)}) collective-permute-start(bf16[2,1,768,128]{2,3,1,0:T(8,128)(2,1)S(1)} %get-tuple-element.37), channel_id=1, source_target_pairs={{0,2},{2,4},{4,6},{6,8},{8,10},{10,12},{12,14},{14,0},{1,3},{3,5},... | collective-permute-start | bytes 1179656 | tf_op jit(solution)/shard_map/ppermute | solution.py:12
  (11 other events, 115.2 us)
Sparse Core Ops, SparseCore 0:
  279.1 15.1 reduce-scatter.1
where the time goes:
time: 302 us; the launch traced here: 301 us
  waiting for transfers between devices  188 us (62%)
  matrix products  51.7 us (17%)
  starting transfers between devices  38.9 us (13%)
  between operations  13.9 us (5%)
  other arithmetic  5.08 us (2%)
  local copies, waits for them, and re-layouts  3.62 us (1%)
    ppermute x24, waiting for transfers between devices, from_behind(): return lax.ppermute(x, axis, [(i, (i + by) % count) for i in range(count)])  173 us
    ppermute x24, starting transfers between devices, from_behind(): return lax.ppermute(x, axis, [(i, (i + by) % count) for i in range(count)])  38.9 us
    dot_general x8, matrix products, forward_apply(): jnp.einsum('fsckm,fsmn->fsckn', maps, front, preferred_element_type=jnp.f...  29.4 us
    dot_general x6, matrix products, adjoint_apply(): jnp.einsum('fsckm,fskn->fscmn', maps, front, preferred_element_type=jnp.f...  17.1 us
    reduce_scatter x1, waiting for transfers between devices, per_device(): lax.psum_scatter(partial_image, 'freq', scatter_dimension=1, tiled=True)  15.3 us
  transfers between devices with their start and end apart: 25, of which 13 were waited for; matrix products, arithmetic and copies ran while one was open for 15% of the time, Pallas kernels for 0%

commit v1 on v0

v1 whole, which is shorter than its diff:
```python
import functools

import jax
import jax.numpy as jnp
import numpy as np
from jax import lax
from jax.experimental import pallas as pl
from jax.experimental.pallas import tpu as pltpu
from jax.sharding import PartitionSpec as P

GY = 4
TICKS = 6
BF16 = jnp.bfloat16
F32 = jnp.float32
TIMES = (((1,), (0,)), ((), ()))
TIMES_TRANSPOSED = (((1,), (1,)), ((), ()))
TRANSPOSED_TIMES = (((0,), (0,)), ((), ()))
VMEM_LIMIT = 24 * 1024 * 1024


class Grid:
    def __init__(self, total, sub_local):
        self.total, self.sub_local = total, sub_local
        self.devices, self.rows = total // sub_local, total // GY

    def place(self, g):
        s = (g - GY - 1) % self.total
        return s // self.sub_local, s % self.sub_local

    def parents(self, way, g):
        row, col = g // GY, g % GY
        if way == 0:
            return [g - 1] * (col != 0) + [g - GY] * (row != 0)
        return [g + 1] * (col != GY - 1) + [g + GY] * (row != self.rows - 1)

    def depth(self, way, g):
        row, col = g // GY, g % GY
        return row + col if way == 0 else self.rows - 1 - row + GY - 1 - col


def tick_program(grid, chunks):
    deepest = grid.rows + GY - 2
    program = []

    def sends(way, chunk, tick):
        permutes = []
        for g in range(grid.total):
            if grid.depth(way, g) != tick:
                continue
            here = grid.place(g)[0]
            for p in grid.parents(way, g):
                there = grid.place(p)[0]
                message = (way, chunk, p, there, here)
                if there == here or any(message in permute for permute in permutes):
                    continue
                for permute in permutes:
                    if all(m[3] != there and m[4] != here for m in permute):
                        permute.append(message)
                        break
                else:
                    permutes.append([message])
        program.extend(("send", permute) for permute in permutes)

    chains = [(way, chunk) for chunk in range(chunks) for way in range(2)]
    for way, chunk in chains:
        sends(way, chunk, 1)
    for tick in range(1, deepest + 1):
        for way, chunk in chains:
            nodes = [
                (g, grid.place(g)[0], tuple(grid.parents(way, g)))
                for g in range(grid.total)
                if grid.depth(way, g) == tick
            ]
            program.append(("compute", way, chunk, nodes))
            sends(way, chunk, tick + 1)
    return program


def bits(devices):
    return sum(1 << d for d in devices)


def flag(mask, device):
    return ((mask >> device) & 1) == 1


def apply_map(way, front, real_map, imag_map, shots):
    dims = TIMES_TRANSPOSED if way == 0 else TIMES
    by_real = lax.dot_general(front, real_map, dims, preferred_element_type=F32)
    by_imag = lax.dot_general(front, imag_map, dims, preferred_element_type=F32)
    if way == 0:
        return by_real[:shots] - by_imag[shots:], by_real[shots:] + by_imag[:shots]
    return by_real[:shots] + by_imag[shots:], by_real[shots:] - by_imag[:shots]


def compute_step(way, chunk, steps, device, maps, origin, arrays, shots):
    width = origin.shape[-1]

    def kernel(device_ref, maps_ref, origin_ref, *refs):
        ins, outs, total = refs[: len(arrays)], refs[len(arrays) : -1], refs[-1]
        me = device_ref[0]
        for out, step in zip(outs, steps):
            everyone = bits(step["slot"])

            @pl.when(flag(everyone, me))
            def _():
                sources = [(ins[i], mask) for i, mask in step["arrays"].items()]
                sources += [(outs[i], mask) for i, mask in step["earlier"].items()]
                if all(mask == everyone for _, mask in sources):
                    front = sources[0][0][...]
                    if len(sources) > 1:
                        front = sum((ref[...].astype(F32) for ref, _ in sources[1:]), front.astype(F32)).astype(BF16)
                else:
                    total[...] = jnp.zeros_like(total)
                    for ref, mask in sources:

                        @pl.when(flag(mask, me))
                        def _(ref=ref):
                            total[...] += ref[...].astype(F32)

                    front = total[...].astype(BF16)
                slot = jnp.int32(0)
                for s in range(1, origin_ref.shape[1]):
                    slot += s * ((bits([d for d, own in step["slot"].items() if own == s]) >> me) & 1)
                real_part, imag_part = apply_map(way, front, maps_ref[chunk, slot, 0], maps_ref[chunk, slot, 1], shots)
                start = origin_ref[chunk, slot].astype(F32)
                out[:shots] = (start[:shots] + real_part).astype(BF16)
                out[shots:] = (start[shots:] + imag_part).astype(BF16)

    vmem = pl.BlockSpec(memory_space=pltpu.VMEM)
    return pl.pallas_call(
        kernel,
        out_shape=[jax.ShapeDtypeStruct((2 * shots, width), BF16)] * len(steps),
        in_specs=[pl.BlockSpec(memory_space=pltpu.SMEM)] + [vmem] * (2 + len(arrays)),
        out_specs=[vmem] * len(steps),
        scratch_shapes=[pltpu.VMEM((2 * shots, width), F32)],
        compiler_params=pltpu.CompilerParams(vmem_limit_bytes=VMEM_LIMIT),
        cost_estimate=pl.CostEstimate(flops=8 * shots * width * width, bytes_accessed=1 << 20, transcendentals=0),
        name=f"front_{way}_{chunk}",
    )(device, maps, origin, *arrays)


def sweep(program, grid, device, maps, origins, shots):
    chunks = maps.shape[0]
    arrays, where, holders = [], {}, {}

    def keep(value):
        arrays.append(value)
        return len(arrays) - 1

    for way in range(2):
        for chunk in range(chunks):
            for g in range(grid.total):
                if grid.depth(way, g) == 0:
                    dev, slot = grid.place(g)
                    where[way, chunk, g, dev] = index = keep(origins[way][chunk, slot])
                    holders[way, chunk, g] = index
    for kind, *body in program:
        if kind == "send":
            (messages,) = body
            by_array = {}
            for way, chunk, value, here, there in messages:
                by_array.setdefault(where[way, chunk, value, here], []).append(here)
            payload = None
            for index, senders in by_array.items():
                if payload is None:
                    payload = arrays[index]
                else:
                    payload = jnp.where(flag(bits(senders), device[0]), arrays[index], payload)
            index = keep(lax.ppermute(payload, "sub", sorted((m[3], m[4]) for m in messages)))
            for way, chunk, value, _, there in messages:
                where[way, chunk, value, there] = index
            continue
        way, chunk, nodes = body
        steps, operands, made, count = [], [], {}, {}
        for value, dev, inputs in nodes:
            position = count.get(dev, 0)
            count[dev] = position + 1
            if position == len(steps):
                steps.append({"slot": {}, "arrays": {}, "earlier": {}})
            step = steps[position]
            step["slot"][dev] = grid.place(value)[1]
            for v in inputs:
                if (v, dev) in made:
                    earlier = made[v, dev]
                    step["earlier"][earlier] = step["earlier"].get(earlier, 0) | 1 << dev
                else:
                    index = where[way, chunk, v, dev]
                    if index not in operands:
                        operands.append(index)
                    index = operands.index(index)
                    step["arrays"][index] = step["arrays"].get(index, 0) | 1 << dev
            made[value, dev] = position
        results = compute_step(
            way, chunk, steps, device, maps, origins[way], [arrays[i] for i in operands], shots
        )
        kept = [keep(r) for r in results]
        for (value, dev), position in made.items():
            where[way, chunk, value, dev] = kept[position]
            holders[way, chunk, value] = kept[position]
    finished = {}
    for (way, chunk, g), index in holders.items():
        dev, slot = grid.place(g)
        finished.setdefault((way, chunk, slot), {}).setdefault(index, []).append(dev)
    return {key: [(arrays[i], bits(devs)) for i, devs in found.items()] for key, found in finished.items()}


def interior_step(finished, device, maps, shots):
    freqs, subs, _, width, _ = maps.shape
    columns = 2 * shots
    arrays, choices = [], {}
    for key, found in finished.items():
        choices[key] = [(len(arrays) + i, mask) for i, (_, mask) in enumerate(found)]
        arrays += [a for a, _ in found]

    def kernel(device_ref, maps_ref, *refs):
        ins, (wave, back), both = refs[: len(arrays)], refs[len(arrays) : -1], refs[-1]
        me = device_ref[0]
        for f in range(freqs):
            for s in range(subs):
                for way in range(2):
                    for i, mask in choices[way, f, s]:

                        @pl.when(flag(mask, me))
                        def _(i=i, way=way):
                            both[way * columns : (way + 1) * columns] = ins[i][...]

                front = both[...]
                by_real = lax.dot_general(front, maps_ref[f, s, 0], TIMES_TRANSPOSED, preferred_element_type=F32)
                by_imag = lax.dot_general(front, maps_ref[f, s, 1], TIMES_TRANSPOSED, preferred_element_type=F32)
                for way, out in enumerate((wave, back)):
                    a, b = way * columns, way * columns + shots
                    out[f, s, :shots] = (by_real[a : a + shots] - by_imag[b : b + shots]).astype(BF16)
                    out[f, s, shots:] = (by_real[b : b + shots] + by_imag[a : a + shots]).astype(BF16)

    vmem = pl.BlockSpec(memory_space=pltpu.VMEM)
    shape = jax.ShapeDtypeStruct((freqs, subs, columns, width), BF16)
    return pl.pallas_call(
        kernel,
        out_shape=[shape, shape],
        in_specs=[pl.BlockSpec(memory_space=pltpu.SMEM)] + [vmem] * (1 + len(arrays)),
        out_specs=[vmem, vmem],
        scratch_shapes=[pltpu.VMEM((2 * columns, width), BF16)],
        compiler_params=pltpu.CompilerParams(vmem_limit_bytes=VMEM_LIMIT),
        name="interior",
    )(device, maps, *arrays)


def image_step(waves, backs, scale):
    freqs, subs, _, share = waves[0].shape
    width = backs[0].shape[-1]
    groups = len(waves)

    def kernel(*refs):
        out = refs[-1]
        for s in range(subs):
            rows = jnp.concatenate([refs[g][f, s] for g in range(groups) for f in range(freqs)], axis=0)
            points = jnp.concatenate([refs[groups + g][f, s] for g in range(groups) for f in range(freqs)], axis=0)
            out[s] = lax.dot_general(rows, points, TRANSPOSED_TIMES, preferred_element_type=F32) * scale

    vmem = pl.BlockSpec(memory_space=pltpu.VMEM)
    return pl.pallas_call(
        kernel,
        out_shape=jax.ShapeDtypeStruct((subs, share, width), F32),
        in_specs=[vmem] * (2 * groups),
        out_specs=vmem,
        compiler_params=pltpu.CompilerParams(vmem_limit_bytes=VMEM_LIMIT),
        name="image",
    )(*waves, *backs)


def pick_shots(table, chooser):
    freqs, subs, width, _, _ = table.shape
    picked = jnp.einsum("fsxcb,bn->fscnx", table, chooser, preferred_element_type=F32)
    return picked.astype(BF16).reshape(freqs, subs, -1, width)


def make_image(wave, back, scale):
    width = wave.shape[-1]
    groups = lax.axis_size("freq")
    core = lax.axis_index("freq")
    share = width // groups

    def rows_of(owner):
        return lax.dynamic_slice_in_dim(wave, owner * share, share, 3)

    waves, backs = [rows_of(core)], [back]
    for shift in range(1, groups):
        ring = [(i, (i + shift) % groups) for i in range(groups)]
        waves.append(lax.ppermute(rows_of((core + shift) % groups), "freq", ring))
        backs.append(lax.ppermute(back, "freq", ring))
    return image_step(waves, backs, scale)


def per_device(trace_map, interior_map, excitation, receiver_data, shot_index):
    freq_local, sub_local = trace_map.shape[:2]
    shots = shot_index.shape[0]
    bank_size = excitation.shape[4]
    chooser = (
        lax.broadcasted_iota(jnp.int32, (bank_size, shots), 0) == shot_index[None, :]
    ).astype(BF16)
    origins = (pick_shots(excitation, chooser), pick_shots(receiver_data, chooser))
    device = lax.axis_index("sub").astype(jnp.int32).reshape(1)
    grid = Grid(sub_local * lax.axis_size("sub"), sub_local)
    scale = (2.0 * shots * freq_local * lax.axis_size("freq")) ** (-0.5)
    if grid.rows + GY - 2 <= TICKS:
        finished = sweep(tick_program(grid, freq_local), grid, device, trace_map, origins, shots)
    else:
        finished = jacobi(grid, device, trace_map, origins, shots)
    wave, back = interior_step(finished, device, interior_map, shots)
    return make_image(wave, back, scale)


def jacobi(grid, device, maps, origins, shots):
    chunks, subs = maps.shape[:2]
    reach = GY // subs
    count = grid.devices
    places = (device[0] * subs + jnp.arange(subs, dtype=jnp.int32) + GY + 1) % grid.total
    column, row = places % GY, places // GY

    def move(x, by):
        return lax.ppermute(x, "sub", [(i, (i + by) % count) for i in range(count)])

    def mask(flags):
        return flags.astype(F32)[None, :, None, None]

    forward, adjoint = origins
    for _ in range(TICKS):
        left = jnp.concatenate([move(forward[:, subs - 1 :], 1), forward[:, : subs - 1]], axis=1)
        above = move(forward, reach)
        right = jnp.concatenate([adjoint[:, 1:], move(adjoint[:, :1], -1)], axis=1)
        below = move(adjoint, -reach)
        forward_in = left.astype(F32) * mask(column != 0) + above.astype(F32) * mask(row != 0)
        adjoint_in = right.astype(F32) * mask(column != GY - 1) + below.astype(F32) * mask(row != grid.rows - 1)
        fronts = []
        for way, total in enumerate((forward_in, adjoint_in)):
            dims = "fsnm,fsckm->fscnk" if way == 0 else "fsnk,fsckm->fscnm"
            product = jnp.einsum(dims, total.astype(BF16), maps, preferred_element_type=F32)
            real, imag = product[:, :, 0], product[:, :, 1]
            sign = 1.0 if way == 0 else -1.0
            moved = jnp.concatenate(
                [
                    real[:, :, :shots] - sign * imag[:, :, shots:],
                    real[:, :, shots:] + sign * imag[:, :, :shots],
                ],
                axis=2,
            )
            fronts.append((origins[way].astype(F32) + moved).astype(BF16))
        forward, adjoint = fronts
    everyone = bits(range(count))
    return {
        (way, f, s): [(front[f, s], everyone)]
        for way, front in enumerate((forward, adjoint))
        for f in range(chunks)
        for s in range(subs)
    }


def solution(mesh):
    placed = (
        P("freq", ("survey", "sub"), None, None, None),
        P("freq", ("survey", "sub"), None, None, None),
        P("freq", ("survey", "sub"), None, None, None),
        P("freq", ("survey", "sub"), None, None, None),
        P("survey"),
    )
    return jax.shard_map(
        per_device,
        mesh=mesh,
        in_specs=placed,
        out_specs=P(("survey", "sub"), "freq", None),
        check_vma=False,
    )
```

time: 302 us -> 198 us (0.66)
  waiting for transfers between devices: 188 us -> 26.8 us
  starting transfers between devices: 38.9 us -> 141 us
  matrix products: 51.7 us -> 2.06 us
  Pallas kernels: 0 us -> 13.7 us
  between operations: 13.9 us -> 0.86 us
  local copies, waits for them, and re-layouts: 3.62 us -> 11.9 us
  other arithmetic: 5.08 us -> 0.01 us
    ppermute x24 -> x50, waiting for transfers between devices: 173 us -> 26.8 us  [the longest x48 25.2 us: sweep(): lax.ppermute(payload, 'sub', sorted(((m[3], m[4]) for m in messages)))]
    ppermute x24 -> x50, starting transfers between devices: 38.9 us -> 141 us  [the longest x48 129 us: sweep(): lax.ppermute(payload, 'sub', sorted(((m[3], m[4]) for m in messages)))]
    dot_general x17 -> x2, matrix products: 51.7 us -> 2.06 us  [pick_shots(): jnp.einsum('fsxcb,bn->fscnx', table, chooser, preferred_element_type=F32)]
    reduce_scatter x1 -> x0, waiting for transfers between devices: 15.3 us -> none  [per_device(): lax.psum_scatter(partial_image, 'freq', scatter_dimension=1, tiled=True)]
    pallas_call x0 -> x26, Pallas kernels: none -> 13.7 us  [the longest x24 6.12 us: compute_step(): pl.pallas_call(kernel, out_shape=[jax.ShapeDtypeStruct((2 * shots, width)...]
    unnamed x20 -> x28, local copies, waits for them, and re-layouts: 2.25 us -> 9.88 us
  transfers between devices with their start and end apart: 25 -> 50, of which waited for: 13 -> 6; matrix products, arithmetic and copies ran while one was open for 15% -> 1% of each run, Pallas kernels for 0% -> 3%
where the time goes in v1:
time: 198 us; the launch traced here: 197 us
  starting transfers between devices  141 us (71%)
  waiting for transfers between devices  26.8 us (14%)
  Pallas kernels  13.7 us (7%)
  local copies, waits for them, and re-layouts  11.9 us (6%)
  matrix products  2.06 us (1%)
    ppermute x48, starting transfers between devices, sweep(): lax.ppermute(payload, 'sub', sorted(((m[3], m[4]) for m in messages)))  129 us
    ppermute x48, waiting for transfers between devices, sweep(): lax.ppermute(payload, 'sub', sorted(((m[3], m[4]) for m in messages)))  25.2 us
    unnamed x28, local copies, waits for them, and re-layouts  9.88 us
    ppermute x1, starting transfers between devices, make_image(): backs.append(lax.ppermute(back, 'freq', ring))  6.45 us
    pallas_call x24, Pallas kernels, compute_step(): pl.pallas_call(kernel, out_shape=[jax.ShapeDtypeStruct((2 * shots, width)...  6.12 us
    ppermute x1, starting transfers between devices, make_image(): waves.append(lax.ppermute(rows_of((core + shift) % groups), 'freq', ring))  5.79 us
    pallas_call x1, Pallas kernels, interior_step(): pl.pallas_call(kernel, out_shape=[shape, shape], in_specs=[pl.BlockSpec(m...  5.35 us
  transfers between devices with their start and end apart: 50, of which 6 were waited for; matrix products, arithmetic and copies ran while one was open for 1% of the time, Pallas kernels for 3%

profile of v1, /device:TPU:21, one launch (start us, length us, event | category | flops | bytes accessed | tf_op | source)
XLA Modules:
  0.0 196.5 jit_solution(5850012005092798692)
XLA Ops:
  2.8 2.1 %collective-permute-start.30 = (bf16[128,768]{1,0:T(8,128)(2,1)S(1)}, bf16[128,768]{1,0:T(8,128)(2,1)S(1)}, u32[]{:S(2)}, u32[]{:S(2)}) collective-permute-start(bf16[128,768]{1,0:T(8,128)(2,1)S(1)} %get-tuple-element.11.refs_18_), channel_id=1, source_target_pairs={{10,6},{11,7},{26,22},{27,23}} | collective-permute-start | bytes 589832 | tf_op jit(solution)/shard_map/ppermute | solution.py:170
  9.0 2.0 %collective-permute-start.11 = (bf16[128,768]{1,0:T(8,128)(2,1)}, bf16[128,768]{1,0:T(8,128)(2,1)}, u32[]{:S(2)}, u32[]{:S(2)}) collective-permute-start(bf16[128,768]{1,0:T(8,128)(2,1)} %get-tuple-element.13.refs_6_), channel_id=1, source_target_pairs={{10,14},{11,15},{26,30},{27,31}} | collective-permute-start | bytes 589832 | tf_op jit(solution)/shard_map/ppermute | solution.py:170
  18.9 2.0 %collective-permute-start.1 = (bf16[128,768]{1,0:T(8,128)(2,1)}, bf16[128,768]{1,0:T(8,128)(2,1)}, u32[]{:S(2)}, u32[]{:S(2)}) collective-permute-start(bf16[128,768]{1,0:T(8,128)(2,1)} %get-tuple-element.14.refs_0_), channel_id=1, source_target_pairs={{10,14},{11,15},{26,30},{27,31}} | collective-permute-start | bytes 589832 | tf_op jit(solution)/shard_map/ppermute | solution.py:170
  20.9 3.7 %copy-done.1 = bf16[2,2,2,768,768]{4,3,2,1,0:T(8,128)(2,1)S(1)} copy-done((bf16[2,2,2,768,768]{4,3,2,1,0:T(8,128)(2,1)S(1)}, bf16[2,2,2,768,768]{4,3,2,1,0:T(8,128)(2,1)}, u32[]{:S(2)}) %copy-start.1) | copy-done | bytes 9437208
  26.4 6.1 %collective-permute-start.32 = (bf16[128,768]{1,0:T(8,128)(2,1)S(1)}, bf16[128,768]{1,0:T(8,128)(2,1)S(1)}, u32[]{:S(2)}, u32[]{:S(2)}) collective-permute-start(bf16[128,768]{1,0:T(8,128)(2,1)S(1)} %front_1_1.6.refs_2_.refs_19_.refs_42_), channel_id=1, source_target_pairs={{6,2},{8,4},{7,3},{9,5},{22,18},{24,20},{23,19},{25,21}} | collective-permute-start | bytes 589832 | tf_op jit(solution)/shard_map/ppermute | solution.py:170
  35.9 8.1 %collective-permute-start.13 = (bf16[128,768]{1,0:T(8,128)(2,1)S(1)}, bf16[128,768]{1,0:T(8,128)(2,1)S(1)}, u32[]{:S(2)}, u32[]{:S(2)}) collective-permute-start(bf16[128,768]{1,0:T(8,128)(2,1)S(1)} %front_0_1.6.refs_0_.refs_7_.refs_36_), channel_id=1, source_target_pairs={{12,0},{14,2},{13,1},{15,3},{28,16},{30,18},{29,17},{31,19}} | collective-permute-start | bytes 589832 | tf_op jit(solution)/shard_map/ppermute | solution.py:170
  44.0 7.0 %collective-permute-start.22 = (bf16[128,768]{1,0:T(8,128)(2,1)S(1)}, bf16[128,768]{1,0:T(8,128)(2,1)S(1)}, u32[]{:S(2)}, u32[]{:S(2)}) collective-permute-start(bf16[128,768]{1,0:T(8,128)(2,1)S(1)} %front_1_0.6.refs_2_.refs_13_.refs_30_), channel_id=1, source_target_pairs={{6,2},{8,4},{7,3},{9,5},{22,18},{24,20},{23,19},{25,21}} | collective-permute-start | bytes 589832 | tf_op jit(solution)/shard_map/ppermute | solution.py:170
  53.4 8.1 %collective-permute-start.3 = (bf16[128,768]{1,0:T(8,128)(2,1)S(1)}, bf16[128,768]{1,0:T(8,128)(2,1)S(1)}, u32[]{:S(2)}, u32[]{:S(2)}) collective-permute-start(bf16[128,768]{1,0:T(8,128)(2,1)S(1)} %front_0_0.6.refs_0_.refs_1_.refs_24_), channel_id=1, source_target_pairs={{12,0},{14,2},{13,1},{15,3},{28,16},{30,18},{29,17},{31,19}} | collective-permute-start | bytes 589832 | tf_op jit(solution)/shard_map/ppermute | solution.py:170
  61.5 7.0 %collective-permute-start.34 = (bf16[128,768]{1,0:T(8,128)(2,1)S(1)}, bf16[128,768]{1,0:T(8,128)(2,1)S(1)}, u32[]{:S(2)}, u32[]{:S(2)}) collective-permute-start(bf16[128,768]{1,0:T(8,128)(2,1)S(1)} %front_1_1.7.refs_2_.refs_20_.refs_43_), channel_id=1, source_target_pairs={{2,14},{4,0},{8,4},{3,15},{5,1},{9,5},{18,30},{20,16},{24,20},{19,... | collective-permute-start | bytes 589832 | tf_op jit(solution)/shard_map/ppermute | solution.py:170
  70.0 8.2 %collective-permute-start.15 = (bf16[128,768]{1,0:T(8,128)(2,1)S(1)}, bf16[128,768]{1,0:T(8,128)(2,1)S(1)}, u32[]{:S(2)}, u32[]{:S(2)}) collective-permute-start(bf16[128,768]{1,0:T(8,128)(2,1)S(1)} %front_0_1.7.refs_1_.refs_8_.refs_37_), channel_id=1, source_target_pairs={{0,4},{2,6},{12,0},{1,5},{3,7},{13,1},{16,20},{18,22},{28,16},{17,... | collective-permute-start | bytes 589832 | tf_op jit(solution)/shard_map/ppermute | solution.py:170
  78.2 6.4 %collective-permute-start.24 = (bf16[128,768]{1,0:T(8,128)(2,1)S(1)}, bf16[128,768]{1,0:T(8,128)(2,1)S(1)}, u32[]{:S(2)}, u32[]{:S(2)}) collective-permute-start(bf16[128,768]{1,0:T(8,128)(2,1)S(1)} %front_1_0.7.refs_2_.refs_14_.refs_31_), channel_id=1, source_target_pairs={{2,14},{4,0},{8,4},{3,15},{5,1},{9,5},{18,30},{20,16},{24,20},{19,... | collective-permute-start | bytes 589832 | tf_op jit(solution)/shard_map/ppermute | solution.py:170
  86.0 8.1 %collective-permute-start.5 = (bf16[128,768]{1,0:T(8,128)(2,1)S(1)}, bf16[128,768]{1,0:T(8,128)(2,1)S(1)}, u32[]{:S(2)}, u32[]{:S(2)}) collective-permute-start(bf16[128,768]{1,0:T(8,128)(2,1)S(1)} %front_0_0.7.refs_1_.refs_2_.refs_25_), channel_id=1, source_target_pairs={{0,4},{2,6},{12,0},{1,5},{3,7},{13,1},{16,20},{18,22},{28,16},{17,... | collective-permute-start | bytes 589832 | tf_op jit(solution)/shard_map/ppermute | solution.py:170
  94.1 6.9 %collective-permute-start.36 = (bf16[128,768]{1,0:T(8,128)(2,1)S(1)}, bf16[128,768]{1,0:T(8,128)(2,1)S(1)}, u32[]{:S(2)}, u32[]{:S(2)}) collective-permute-start(bf16[128,768]{1,0:T(8,128)(2,1)S(1)} %front_1_1.8.refs_2_.refs_21_.refs_44_), channel_id=1, source_target_pairs={{4,0},{6,2},{14,12},{5,1},{7,3},{15,13},{20,16},{22,18},{30,28},{2... | collective-permute-start | bytes 589832 | tf_op jit(solution)/shard_map/ppermute | solution.py:170
  102.5 8.8 %collective-permute-start.17 = (bf16[128,768]{1,0:T(8,128)(2,1)S(1)}, bf16[128,768]{1,0:T(8,128)(2,1)S(1)}, u32[]{:S(2)}, u32[]{:S(2)}) collective-permute-start(bf16[128,768]{1,0:T(8,128)(2,1)S(1)} %front_0_1.8.refs_2_.refs_9_.refs_38_), channel_id=1, source_target_pairs={{0,4},{4,8},{14,2},{1,5},{5,9},{15,3},{16,20},{20,24},{30,18},{17,... | collective-permute-start | bytes 589832 | tf_op jit(solution)/shard_map/ppermute | solution.py:170
  111.4 7.6 %collective-permute-start.26 = (bf16[128,768]{1,0:T(8,128)(2,1)S(1)}, bf16[128,768]{1,0:T(8,128)(2,1)S(1)}, u32[]{:S(2)}, u32[]{:S(2)}) collective-permute-start(bf16[128,768]{1,0:T(8,128)(2,1)S(1)} %front_1_0.8.refs_2_.refs_15_.refs_32_), channel_id=1, source_target_pairs={{4,0},{6,2},{14,12},{5,1},{7,3},{15,13},{20,16},{22,18},{30,28},{2... | collective-permute-start | bytes 589832 | tf_op jit(solution)/shard_map/ppermute | solution.py:170
  120.4 8.4 %collective-permute-start.7 = (bf16[128,768]{1,0:T(8,128)(2,1)S(1)}, bf16[128,768]{1,0:T(8,128)(2,1)S(1)}, u32[]{:S(2)}, u32[]{:S(2)}) collective-permute-start(bf16[128,768]{1,0:T(8,128)(2,1)S(1)} %front_0_0.8.refs_2_.refs_3_.refs_26_), channel_id=1, source_target_pairs={{0,4},{4,8},{14,2},{1,5},{5,9},{15,3},{16,20},{20,24},{30,18},{17,... | collective-permute-start | bytes 589832 | tf_op jit(solution)/shard_map/ppermute | solution.py:170
  141.1 5.7 %collective-permute-done.46.refs_0_ = bf16[128,768]{1,0:T(8,128)(2,1)S(1)} collective-permute-done((bf16[128,768]{1,0:T(8,128)(2,1)S(1)}, bf16[128,768]{1,0:T(8,128)(2,1)S(1)}, u32[]{:S(2)}, u32[]{:S(2)}) %collective-permute-start.46) | collective-permute-done | bytes 196640 | tf_op jit(solution)/shard_map/ppermute | solution.py:170
  148.2 6.3 %collective-permute-done.47.refs_1_ = bf16[128,768]{1,0:T(8,128)(2,1)S(1)} collective-permute-done((bf16[128,768]{1,0:T(8,128)(2,1)S(1)}, bf16[128,768]{1,0:T(8,128)(2,1)S(1)}, u32[]{:S(2)}, u32[]{:S(2)}) %collective-permute-start.47) | collective-permute-done | bytes 196640 | tf_op jit(solution)/shard_map/ppermute | solution.py:170
  155.8 9.1 %collective-permute-done.44.refs_0_ = bf16[128,768]{1,0:T(8,128)(2,1)S(1)} collective-permute-done((bf16[128,768]{1,0:T(8,128)(2,1)S(1)}, bf16[128,768]{1,0:T(8,128)(2,1)S(1)}, u32[]{:S(2)}, u32[]{:S(2)}) %collective-permute-start.44) | collective-permute-done | bytes 196640 | tf_op jit(solution)/shard_map/ppermute | solution.py:170
  169.3 2.8 %collective-permute-done.41.refs_1_ = bf16[128,768]{1,0:T(8,128)(2,1)S(1)} collective-permute-done((bf16[128,768]{1,0:T(8,128)(2,1)S(1)}, bf16[128,768]{1,0:T(8,128)(2,1)S(1)}, u32[]{:S(2)}, u32[]{:S(2)}) %collective-permute-start.41) | collective-permute-done | bytes 196640 | tf_op jit(solution)/shard_map/ppermute | solution.py:170
  173.0 5.4 %interior.1 = (bf16[2,2,128,768]{3,2,1,0:T(8,128)(2,1)S(1)}, bf16[2,2,128,768]{3,2,1,0:T(8,128)(2,1)S(1)}) custom-call(s32[1]{0:T(128)} %bitcast.device_ref, bf16[2,2,2,768,768]{4,3,2,1,0:T(8,128)(2,1)S(1)} %bitcast.48, bf16[128,768]{1,0:T(8,128)(2,1)} %get-tuple-element.14.refs_0_, bf16[128,768]{1,0:T(8,128)(2,1)S(1)} %front_0_0.6.refs_0_.refs_1_.refs_24_, ...), custom_call_target="tpu_custom_call" | custom-call | tf_op jit(solution)/shard_map/interior/pallas_call | solution.py:238
  179.3 6.4 %collective-permute-start.49 = (bf16[2,2,128,768]{3,2,1,0:T(8,128)(2,1)S(1)}, bf16[2,2,128,768]{3,2,1,0:T(8,128)(2,1)S(1)}, u32[]{:S(2)}, u32[]{:S(2)}) collective-permute-start(bf16[2,2,128,768]{3,2,1,0:T(8,128)(2,1)S(1)} %get-tuple-element.8.refs_2_), channel_id=1, source_target_pairs={{0,1},{1,0},{2,3},{3,2},{4,5},{5,4},{6,7},{7,6},{8,9},{9,8},{10,11... | collective-permute-start | bytes 2359304 | tf_op jit(solution)/shard_map/ppermute | solution.py:291
  186.9 5.8 %collective-permute-start.48 = (bf16[2,2,128,384]{3,2,1,0:T(8,128)(2,1)S(1)}, bf16[2,2,128,384]{3,2,1,0:T(8,128)(2,1)S(1)}, u32[]{:S(2)}, u32[]{:S(2)}) collective-permute-start(bf16[2,2,128,384]{3,2,1,0:T(8,128)(2,1)S(1)} %get-tuple-element.9), channel_id=1, source_target_pairs={{0,1},{1,0},{2,3},{3,2},{4,5},{5,4},{6,7},{7,6},{8,9},{9,8},{10,11... | collective-permute-start | bytes 1179656 | tf_op jit(solution)/shard_map/ppermute | solution.py:290
  194.3 2.2 %image.1 = f32[2,384,768]{2,1,0:T(8,128)} custom-call(bf16[2,2,128,384]{3,2,1,0:T(8,128)(2,1)S(1)} %get-tuple-element.10.refs_0_, bf16[2,2,128,384]{3,2,1,0:T(8,128)(2,1)S(1)} %collective-permute-done.48.refs_1_, bf16[2,2,128,768]{3,2,1,0:T(8,128)(2,1)S(1)} %get-tuple-element.8.refs_2_, bf16[2,2,128,768]{3,2,1,0:T(8,128)(2,1)S(1)} %collective-permute-done.49.refs_3_), custom_call_target="tpu_custom_call" | custom-call | tf_op jit(solution)/shard_map/image/pallas_call | solution.py:262
  (136 shorter events, 51.5 us)
Async XLA Ops:
  11.0 22.5 %collective-permute-start.20 = (bf16[128,768]{1,0:T(8,128)(2,1)S(1)}, bf16[128,768]{1,0:T(8,128)(2,1)}, u32[]{:S(2)}, u32[]{:S(2)}) collective-permute-start(bf16[128,768]{1,0:T(8,128)(2,1)S(1)} %get-tuple-element.12.refs_12_), channel_id=1, source_target_pairs={{10,6},{11,7},{26,22},{27,23}} | collective-permute-start | bytes 589832 | tf_op jit(solution)/shard_map/ppermute | solution.py:170
  13.6 20.5 %collective-permute-start.21 = (bf16[128,768]{1,0:T(8,128)(2,1)S(1)}, bf16[128,768]{1,0:T(8,128)(2,1)}, u32[]{:S(2)}, u32[]{:S(2)}) collective-permute-start(bf16[128,768]{1,0:T(8,128)(2,1)S(1)} %get-tuple-element.12.refs_12_), channel_id=1, source_target_pairs={{10,8},{11,9},{26,24},{27,25}} | collective-permute-start | bytes 589832 | tf_op jit(solution)/shard_map/ppermute | solution.py:170
  16.3 19.6 %collective-permute-start = (bf16[128,768]{1,0:T(8,128)(2,1)}, bf16[128,768]{1,0:T(8,128)(2,1)}, u32[]{:S(2)}, u32[]{:S(2)}) collective-permute-start(bf16[128,768]{1,0:T(8,128)(2,1)} %get-tuple-element.14.refs_0_), channel_id=1, source_target_pairs={{10,12},{11,13},{26,28},{27,29}} | collective-permute-start | bytes 589832 | tf_op jit(solution)/shard_map/ppermute | solution.py:170
  18.9 25.1 %collective-permute-start.1 = (bf16[128,768]{1,0:T(8,128)(2,1)}, bf16[128,768]{1,0:T(8,128)(2,1)}, u32[]{:S(2)}, u32[]{:S(2)}) collective-permute-start(bf16[128,768]{1,0:T(8,128)(2,1)} %get-tuple-element.14.refs_0_), channel_id=1, source_target_pairs={{10,14},{11,15},{26,30},{27,31}} | collective-permute-start | bytes 589832 | tf_op jit(solution)/shard_map/ppermute | solution.py:170
  26.4 24.6 %collective-permute-start.32 = (bf16[128,768]{1,0:T(8,128)(2,1)S(1)}, bf16[128,768]{1,0:T(8,128)(2,1)S(1)}, u32[]{:S(2)}, u32[]{:S(2)}) collective-permute-start(bf16[128,768]{1,0:T(8,128)(2,1)S(1)} %front_1_1.6.refs_2_.refs_19_.refs_42_), channel_id=1, source_target_pairs={{6,2},{8,4},{7,3},{9,5},{22,18},{24,20},{23,19},{25,21}} | collective-permute-start | bytes 589832 | tf_op jit(solution)/shard_map/ppermute | solution.py:170
  33.5 19.2 %collective-permute-start.33 = (bf16[128,768]{1,0:T(8,128)(2,1)S(1)}, bf16[128,768]{1,0:T(8,128)(2,1)S(1)}, u32[]{:S(2)}, u32[]{:S(2)}) collective-permute-start(bf16[128,768]{1,0:T(8,128)(2,1)S(1)} %front_1_1.6.refs_2_.refs_19_.refs_42_), channel_id=1, source_target_pairs={{6,4},{7,5},{22,20},{23,21}} | collective-permute-start | bytes 589832 | tf_op jit(solution)/shard_map/ppermute | solution.py:170
  34.2 19.2 %collective-permute-start.12 = (bf16[128,768]{1,0:T(8,128)(2,1)S(1)}, bf16[128,768]{1,0:T(8,128)(2,1)S(1)}, u32[]{:S(2)}, u32[]{:S(2)}) collective-permute-start(bf16[128,768]{1,0:T(8,128)(2,1)S(1)} %front_0_1.6.refs_0_.refs_7_.refs_36_), channel_id=1, source_target_pairs={{14,0},{15,1},{30,16},{31,17}} | collective-permute-start | bytes 589832 | tf_op jit(solution)/shard_map/ppermute | solution.py:170
  35.9 25.6 %collective-permute-start.13 = (bf16[128,768]{1,0:T(8,128)(2,1)S(1)}, bf16[128,768]{1,0:T(8,128)(2,1)S(1)}, u32[]{:S(2)}, u32[]{:S(2)}) collective-permute-start(bf16[128,768]{1,0:T(8,128)(2,1)S(1)} %front_0_1.6.refs_0_.refs_7_.refs_36_), channel_id=1, source_target_pairs={{12,0},{14,2},{13,1},{15,3},{28,16},{30,18},{29,17},{31,19}} | collective-permute-start | bytes 589832 | tf_op jit(solution)/shard_map/ppermute | solution.py:170
  44.0 24.6 %collective-permute-start.22 = (bf16[128,768]{1,0:T(8,128)(2,1)S(1)}, bf16[128,768]{1,0:T(8,128)(2,1)S(1)}, u32[]{:S(2)}, u32[]{:S(2)}) collective-permute-start(bf16[128,768]{1,0:T(8,128)(2,1)S(1)} %front_1_0.6.refs_2_.refs_13_.refs_30_), channel_id=1, source_target_pairs={{6,2},{8,4},{7,3},{9,5},{22,18},{24,20},{23,19},{25,21}} | collective-permute-start | bytes 589832 | tf_op jit(solution)/shard_map/ppermute | solution.py:170
  51.0 18.2 %collective-permute-start.23 = (bf16[128,768]{1,0:T(8,128)(2,1)S(1)}, bf16[128,768]{1,0:T(8,128)(2,1)S(1)}, u32[]{:S(2)}, u32[]{:S(2)}) collective-permute-start(bf16[128,768]{1,0:T(8,128)(2,1)S(1)} %front_1_0.6.refs_2_.refs_13_.refs_30_), channel_id=1, source_target_pairs={{6,4},{7,5},{22,20},{23,21}} | collective-permute-start | bytes 589832 | tf_op jit(solution)/shard_map/ppermute | solution.py:170
  53.4 24.7 %collective-permute-start.3 = (bf16[128,768]{1,0:T(8,128)(2,1)S(1)}, bf16[128,768]{1,0:T(8,128)(2,1)S(1)}, u32[]{:S(2)}, u32[]{:S(2)}) collective-permute-start(bf16[128,768]{1,0:T(8,128)(2,1)S(1)} %front_0_0.6.refs_0_.refs_1_.refs_24_), channel_id=1, source_target_pairs={{12,0},{14,2},{13,1},{15,3},{28,16},{30,18},{29,17},{31,19}} | collective-permute-start | bytes 589832 | tf_op jit(solution)/shard_map/ppermute | solution.py:170
  61.5 23.0 %collective-permute-start.34 = (bf16[128,768]{1,0:T(8,128)(2,1)S(1)}, bf16[128,768]{1,0:T(8,128)(2,1)S(1)}, u32[]{:S(2)}, u32[]{:S(2)}) collective-permute-start(bf16[128,768]{1,0:T(8,128)(2,1)S(1)} %front_1_1.7.refs_2_.refs_20_.refs_43_), channel_id=1, source_target_pairs={{2,14},{4,0},{8,4},{3,15},{5,1},{9,5},{18,30},{20,16},{24,20},{19,... | collective-permute-start | bytes 589832 | tf_op jit(solution)/shard_map/ppermute | solution.py:170
  70.0 24.1 %collective-permute-start.15 = (bf16[128,768]{1,0:T(8,128)(2,1)S(1)}, bf16[128,768]{1,0:T(8,128)(2,1)S(1)}, u32[]{:S(2)}, u32[]{:S(2)}) collective-permute-start(bf16[128,768]{1,0:T(8,128)(2,1)S(1)} %front_0_1.7.refs_1_.refs_8_.refs_37_), channel_id=1, source_target_pairs={{0,4},{2,6},{12,0},{1,5},{3,7},{13,1},{16,20},{18,22},{28,16},{17,... | collective-permute-start | bytes 589832 | tf_op jit(solution)/shard_map/ppermute | solution.py:170
  78.2 22.9 %collective-permute-start.24 = (bf16[128,768]{1,0:T(8,128)(2,1)S(1)}, bf16[128,768]{1,0:T(8,128)(2,1)S(1)}, u32[]{:S(2)}, u32[]{:S(2)}) collective-permute-start(bf16[128,768]{1,0:T(8,128)(2,1)S(1)} %front_1_0.7.refs_2_.refs_14_.refs_31_), channel_id=1, source_target_pairs={{2,14},{4,0},{8,4},{3,15},{5,1},{9,5},{18,30},{20,16},{24,20},{19,... | collective-permute-start | bytes 589832 | tf_op jit(solution)/shard_map/ppermute | solution.py:170
  86.0 25.4 %collective-permute-start.5 = (bf16[128,768]{1,0:T(8,128)(2,1)S(1)}, bf16[128,768]{1,0:T(8,128)(2,1)S(1)}, u32[]{:S(2)}, u32[]{:S(2)}) collective-permute-start(bf16[128,768]{1,0:T(8,128)(2,1)S(1)} %front_0_0.7.refs_1_.refs_2_.refs_25_), channel_id=1, source_target_pairs={{0,4},{2,6},{12,0},{1,5},{3,7},{13,1},{16,20},{18,22},{28,16},{17,... | collective-permute-start | bytes 589832 | tf_op jit(solution)/shard_map/ppermute | solution.py:170
  94.1 24.8 %collective-permute-start.36 = (bf16[128,768]{1,0:T(8,128)(2,1)S(1)}, bf16[128,768]{1,0:T(8,128)(2,1)S(1)}, u32[]{:S(2)}, u32[]{:S(2)}) collective-permute-start(bf16[128,768]{1,0:T(8,128)(2,1)S(1)} %front_1_1.8.refs_2_.refs_21_.refs_44_), channel_id=1, source_target_pairs={{4,0},{6,2},{14,12},{5,1},{7,3},{15,13},{20,16},{22,18},{30,28},{2... | collective-permute-start | bytes 589832 | tf_op jit(solution)/shard_map/ppermute | solution.py:170
  101.1 18.6 %collective-permute-start.37 = (bf16[128,768]{1,0:T(8,128)(2,1)S(1)}, bf16[128,768]{1,0:T(8,128)(2,1)S(1)}, u32[]{:S(2)}, u32[]{:S(2)}) collective-permute-start(bf16[128,768]{1,0:T(8,128)(2,1)S(1)} %front_1_1.8.refs_2_.refs_21_.refs_44_), channel_id=1, source_target_pairs={{0,12},{4,2},{1,13},{5,3},{16,28},{20,18},{17,29},{21,19}} | collective-permute-start | bytes 589832 | tf_op jit(solution)/shard_map/ppermute | solution.py:170
  101.8 18.6 %collective-permute-start.16 = (bf16[128,768]{1,0:T(8,128)(2,1)S(1)}, bf16[128,768]{1,0:T(8,128)(2,1)S(1)}, u32[]{:S(2)}, u32[]{:S(2)}) collective-permute-start(bf16[128,768]{1,0:T(8,128)(2,1)S(1)} %front_0_1.8.refs_2_.refs_9_.refs_38_), channel_id=1, source_target_pairs={{0,2},{6,8},{1,3},{7,9},{16,18},{22,24},{17,19},{23,25}} | collective-permute-start | bytes 589832 | tf_op jit(solution)/shard_map/ppermute | solution.py:170
  102.5 26.3 %collective-permute-start.17 = (bf16[128,768]{1,0:T(8,128)(2,1)S(1)}, bf16[128,768]{1,0:T(8,128)(2,1)S(1)}, u32[]{:S(2)}, u32[]{:S(2)}) collective-permute-start(bf16[128,768]{1,0:T(8,128)(2,1)S(1)} %front_0_1.8.refs_2_.refs_9_.refs_38_), channel_id=1, source_target_pairs={{0,4},{4,8},{14,2},{1,5},{5,9},{15,3},{16,20},{20,24},{30,18},{17,... | collective-permute-start | bytes 589832 | tf_op jit(solution)/shard_map/ppermute | solution.py:170
  135.9 18.6 %collective-permute-start.47 = (bf16[128,768]{1,0:T(8,128)(2,1)S(1)}, bf16[128,768]{1,0:T(8,128)(2,1)S(1)}, u32[]{:S(2)}, u32[]{:S(2)}) collective-permute-start(bf16[128,768]{1,0:T(8,128)(2,1)S(1)} %front_1_1.10.refs_23_.refs_46_), channel_id=1, source_target_pairs={{14,10},{15,11},{30,26},{31,27}} | collective-permute-start | bytes 589832 | tf_op jit(solution)/shard_map/ppermute | solution.py:170
  137.2 27.7 %collective-permute-start.44 = (bf16[128,768]{1,0:T(8,128)(2,1)S(1)}, bf16[128,768]{1,0:T(8,128)(2,1)S(1)}, u32[]{:S(2)}, u32[]{:S(2)}) collective-permute-start(bf16[128,768]{1,0:T(8,128)(2,1)S(1)} %front_0_1.10.refs_11_.refs_40_), channel_id=1, source_target_pairs={{8,10},{9,11},{24,26},{25,27}} | collective-permute-start | bytes 589832 | tf_op jit(solution)/shard_map/ppermute | solution.py:170
  138.5 28.2 %collective-permute-start.45 = (bf16[128,768]{1,0:T(8,128)(2,1)S(1)}, bf16[128,768]{1,0:T(8,128)(2,1)S(1)}, u32[]{:S(2)}, u32[]{:S(2)}) collective-permute-start(bf16[128,768]{1,0:T(8,128)(2,1)S(1)} %front_0_1.10.refs_11_.refs_40_), channel_id=1, source_target_pairs={{6,10},{7,11},{22,26},{23,27}} | collective-permute-start | bytes 589832 | tf_op jit(solution)/shard_map/ppermute | solution.py:170
  139.8 27.8 %collective-permute-start.42 = (bf16[128,768]{1,0:T(8,128)(2,1)S(1)}, bf16[128,768]{1,0:T(8,128)(2,1)S(1)}, u32[]{:S(2)}, u32[]{:S(2)}) collective-permute-start(bf16[128,768]{1,0:T(8,128)(2,1)S(1)} %front_1_0.10.refs_17_.refs_34_), channel_id=1, source_target_pairs={{12,10},{13,11},{28,26},{29,27}} | collective-permute-start | bytes 589832 | tf_op jit(solution)/shard_map/ppermute | solution.py:170
  146.9 20.8 %collective-permute-start.43 = (bf16[128,768]{1,0:T(8,128)(2,1)S(1)}, bf16[128,768]{1,0:T(8,128)(2,1)S(1)}, u32[]{:S(2)}, u32[]{:S(2)}) collective-permute-start(bf16[128,768]{1,0:T(8,128)(2,1)S(1)} %front_1_0.10.refs_17_.refs_34_), channel_id=1, source_target_pairs={{14,10},{15,11},{30,26},{31,27}} | collective-permute-start | bytes 589832 | tf_op jit(solution)/shard_map/ppermute | solution.py:170
  (40 other events, 321.4 us)

commit v2 on v1

--- a/solution.py
+++ b/solution.py
@@ -10,6 +10,7 @@
 
 GY = 4
 TICKS = 6
+CHUNKS = 1
 BF16 = jnp.bfloat16
 F32 = jnp.float32
 TIMES = (((1,), (0,)), ((), ()))
@@ -95,6 +96,7 @@
 
 def compute_step(way, chunk, steps, device, maps, origin, arrays, shots):
     width = origin.shape[-1]
+    shape = (len(chunk), 2 * shots, width)
 
     def kernel(device_ref, maps_ref, origin_ref, *refs):
         ins, outs, total = refs[: len(arrays)], refs[len(arrays) : -1], refs[-1]
@@ -122,26 +124,27 @@
                 slot = jnp.int32(0)
                 for s in range(1, origin_ref.shape[1]):
                     slot += s * ((bits([d for d, own in step["slot"].items() if own == s]) >> me) & 1)
-                real_part, imag_part = apply_map(way, front, maps_ref[chunk, slot, 0], maps_ref[chunk, slot, 1], shots)
-                start = origin_ref[chunk, slot].astype(F32)
-                out[:shots] = (start[:shots] + real_part).astype(BF16)
-                out[shots:] = (start[shots:] + imag_part).astype(BF16)
+                for i, f in enumerate(chunk):
+                    real_part, imag_part = apply_map(way, front[i], maps_ref[f, slot, 0], maps_ref[f, slot, 1], shots)
+                    start = origin_ref[f, slot].astype(F32)
+                    out[i, :shots] = (start[:shots] + real_part).astype(BF16)
+                    out[i, shots:] = (start[shots:] + imag_part).astype(BF16)
 
     vmem = pl.BlockSpec(memory_space=pltpu.VMEM)
     return pl.pallas_call(
         kernel,
-        out_shape=[jax.ShapeDtypeStruct((2 * shots, width), BF16)] * len(steps),
+        out_shape=[jax.ShapeDtypeStruct(shape, BF16)] * len(steps),
         in_specs=[pl.BlockSpec(memory_space=pltpu.SMEM)] + [vmem] * (2 + len(arrays)),
         out_specs=[vmem] * len(steps),
-        scratch_shapes=[pltpu.VMEM((2 * shots, width), F32)],
+        scratch_shapes=[pltpu.VMEM(shape, F32)],
         compiler_params=pltpu.CompilerParams(vmem_limit_bytes=VMEM_LIMIT),
         cost_estimate=pl.CostEstimate(flops=8 * shots * width * width, bytes_accessed=1 << 20, transcendentals=0),
-        name=f"front_{way}_{chunk}",
+        name=f"front_{way}_{chunk[0]}",
     )(device, maps, origin, *arrays)
 
 
-def sweep(program, grid, device, maps, origins, shots):
-    chunks = maps.shape[0]
+def sweep(program, chunks, grid, device, maps, origins, shots):
+    per_chunk = maps.shape[0] // chunks
     arrays, where, holders = [], {}, {}
 
     def keep(value):
@@ -153,7 +156,7 @@
             for g in range(grid.total):
                 if grid.depth(way, g) == 0:
                     dev, slot = grid.place(g)
-                    where[way, chunk, g, dev] = index = keep(origins[way][chunk, slot])
+                    where[way, chunk, g, dev] = index = keep(origins[way][chunk * per_chunk : (chunk + 1) * per_chunk, slot])
                     holders[way, chunk, g] = index
     for kind, *body in program:
         if kind == "send":
@@ -192,7 +195,8 @@
                     step["arrays"][index] = step["arrays"].get(index, 0) | 1 << dev
             made[value, dev] = position
         results = compute_step(
-            way, chunk, steps, device, maps, origins[way], [arrays[i] for i in operands], shots
+            way, range(chunk * per_chunk, (chunk + 1) * per_chunk), steps, device, maps, origins[way],
+            [arrays[i] for i in operands], shots
         )
         kept = [keep(r) for r in results]
         for (value, dev), position in made.items():
@@ -201,8 +205,9 @@
     finished = {}
     for (way, chunk, g), index in holders.items():
         dev, slot = grid.place(g)
-        finished.setdefault((way, chunk, slot), {}).setdefault(index, []).append(dev)
-    return {key: [(arrays[i], bits(devs)) for i, devs in found.items()] for key, found in finished.items()}
+        for f in range(per_chunk):
+            finished.setdefault((way, chunk * per_chunk + f, slot), {}).setdefault((index, f), []).append(dev)
+    return {key: [(arrays[i], f, bits(devs)) for (i, f), devs in found.items()] for key, found in finished.items()}
 
 
 def interior_step(finished, device, maps, shots):
@@ -210,8 +215,11 @@
     columns = 2 * shots
     arrays, choices = [], {}
     for key, found in finished.items():
-        choices[key] = [(len(arrays) + i, mask) for i, (_, mask) in enumerate(found)]
-        arrays += [a for a, _ in found]
+        choices[key] = []
+        for array, f, mask in found:
+            if not any(array is a for a in arrays):
+                arrays.append(array)
+            choices[key].append((next(i for i, a in enumerate(arrays) if a is array), f, mask))
 
     def kernel(device_ref, maps_ref, *refs):
         ins, (wave, back), both = refs[: len(arrays)], refs[len(arrays) : -1], refs[-1]
@@ -219,11 +227,11 @@
         for f in range(freqs):
             for s in range(subs):
                 for way in range(2):
-                    for i, mask in choices[way, f, s]:
+                    for i, part, mask in choices[way, f, s]:
 
                         @pl.when(flag(mask, me))
-                        def _(i=i, way=way):
-                            both[way * columns : (way + 1) * columns] = ins[i][...]
+                        def _(i=i, part=part, way=way):
+                            both[way * columns : (way + 1) * columns] = ins[i][part]
 
                 front = both[...]
                 by_real = lax.dot_general(front, maps_ref[f, s, 0], TIMES_TRANSPOSED, preferred_element_type=F32)
@@ -304,7 +312,7 @@
     grid = Grid(sub_local * lax.axis_size("sub"), sub_local)
     scale = (2.0 * shots * freq_local * lax.axis_size("freq")) ** (-0.5)
     if grid.rows + GY - 2 <= TICKS:
-        finished = sweep(tick_program(grid, freq_local), grid, device, trace_map, origins, shots)
+        finished = sweep(tick_program(grid, CHUNKS), CHUNKS, grid, device, trace_map, origins, shots)
     else:
         finished = jacobi(grid, device, trace_map, origins, shots)
     wave, back = interior_step(finished, device, interior_map, shots)
@@ -349,7 +357,7 @@
         forward, adjoint = fronts
     everyone = bits(range(count))
     return {
-        (way, f, s): [(front[f, s], everyone)]
+        (way, f, s): [(front[:, s], f, everyone)]
         for way, front in enumerate((forward, adjoint))
         for f in range(chunks)
         for s in range(subs)

time: 198 us -> 136 us (0.69)
  starting transfers between devices: 141 us -> 26.3 us
  waiting for transfers between devices: 26.8 us -> 86.4 us
  local copies, waits for them, and re-layouts: 11.9 us -> 8.09 us
    ppermute x48 -> x24, starting transfers between devices: 129 us -> 25.2 us  [sweep(): lax.ppermute(payload, 'sub', sorted(((m[3], m[4]) for m in messages)))]
    ppermute x48 -> x24, waiting for transfers between devices: 25.2 us -> 84.7 us  [sweep(): lax.ppermute(payload, 'sub', sorted(((m[3], m[4]) for m in messages)))]
    ppermute x1, starting transfers between devices: 5.79 us -> 0.07 us  [make_image(): waves.append(lax.ppermute(rows_of((core + shift) % groups), 'freq', ring))]
    ppermute x1, starting transfers between devices: 6.45 us -> 1.03 us  [make_image(): backs.append(lax.ppermute(back, 'freq', ring))]
    unnamed x28 -> x16, local copies, waits for them, and re-layouts: 9.88 us -> 5.99 us
    pallas_call x24 -> x12, Pallas kernels: 6.12 us -> 4.94 us  [compute_step(): pl.pallas_call(kernel, out_shape=[jax.ShapeDtypeStruct(shape, BF16)] * le...]
  transfers between devices with their start and end apart: 50 -> 26, of which waited for: 6 -> 6; matrix products, arithmetic and copies ran while one was open for 1% -> 2% of each run, Pallas kernels for 3% -> 2%
where the time goes in v2:
time: 136 us
  waiting for transfers between devices  86.4 us (64%)
  starting transfers between devices  26.3 us (19%)
  Pallas kernels  12.4 us (9%)
  local copies, waits for them, and re-layouts  8.09 us (6%)
  matrix products  2.06 us (2%)
    ppermute x24, waiting for transfers between devices, sweep(): lax.ppermute(payload, 'sub', sorted(((m[3], m[4]) for m in messages)))  84.7 us
    ppermute x24, starting transfers between devices, sweep(): lax.ppermute(payload, 'sub', sorted(((m[3], m[4]) for m in messages)))  25.2 us
    unnamed x16, local copies, waits for them, and re-layouts  5.99 us
    pallas_call x1, Pallas kernels, interior_step(): pl.pallas_call(kernel, out_shape=[shape, shape], in_specs=[pl.BlockSpec(m...  5.27 us
    pallas_call x12, Pallas kernels, compute_step(): pl.pallas_call(kernel, out_shape=[jax.ShapeDtypeStruct(shape, BF16)] * le...  4.94 us
  transfers between devices with their start and end apart: 26, of which 6 were waited for; matrix products, arithmetic and copies ran while one was open for 2% of the time, Pallas kernels for 2%

profile of v2, /device:TPU:21, one launch (start us, length us, event | category | flops | bytes accessed | tf_op | source)
XLA Modules:
  0.0 135.8 jit_solution(4714069184485699415)
XLA Ops:
  0.0 1.4 %copy-done = bf16[2,2,768,2,128]{4,3,2,1,0:T(2,128)(2,1)S(1)} copy-done((bf16[2,2,768,2,128]{4,3,2,1,0:T(2,128)(2,1)S(1)}, bf16[2,2,768,2,128]{4,3,2,1,0:T(2,128)(2,1)}, u32[]{:S(2)}) %copy-start) | copy-done | bytes 1572888
  1.4 1.4 fusion.7
  2.9 3.0 %collective-permute-start.10 = (bf16[2,128,768]{2,1,0:T(8,128)(2,1)S(1)}, bf16[2,128,768]{2,1,0:T(8,128)(2,1)}, u32[]{:S(2)}, u32[]{:S(2)}) collective-permute-start(bf16[2,128,768]{2,1,0:T(8,128)(2,1)S(1)} %slice_bitcast_fusion.refs_6_), channel_id=1, source_target_pairs={{10,6},{11,7},{26,22},{27,23}} | collective-permute-start | bytes 1179656 | tf_op jit(solution)/shard_map/ppermute | solution.py:173
  5.9 2.0 %collective-permute-start.11 = (bf16[2,128,768]{2,1,0:T(8,128)(2,1)S(1)}, bf16[2,128,768]{2,1,0:T(8,128)(2,1)}, u32[]{:S(2)}, u32[]{:S(2)}) collective-permute-start(bf16[2,128,768]{2,1,0:T(8,128)(2,1)S(1)} %slice_bitcast_fusion.refs_6_), channel_id=1, source_target_pairs={{10,8},{11,9},{26,24},{27,25}} | collective-permute-start | bytes 1179656 | tf_op jit(solution)/shard_map/ppermute | solution.py:173
  9.5 2.0 %collective-permute-start = (bf16[2,128,768]{2,1,0:T(8,128)(2,1)}, bf16[2,128,768]{2,1,0:T(8,128)(2,1)}, u32[]{:S(2)}, u32[]{:S(2)}) collective-permute-start(bf16[2,128,768]{2,1,0:T(8,128)(2,1)} %slice_bitcast_fusion.1.refs_0_), channel_id=1, source_target_pairs={{10,12},{11,13},{26,28},{27,29}} | collective-permute-start | bytes 1179656 | tf_op jit(solution)/shard_map/ppermute | solution.py:173
  11.5 2.0 %collective-permute-start.1 = (bf16[2,128,768]{2,1,0:T(8,128)(2,1)}, bf16[2,128,768]{2,1,0:T(8,128)(2,1)}, u32[]{:S(2)}, u32[]{:S(2)}) collective-permute-start(bf16[2,128,768]{2,1,0:T(8,128)(2,1)} %slice_bitcast_fusion.1.refs_0_), channel_id=1, source_target_pairs={{10,14},{11,15},{26,30},{27,31}} | collective-permute-start | bytes 1179656 | tf_op jit(solution)/shard_map/ppermute | solution.py:173
  13.6 1.4 %collective-permute-done.11.refs_1_ = bf16[2,128,768]{2,1,0:T(8,128)(2,1)} collective-permute-done((bf16[2,128,768]{2,1,0:T(8,128)(2,1)S(1)}, bf16[2,128,768]{2,1,0:T(8,128)(2,1)}, u32[]{:S(2)}, u32[]{:S(2)}) %collective-permute-start.11) | collective-permute-done | bytes 393248 | tf_op jit(solution)/shard_map/ppermute | solution.py:173
  14.9 3.7 %copy-done.1 = bf16[2,2,2,768,768]{4,3,2,1,0:T(8,128)(2,1)S(1)} copy-done((bf16[2,2,2,768,768]{4,3,2,1,0:T(8,128)(2,1)S(1)}, bf16[2,2,2,768,768]{4,3,2,1,0:T(8,128)(2,1)}, u32[]{:S(2)}) %copy-start.1) | copy-done | bytes 9437208
  18.6 1.1 front_1_0.6.refs_2_.refs_7_
  21.1 6.1 %collective-permute-done.1.refs_1_ = bf16[2,128,768]{2,1,0:T(8,128)(2,1)} collective-permute-done((bf16[2,128,768]{2,1,0:T(8,128)(2,1)}, bf16[2,128,768]{2,1,0:T(8,128)(2,1)}, u32[]{:S(2)}, u32[]{:S(2)}) %collective-permute-start.1) | collective-permute-done | bytes 393248 | tf_op jit(solution)/shard_map/ppermute | solution.py:173
  27.3 1.1 front_0_0.6.refs_0_.refs_1_
  38.5 1.3 collective-permute-start.22
  39.8 1.3 collective-permute-start.23
  41.2 1.3 collective-permute-start.20
  42.5 1.3 collective-permute-start.21
  43.8 54.1 %collective-permute-done.22.refs_0_ = bf16[2,128,768]{2,1,0:T(8,128)(2,1)S(1)} collective-permute-done((bf16[2,128,768]{2,1,0:T(8,128)(2,1)S(1)}, bf16[2,128,768]{2,1,0:T(8,128)(2,1)S(1)}, u32[]{:S(2)}, u32[]{:S(2)}) %collective-permute-start.22) | collective-permute-done | bytes 393248 | tf_op jit(solution)/shard_map/ppermute | solution.py:173
  97.9 9.2 %collective-permute-done.23.refs_1_ = bf16[2,128,768]{2,1,0:T(8,128)(2,1)S(1)} collective-permute-done((bf16[2,128,768]{2,1,0:T(8,128)(2,1)S(1)}, bf16[2,128,768]{2,1,0:T(8,128)(2,1)S(1)}, u32[]{:S(2)}, u32[]{:S(2)}) %collective-permute-start.23) | collective-permute-done | bytes 393248 | tf_op jit(solution)/shard_map/ppermute | solution.py:173
  107.9 13.8 %collective-permute-done.20.refs_0_ = bf16[2,128,768]{2,1,0:T(8,128)(2,1)S(1)} collective-permute-done((bf16[2,128,768]{2,1,0:T(8,128)(2,1)S(1)}, bf16[2,128,768]{2,1,0:T(8,128)(2,1)S(1)}, u32[]{:S(2)}, u32[]{:S(2)}) %collective-permute-start.20) | collective-permute-done | bytes 393248 | tf_op jit(solution)/shard_map/ppermute | solution.py:173
  121.7 1.6 %front_0_0.11.refs_12_ = bf16[2,128,768]{2,1,0:T(8,128)(2,1)S(1)} custom-call(s32[1]{0:T(128)} %bitcast.device_ref, bf16[2,2,2,768,768]{4,3,2,1,0:T(8,128)(2,1)S(1)} %copy-done.1, bf16[2,2,128,768]{3,2,1,0:T(8,128)(2,1)S(1)} %bitcast.42, bf16[2,128,768]{2,1,0:T(8,128)(2,1)S(1)} %collective-permute-done.20.refs_0_, ...), custom_call_target="tpu_custom_call" | custom-call | flops 301989888 | bytes 1048576 | tf_op jit(solution)/shard_map/front_0_0/pallas_call | solution.py:134
  123.4 5.3 %interior.1 = (bf16[2,2,128,768]{3,2,1,0:T(8,128)(2,1)S(1)}, bf16[2,2,128,768]{3,2,1,0:T(8,128)(2,1)S(1)}) custom-call(s32[1]{0:T(128)} %bitcast.device_ref, bf16[2,2,2,768,768]{4,3,2,1,0:T(8,128)(2,1)S(1)} %bitcast.44, bf16[2,128,768]{2,1,0:T(8,128)(2,1)} %slice_bitcast_fusion.1.refs_0_, bf16[2,128,768]{2,1,0:T(8,128)(2,1)S(1)} %front_0_0.6.refs_0_.refs_1_, ...), custom_call_target="tpu_custom_call" | custom-call | tf_op jit(solution)/shard_map/interior/pallas_call | solution.py:246
  129.5 1.0 collective-permute-start.25
  130.6 1.2 constant_dynamic-slice_fusion
  131.8 1.7 %collective-permute-done.24.refs_1_ = bf16[2,2,128,384]{3,2,1,0:T(8,128)(2,1)S(1)} collective-permute-done((bf16[2,2,128,384]{3,2,1,0:T(8,128)(2,1)S(1)}, bf16[2,2,128,384]{3,2,1,0:T(8,128)(2,1)S(1)}, u32[]{:S(2)}, u32[]{:S(2)}) %collective-permute-start.24) | collective-permute-done | bytes 393248 | tf_op jit(solution)/shard_map/ppermute | solution.py:298
  133.6 2.2 %image.1 = f32[2,384,768]{2,1,0:T(8,128)} custom-call(bf16[2,2,128,384]{3,2,1,0:T(8,128)(2,1)S(1)} %get-tuple-element.10.refs_0_, bf16[2,2,128,384]{3,2,1,0:T(8,128)(2,1)S(1)} %collective-permute-done.24.refs_1_, bf16[2,2,128,768]{3,2,1,0:T(8,128)(2,1)S(1)} %get-tuple-element.8.refs_2_, bf16[2,2,128,768]{3,2,1,0:T(8,128)(2,1)S(1)} %collective-permute-done.25.refs_3_), custom_call_target="tpu_custom_call" | custom-call | tf_op jit(solution)/shard_map/image/pallas_call | solution.py:270
  (66 shorter events, 14.7 us)
Async XLA Ops:
  2.9 10.7 %collective-permute-start.10 = (bf16[2,128,768]{2,1,0:T(8,128)(2,1)S(1)}, bf16[2,128,768]{2,1,0:T(8,128)(2,1)}, u32[]{:S(2)}, u32[]{:S(2)}) collective-permute-start(bf16[2,128,768]{2,1,0:T(8,128)(2,1)S(1)} %slice_bitcast_fusion.refs_6_), channel_id=1, source_target_pairs={{10,6},{11,7},{26,22},{27,23}} | collective-permute-start | bytes 1179656 | tf_op jit(solution)/shard_map/ppermute | solution.py:173
  5.9 9.1 %collective-permute-start.11 = (bf16[2,128,768]{2,1,0:T(8,128)(2,1)S(1)}, bf16[2,128,768]{2,1,0:T(8,128)(2,1)}, u32[]{:S(2)}, u32[]{:S(2)}) collective-permute-start(bf16[2,128,768]{2,1,0:T(8,128)(2,1)S(1)} %slice_bitcast_fusion.refs_6_), channel_id=1, source_target_pairs={{10,8},{11,9},{26,24},{27,25}} | collective-permute-start | bytes 1179656 | tf_op jit(solution)/shard_map/ppermute | solution.py:173
  9.5 11.6 %collective-permute-start = (bf16[2,128,768]{2,1,0:T(8,128)(2,1)}, bf16[2,128,768]{2,1,0:T(8,128)(2,1)}, u32[]{:S(2)}, u32[]{:S(2)}) collective-permute-start(bf16[2,128,768]{2,1,0:T(8,128)(2,1)} %slice_bitcast_fusion.1.refs_0_), channel_id=1, source_target_pairs={{10,12},{11,13},{26,28},{27,29}} | collective-permute-start | bytes 1179656 | tf_op jit(solution)/shard_map/ppermute | solution.py:173
  11.5 15.7 %collective-permute-start.1 = (bf16[2,128,768]{2,1,0:T(8,128)(2,1)}, bf16[2,128,768]{2,1,0:T(8,128)(2,1)}, u32[]{:S(2)}, u32[]{:S(2)}) collective-permute-start(bf16[2,128,768]{2,1,0:T(8,128)(2,1)} %slice_bitcast_fusion.1.refs_0_), channel_id=1, source_target_pairs={{10,14},{11,15},{26,30},{27,31}} | collective-permute-start | bytes 1179656 | tf_op jit(solution)/shard_map/ppermute | solution.py:173
  19.7 10.0 %collective-permute-start.12 = (bf16[2,128,768]{2,1,0:T(8,128)(2,1)S(1)}, bf16[2,128,768]{2,1,0:T(8,128)(2,1)S(1)}, u32[]{:S(2)}, u32[]{:S(2)}) collective-permute-start(bf16[2,128,768]{2,1,0:T(8,128)(2,1)S(1)} %front_1_0.6.refs_2_.refs_7_), channel_id=1, source_target_pairs={{6,2},{8,4},{7,3},{9,5},{22,18},{24,20},{23,19},{25,21}} | collective-permute-start | bytes 1179656 | tf_op jit(solution)/shard_map/ppermute | solution.py:173
  20.4 9.4 %collective-permute-start.13 = (bf16[2,128,768]{2,1,0:T(8,128)(2,1)S(1)}, bf16[2,128,768]{2,1,0:T(8,128)(2,1)S(1)}, u32[]{:S(2)}, u32[]{:S(2)}) collective-permute-start(bf16[2,128,768]{2,1,0:T(8,128)(2,1)S(1)} %front_1_0.6.refs_2_.refs_7_), channel_id=1, source_target_pairs={{6,4},{7,5},{22,20},{23,21}} | collective-permute-start | bytes 1179656 | tf_op jit(solution)/shard_map/ppermute | solution.py:173
  28.4 2.8 %collective-permute-start.2 = (bf16[2,128,768]{2,1,0:T(8,128)(2,1)S(1)}, bf16[2,128,768]{2,1,0:T(8,128)(2,1)S(1)}, u32[]{:S(2)}, u32[]{:S(2)}) collective-permute-start(bf16[2,128,768]{2,1,0:T(8,128)(2,1)S(1)} %front_0_0.6.refs_0_.refs_1_), channel_id=1, source_target_pairs={{14,0},{15,1},{30,16},{31,17}} | collective-permute-start | bytes 1179656 | tf_op jit(solution)/shard_map/ppermute | solution.py:173
  29.1 2.1 %collective-permute-start.3 = (bf16[2,128,768]{2,1,0:T(8,128)(2,1)S(1)}, bf16[2,128,768]{2,1,0:T(8,128)(2,1)S(1)}, u32[]{:S(2)}, u32[]{:S(2)}) collective-permute-start(bf16[2,128,768]{2,1,0:T(8,128)(2,1)S(1)} %front_0_0.6.refs_0_.refs_1_), channel_id=1, source_target_pairs={{12,0},{14,2},{13,1},{15,3},{28,16},{30,18},{29,17},{31,19}} | collective-permute-start | bytes 1179656 | tf_op jit(solution)/shard_map/ppermute | solution.py:173
  29.8 2.8 %collective-permute-start.14 = (bf16[2,128,768]{2,1,0:T(8,128)(2,1)S(1)}, bf16[2,128,768]{2,1,0:T(8,128)(2,1)S(1)}, u32[]{:S(2)}, u32[]{:S(2)}) collective-permute-start(bf16[2,128,768]{2,1,0:T(8,128)(2,1)S(1)} %front_1_0.7.refs_2_.refs_8_), channel_id=1, source_target_pairs={{2,14},{4,0},{8,4},{3,15},{5,1},{9,5},{18,30},{20,16},{24,20},{19,... | collective-permute-start | bytes 1179656 | tf_op jit(solution)/shard_map/ppermute | solution.py:173
  30.5 2.1 %collective-permute-start.15 = (bf16[2,128,768]{2,1,0:T(8,128)(2,1)S(1)}, bf16[2,128,768]{2,1,0:T(8,128)(2,1)S(1)}, u32[]{:S(2)}, u32[]{:S(2)}) collective-permute-start(bf16[2,128,768]{2,1,0:T(8,128)(2,1)S(1)} %front_1_0.7.refs_2_.refs_8_), channel_id=1, source_target_pairs={{2,0},{8,6},{3,1},{9,7},{18,16},{24,22},{19,17},{25,23}} | collective-permute-start | bytes 1179656 | tf_op jit(solution)/shard_map/ppermute | solution.py:173
  31.2 2.8 %collective-permute-start.4 = (bf16[2,128,768]{2,1,0:T(8,128)(2,1)S(1)}, bf16[2,128,768]{2,1,0:T(8,128)(2,1)S(1)}, u32[]{:S(2)}, u32[]{:S(2)}) collective-permute-start(bf16[2,128,768]{2,1,0:T(8,128)(2,1)S(1)} %front_0_0.7.refs_1_.refs_2_), channel_id=1, source_target_pairs={{2,4},{12,14},{3,5},{13,15},{18,20},{28,30},{19,21},{29,31}} | collective-permute-start | bytes 1179656 | tf_op jit(solution)/shard_map/ppermute | solution.py:173
  32.6 2.8 %collective-permute-start.16 = (bf16[2,128,768]{2,1,0:T(8,128)(2,1)S(1)}, bf16[2,128,768]{2,1,0:T(8,128)(2,1)S(1)}, u32[]{:S(2)}, u32[]{:S(2)}) collective-permute-start(bf16[2,128,768]{2,1,0:T(8,128)(2,1)S(1)} %front_1_0.8.refs_2_.refs_9_), channel_id=1, source_target_pairs={{4,0},{6,2},{14,12},{5,1},{7,3},{15,13},{20,16},{22,18},{30,28},{2... | collective-permute-start | bytes 1179656 | tf_op jit(solution)/shard_map/ppermute | solution.py:173
  33.3 2.1 %collective-permute-start.17 = (bf16[2,128,768]{2,1,0:T(8,128)(2,1)S(1)}, bf16[2,128,768]{2,1,0:T(8,128)(2,1)S(1)}, u32[]{:S(2)}, u32[]{:S(2)}) collective-permute-start(bf16[2,128,768]{2,1,0:T(8,128)(2,1)S(1)} %front_1_0.8.refs_2_.refs_9_), channel_id=1, source_target_pairs={{0,12},{4,2},{1,13},{5,3},{16,28},{20,18},{17,29},{21,19}} | collective-permute-start | bytes 1179656 | tf_op jit(solution)/shard_map/ppermute | solution.py:173
  34.1 2.8 %collective-permute-start.6 = (bf16[2,128,768]{2,1,0:T(8,128)(2,1)S(1)}, bf16[2,128,768]{2,1,0:T(8,128)(2,1)S(1)}, u32[]{:S(2)}, u32[]{:S(2)}) collective-permute-start(bf16[2,128,768]{2,1,0:T(8,128)(2,1)S(1)} %front_0_0.8.refs_2_.refs_3_), channel_id=1, source_target_pairs={{0,2},{6,8},{1,3},{7,9},{16,18},{22,24},{17,19},{23,25}} | collective-permute-start | bytes 1179656 | tf_op jit(solution)/shard_map/ppermute | solution.py:173
  34.8 2.1 %collective-permute-start.7 = (bf16[2,128,768]{2,1,0:T(8,128)(2,1)S(1)}, bf16[2,128,768]{2,1,0:T(8,128)(2,1)S(1)}, u32[]{:S(2)}, u32[]{:S(2)}) collective-permute-start(bf16[2,128,768]{2,1,0:T(8,128)(2,1)S(1)} %front_0_0.8.refs_2_.refs_3_), channel_id=1, source_target_pairs={{0,4},{4,8},{14,2},{1,5},{5,9},{15,3},{16,20},{20,24},{30,18},{17,... | collective-permute-start | bytes 1179656 | tf_op jit(solution)/shard_map/ppermute | solution.py:173
  35.5 2.8 %collective-permute-start.18 = (bf16[2,128,768]{2,1,0:T(8,128)(2,1)S(1)}, bf16[2,128,768]{2,1,0:T(8,128)(2,1)S(1)}, u32[]{:S(2)}, u32[]{:S(2)}) collective-permute-start(bf16[2,128,768]{2,1,0:T(8,128)(2,1)S(1)} %front_1_0.9.refs_0_.refs_10_), channel_id=1, source_target_pairs={{0,12},{2,14},{1,13},{3,15},{16,28},{18,30},{17,29},{19,31}} | collective-permute-start | bytes 1179656 | tf_op jit(solution)/shard_map/ppermute | solution.py:173
  36.2 2.1 %collective-permute-start.19 = (bf16[2,128,768]{2,1,0:T(8,128)(2,1)S(1)}, bf16[2,128,768]{2,1,0:T(8,128)(2,1)S(1)}, u32[]{:S(2)}, u32[]{:S(2)}) collective-permute-start(bf16[2,128,768]{2,1,0:T(8,128)(2,1)S(1)} %front_1_0.9.refs_0_.refs_10_), channel_id=1, source_target_pairs={{0,14},{1,15},{16,30},{17,31}} | collective-permute-start | bytes 1179656 | tf_op jit(solution)/shard_map/ppermute | solution.py:173
  36.9 4.2 %collective-permute-start.8 = (bf16[2,128,768]{2,1,0:T(8,128)(2,1)S(1)}, bf16[2,128,768]{2,1,0:T(8,128)(2,1)S(1)}, u32[]{:S(2)}, u32[]{:S(2)}) collective-permute-start(bf16[2,128,768]{2,1,0:T(8,128)(2,1)S(1)} %front_0_0.9.refs_2_.refs_4_), channel_id=1, source_target_pairs={{4,6},{5,7},{20,22},{21,23}} | collective-permute-start | bytes 1179656 | tf_op jit(solution)/shard_map/ppermute | solution.py:173
  37.6 3.5 %collective-permute-start.9 = (bf16[2,128,768]{2,1,0:T(8,128)(2,1)S(1)}, bf16[2,128,768]{2,1,0:T(8,128)(2,1)S(1)}, u32[]{:S(2)}, u32[]{:S(2)}) collective-permute-start(bf16[2,128,768]{2,1,0:T(8,128)(2,1)S(1)} %front_0_0.9.refs_2_.refs_4_), channel_id=1, source_target_pairs={{2,6},{4,8},{3,7},{5,9},{18,22},{20,24},{19,23},{21,25}} | collective-permute-start | bytes 1179656 | tf_op jit(solution)/shard_map/ppermute | solution.py:173
  38.5 59.4 %collective-permute-start.22 = (bf16[2,128,768]{2,1,0:T(8,128)(2,1)S(1)}, bf16[2,128,768]{2,1,0:T(8,128)(2,1)S(1)}, u32[]{:S(2)}, u32[]{:S(2)}) collective-permute-start(bf16[2,128,768]{2,1,0:T(8,128)(2,1)S(1)} %front_1_0.10.refs_11_), channel_id=1, source_target_pairs={{12,10},{13,11},{28,26},{29,27}} | collective-permute-start | bytes 1179656 | tf_op jit(solution)/shard_map/ppermute | solution.py:173
  39.8 67.2 %collective-permute-start.23 = (bf16[2,128,768]{2,1,0:T(8,128)(2,1)S(1)}, bf16[2,128,768]{2,1,0:T(8,128)(2,1)S(1)}, u32[]{:S(2)}, u32[]{:S(2)}) collective-permute-start(bf16[2,128,768]{2,1,0:T(8,128)(2,1)S(1)} %front_1_0.10.refs_11_), channel_id=1, source_target_pairs={{14,10},{15,11},{30,26},{31,27}} | collective-permute-start | bytes 1179656 | tf_op jit(solution)/shard_map/ppermute | solution.py:173
  41.2 80.5 %collective-permute-start.20 = (bf16[2,128,768]{2,1,0:T(8,128)(2,1)S(1)}, bf16[2,128,768]{2,1,0:T(8,128)(2,1)S(1)}, u32[]{:S(2)}, u32[]{:S(2)}) collective-permute-start(bf16[2,128,768]{2,1,0:T(8,128)(2,1)S(1)} %front_0_0.10.refs_5_), channel_id=1, source_target_pairs={{8,10},{9,11},{24,26},{25,27}} | collective-permute-start | bytes 1179656 | tf_op jit(solution)/shard_map/ppermute | solution.py:173
  42.5 79.2 %collective-permute-start.21 = (bf16[2,128,768]{2,1,0:T(8,128)(2,1)S(1)}, bf16[2,128,768]{2,1,0:T(8,128)(2,1)S(1)}, u32[]{:S(2)}, u32[]{:S(2)}) collective-permute-start(bf16[2,128,768]{2,1,0:T(8,128)(2,1)S(1)} %front_0_0.10.refs_5_), channel_id=1, source_target_pairs={{6,10},{7,11},{22,26},{23,27}} | collective-permute-start | bytes 1179656 | tf_op jit(solution)/shard_map/ppermute | solution.py:173
  129.5 4.0 %collective-permute-start.25 = (bf16[2,2,128,768]{3,2,1,0:T(8,128)(2,1)S(1)}, bf16[2,2,128,768]{3,2,1,0:T(8,128)(2,1)S(1)}, u32[]{:S(2)}, u32[]{:S(2)}) collective-permute-start(bf16[2,2,128,768]{3,2,1,0:T(8,128)(2,1)S(1)} %get-tuple-element.8.refs_2_), channel_id=1, source_target_pairs={{0,1},{1,0},{2,3},{3,2},{4,5},{5,4},{6,7},{7,6},{8,9},{9,8},{10,11... | collective-permute-start | bytes 2359304 | tf_op jit(solution)/shard_map/ppermute | solution.py:299
  (10 other events, 68.3 us)

commit v3 on v2

v3 whole, which is shorter than its diff:
```python
import functools

import jax
import jax.numpy as jnp
import numpy as np
from jax import lax
from jax.experimental import pallas as pl
from jax.experimental.pallas import tpu as pltpu
from jax.sharding import PartitionSpec as P

GY = 4
TICKS = 6
BF16 = jnp.bfloat16
F32 = jnp.float32
TIMES = (((1,), (0,)), ((), ()))
TIMES_TRANSPOSED = (((1,), (1,)), ((), ()))
TRANSPOSED_TIMES = (((0,), (0,)), ((), ()))
VMEM_LIMIT = 12 * 1024 * 1024
CHUNKS_OF_4X4 = 1
PROGRAM_OF_4X4 = (
    (0, ((1, 0, 15, 5, 4),)),
    (0, ((1, 0, 15, 5, 3),)),
    (0, ((0, 0, 0, 5, 6),)),
    (1, 1, 0, ((14, 4),)),
    (0, ((1, 0, 14, 4, 2),)),
    (0, ((0, 0, 0, 5, 7),)),
    (1, 0, 0, ((1, 6), (2, 6))),
    (1, 1, 0, ((11, 3),)),
    (0, ((1, 0, 11, 3, 2), (0, 0, 2, 6, 7))),
    (0, ((1, 0, 11, 3, 1),)),
    (1, 0, 0, ((4, 7),)),
    (0, ((0, 0, 4, 7, 1),)),
    (1, 1, 0, ((7, 1), (13, 4))),
    (0, ((1, 0, 7, 1, 0),)),
    (0, ((1, 0, 7, 1, 7),)),
    (1, 0, 0, ((8, 1),)),
    (0, ((1, 0, 13, 4, 2),)),
    (1, 1, 0, ((10, 2),)),
    (0, ((1, 0, 10, 2, 0),)),
    (1, 1, 0, ((3, 7),)),
    (0, ((1, 0, 13, 2, 3),)),
    (1, 1, 0, ((9, 2),)),
    (0, ((1, 0, 9, 2, 0),)),
    (0, ((0, 0, 4, 1, 0),)),
    (1, 1, 0, ((6, 0),)),
    (0, ((0, 0, 1, 6, 0), (1, 0, 6, 0, 6), (0, 0, 8, 1, 3))),
    (1, 1, 0, ((12, 3), (5, 0))),
    (0, ((1, 0, 5, 0, 6), (1, 0, 12, 3, 1))),
    (0, ((1, 0, 9, 0, 1), (0, 0, 2, 6, 0), (1, 0, 3, 7, 6))),
    (1, 0, 0, ((3, 7), (5, 0))),
    (0, ((0, 0, 5, 0, 2),)),
    (0, ((0, 0, 8, 3, 2), (0, 0, 3, 7, 1))),
    (1, 0, 0, ((12, 3), (6, 0))),
    (0, ((0, 0, 6, 0, 2),)),
    (0, ((0, 0, 6, 0, 1),)),
    (1, 1, 0, ((8, 1),)),
    (1, 1, 0, ((2, 6), (1, 6))),
    (0, ((1, 0, 8, 1, 7), (0, 0, 12, 3, 4))),
    (1, 0, 0, ((9, 2),)),
    (1, 0, 0, ((7, 1),)),
    (0, ((0, 0, 7, 1, 3), (1, 0, 1, 6, 5), (0, 0, 9, 2, 4))),
    (1, 0, 0, ((10, 2),)),
    (0, ((0, 0, 10, 2, 4),)),
    (0, ((0, 0, 10, 2, 3), (1, 0, 5, 6, 7))),
    (1, 0, 0, ((11, 3),)),
    (0, ((0, 0, 11, 3, 5),)),
    (1, 1, 0, ((4, 7),)),
    (1, 0, 0, ((13, 4),)),
    (1, 0, 0, ((14, 4),)),
    (0, ((1, 0, 4, 7, 5),)),
    (0, ((0, 0, 14, 4, 5),)),
    (1, 1, 0, ((0, 5),)),
    (1, 0, 0, ((15, 5),)),
)


class Grid:
    def __init__(self, total, sub_local):
        self.total, self.sub_local = total, sub_local
        self.devices, self.rows = total // sub_local, total // GY

    def place(self, g):
        s = (g - GY - 1) % self.total
        return s // self.sub_local, s % self.sub_local

    def parents(self, way, g):
        row, col = g // GY, g % GY
        if way == 0:
            return [g - 1] * (col != 0) + [g - GY] * (row != 0)
        return [g + 1] * (col != GY - 1) + [g + GY] * (row != self.rows - 1)

    def depth(self, way, g):
        row, col = g // GY, g % GY
        return row + col if way == 0 else self.rows - 1 - row + GY - 1 - col


def tick_program(grid, chunks):
    deepest = grid.rows + GY - 2
    program = []

    def sends(way, chunk, tick):
        permutes = []
        for g in range(grid.total):
            if grid.depth(way, g) != tick:
                continue
            here = grid.place(g)[0]
            for p in grid.parents(way, g):
                there = grid.place(p)[0]
                message = (way, chunk, p, there, here)
                if there == here or any(message in permute for permute in permutes):
                    continue
                for permute in permutes:
                    if all(m[3] != there and m[4] != here for m in permute):
                        permute.append(message)
                        break
                else:
                    permutes.append([message])
        program.extend(("send", permute) for permute in permutes)

    chains = [(way, chunk) for chunk in range(chunks) for way in range(2)]
    for way, chunk in chains:
        sends(way, chunk, 1)
    for tick in range(1, deepest + 1):
        for way, chunk in chains:
            nodes = [(g, grid.place(g)[0]) for g in range(grid.total) if grid.depth(way, g) == tick]
            program.append(("compute", way, chunk, nodes))
            sends(way, chunk, tick + 1)
    return program


def bits(devices):
    return sum(1 << d for d in devices)


def flag(mask, device):
    return ((mask >> device) & 1) == 1


def apply_map(way, front, real_map, imag_map, shots):
    dims = TIMES_TRANSPOSED if way == 0 else TIMES
    by_real = lax.dot_general(front, real_map, dims, preferred_element_type=F32)
    by_imag = lax.dot_general(front, imag_map, dims, preferred_element_type=F32)
    if way == 0:
        return by_real[:shots] - by_imag[shots:], by_real[shots:] + by_imag[:shots]
    return by_real[:shots] + by_imag[shots:], by_real[shots:] - by_imag[:shots]


def compute_step(way, chunk, steps, place, groups, maps, origin, arrays, before, shots):
    width = origin.shape[-1]
    shape = (len(chunk), 2 * shots, width)

    def kernel(place_ref, maps_ref, origin_ref, _, *refs):
        ins, outs, total = refs[: len(arrays)], refs[len(arrays) : -1], refs[-1]
        me = place_ref[0] // groups
        for out, step in zip(outs, steps):
            everyone = bits(step["slot"])

            @pl.when(flag(everyone, me))
            def _():
                sources = [(ins[i], part, mask) for (i, part), mask in step["arrays"].items()]
                sources += [(outs[i], 0, mask) for i, mask in step["earlier"].items()]
                if all(mask == everyone for _, _, mask in sources):
                    first, part, _ = sources[0]
                    front = first[pl.ds(part, len(chunk))]
                    if len(sources) > 1:
                        front = front.astype(F32)
                        for ref, part, _ in sources[1:]:
                            front += ref[pl.ds(part, len(chunk))].astype(F32)
                        front = front.astype(BF16)
                else:
                    total[...] = jnp.zeros_like(total)
                    for ref, part, mask in sources:

                        @pl.when(flag(mask, me))
                        def _(ref=ref, part=part):
                            total[...] += ref[pl.ds(part, len(chunk))].astype(F32)

                    front = total[...].astype(BF16)
                sums = step["sums"]
                if sums:

                    @pl.when(flag(bits(sums), me))
                    def _():
                        out[...] = front

                if len(sums) == len(step["slot"]):
                    return

                @pl.when(flag(everyone & ~bits(sums), me))
                def _():
                    slot = jnp.int32(0)
                    for s in range(1, origin_ref.shape[1]):
                        slot += s * ((bits([d for d, own in step["slot"].items() if own == s]) >> me) & 1)
                    for i, f in enumerate(chunk):
                        real_part, imag_part = apply_map(way, front[i], maps_ref[f, slot, 0], maps_ref[f, slot, 1], shots)
                        start = origin_ref[f, slot].astype(F32)
                        out[i, :shots] = (start[:shots] + real_part).astype(BF16)
                        out[i, shots:] = (start[shots:] + imag_part).astype(BF16)

    vmem = pl.BlockSpec(memory_space=pltpu.VMEM)
    return pl.pallas_call(
        kernel,
        out_shape=[jax.ShapeDtypeStruct(shape, BF16)] * len(steps),
        in_specs=[pl.BlockSpec(memory_space=pltpu.SMEM), vmem, vmem, pl.BlockSpec(memory_space=pl.ANY)]
        + [vmem] * len(arrays),
        out_specs=[vmem] * len(steps),
        scratch_shapes=[pltpu.VMEM(shape, F32)],
        compiler_params=pltpu.CompilerParams(vmem_limit_bytes=VMEM_LIMIT),
        cost_estimate=pl.CostEstimate(flops=8 * shots * width * width, bytes_accessed=1 << 20, transcendentals=0),
        name=f"front_{way}_{chunk[0]}",
    )(place, maps, origin, before, *arrays)


def choose_step(found, place, groups):
    def kernel(place_ref, *refs):
        me = place_ref[0] // groups
        for ref, (_, mask) in zip(refs, found):

            @pl.when(flag(mask, me))
            def _(ref=ref):
                refs[-1][...] = ref[...]

    vmem = pl.BlockSpec(memory_space=pltpu.VMEM)
    return pl.pallas_call(
        kernel,
        out_shape=jax.ShapeDtypeStruct(found[0][0].shape, BF16),
        in_specs=[pl.BlockSpec(memory_space=pltpu.SMEM)] + [vmem] * len(found),
        out_specs=vmem,
        compiler_params=pltpu.CompilerParams(vmem_limit_bytes=VMEM_LIMIT),
        name="choose",
    )(place, *[array for array, _ in found])


def sweep(program, chunks, grid, place, groups, maps, origins, shots):
    per_chunk = maps.shape[0] // chunks
    arrays, where = [], {}
    before = place

    def keep(value):
        arrays.append(value)
        return len(arrays) - 1

    for way in range(2):
        for g in range(grid.total):
            if grid.depth(way, g) == 0:
                dev, slot = grid.place(g)
                index = keep(origins[way][:, slot])
                for chunk in range(chunks):
                    where[way, chunk, g, dev] = index, chunk * per_chunk

    def fetch(holders):
        found = []
        for (index, part), devices in holders.items():
            array = arrays[index]
            if array.shape[0] != per_chunk:
                array = array[part : part + per_chunk]
            found.append((array, bits(devices)))
        return found[0][0] if len(found) == 1 else choose_step(found, place, groups)

    for kind, *body in program:
        if kind == "send":
            (messages,) = body
            chunk = messages[0][1]
            both = chunk < 0
            payloads, holders = [], []
            for c in range(chunks if both else 1):
                found = {}
                for way, chunk, value, here, there in messages:
                    found.setdefault(where[way, c if both else chunk, value, here], []).append(here)
                holders.append(found)
            if both and len(holders[0]) == 1 and len({i for found in holders for i, _ in found}) == 1:
                payload = arrays[next(iter(holders[0]))[0]]
            else:
                payloads = [fetch(found) for found in holders]
                payload = payloads[0] if len(payloads) == 1 else jnp.concatenate(payloads, axis=0)
            index = keep(lax.ppermute(payload, "sub", sorted((m[3], m[4]) for m in messages)))
            for way, chunk, value, _, there in messages:
                for c in range(chunks) if both else (chunk,):
                    where[way, c, value, there] = index, c * per_chunk if both else 0
            continue
        way, chunk, nodes = body
        steps, operands, made, count = [], [], {}, {}
        for value, dev in nodes:
            position = count.get(dev, 0)
            count[dev] = position + 1
            if position == len(steps):
                steps.append({"slot": {}, "arrays": {}, "earlier": {}, "sums": []})
            step = steps[position]
            g = value % grid.total
            step["slot"][dev] = grid.place(g)[1]
            inputs = grid.parents(way, g)
            if value >= grid.total:
                step["sums"].append(dev)
            elif (way, chunk, value + grid.total, dev) in where:
                inputs = [value + grid.total]
            for v in inputs:
                if (v, dev) in made:
                    earlier = made[v, dev]
                    step["earlier"][earlier] = step["earlier"].get(earlier, 0) | 1 << dev
                else:
                    index, part = where[way, chunk, v, dev]
                    if index not in operands:
                        operands.append(index)
                    index = operands.index(index), part
                    step["arrays"][index] = step["arrays"].get(index, 0) | 1 << dev
            made[value, dev] = position
        results = compute_step(
            way, range(chunk * per_chunk, (chunk + 1) * per_chunk), steps, place, groups, maps, origins[way],
            [arrays[i] for i in operands], before, shots
        )
        before = results[0]
        kept = [keep(r) for r in results]
        for (value, dev), position in made.items():
            where[way, chunk, value, dev] = kept[position], 0
    finished = {}
    for way in range(2):
        for chunk in range(chunks):
            for g in range(grid.total):
                dev, slot = grid.place(g)
                index, part = where[way, chunk, g, dev]
                for f in range(per_chunk):
                    places = finished.setdefault((way, chunk * per_chunk + f, slot), {})
                    places.setdefault((index, part + f), []).append(dev)
    return {key: [(arrays[i], f, bits(devs)) for (i, f), devs in found.items()] for key, found in finished.items()}


def interior_step(finished, place, maps, shots, groups, name):
    freqs, subs, _, width, _ = maps.shape
    one_slot = all(len({s for way, _, s in finished if way == w}) == 1 for w in range(2))
    slots = 1 if one_slot else subs
    columns = 2 * shots
    share = width // groups
    arrays, choices = [], {}
    for key, found in finished.items():
        choices[key] = []
        for array, f, mask in found:
            if not any(array is a for a in arrays):
                arrays.append(array)
            choices[key].append((next(i for i, a in enumerate(arrays) if a is array), f, mask))

    def kernel(place_ref, maps_ref, *refs):
        ins, (kept, back, sent), (both, wave) = refs[: len(arrays)], refs[len(arrays) : -2], refs[-2:]
        me, core = place_ref[0] // groups, lax.rem(place_ref[0], groups)
        for f in range(freqs):
            for s in range(subs):
                found = [(way, *c) for way in range(2) for c in choices.get((way, f, s), ())]
                if not found:
                    continue
                anyone = functools.reduce(lambda a, b: a | b, [c[-1] for c in found])

                @pl.when(flag(anyone, me))
                def _(f=f, s=s, found=found):
                    ways = sorted({c[0] for c in found})
                    for way, i, part, mask in found:

                        @pl.when(flag(mask, me))
                        def _(i=i, part=part, at=ways.index(way) * columns):
                            both[at : at + columns] = ins[i][part]

                    front = both[: len(ways) * columns]
                    by_real = lax.dot_general(front, maps_ref[f, s, 0], TIMES_TRANSPOSED, preferred_element_type=F32)
                    by_imag = lax.dot_general(front, maps_ref[f, s, 1], TIMES_TRANSPOSED, preferred_element_type=F32)
                    for at, way in enumerate(ways):
                        a, b = at * columns, at * columns + shots
                        real_part = (by_real[a : a + shots] - by_imag[b : b + shots]).astype(BF16)
                        imag_part = (by_real[b : b + shots] + by_imag[a : a + shots]).astype(BF16)
                        if way == 0:
                            wave[:shots] = real_part
                            wave[shots:] = imag_part
                            kept[f, s % slots] = wave[:, pl.ds(pl.multiple_of(core * share, share), share)]
                            for shift in range(1, groups):
                                owner = lax.rem(core + shift, groups)
                                rows = wave[:, pl.ds(pl.multiple_of(owner * share, share), share)]
                                sent[shift - 1, f, s % slots, :, :share] = rows
                        else:
                            back[f, s % slots, :shots] = real_part
                            back[f, s % slots, shots:] = imag_part
                            for shift in range(1, groups):
                                sent[shift - 1, f, s % slots, :shots, share:] = real_part
                                sent[shift - 1, f, s % slots, shots:, share:] = imag_part

    vmem = pl.BlockSpec(memory_space=pltpu.VMEM)
    return pl.pallas_call(
        kernel,
        out_shape=[
            jax.ShapeDtypeStruct((freqs, slots, columns, share), BF16),
            jax.ShapeDtypeStruct((freqs, slots, columns, width), BF16),
            jax.ShapeDtypeStruct((groups - 1, freqs, slots, columns, share + width), BF16),
        ],
        in_specs=[pl.BlockSpec(memory_space=pltpu.SMEM)] + [vmem] * (1 + len(arrays)),
        out_specs=[vmem] * 3,
        scratch_shapes=[pltpu.VMEM((2 * columns, width), BF16), pltpu.VMEM((columns, width), BF16)],
        compiler_params=pltpu.CompilerParams(vmem_limit_bytes=VMEM_LIMIT),
        cost_estimate=pl.CostEstimate(
            flops=8 * freqs * subs * columns * width * width, bytes_accessed=1 << 24, transcendentals=0
        ),
        name=name,
    )(place, maps, *arrays)


def exchange(sent, groups):
    received = []
    for shift in range(1, groups):
        ring = [(i, (i + shift) % groups) for i in range(groups)]
        received.append(lax.ppermute(sent[shift - 1], "freq", ring))
    return received


def image_step(early, late, late_masks, place, scale):
    kept, back, others = early
    freqs, subs, columns, share = kept.shape
    width = back.shape[-1]
    groups = 1 + len(others)
    total = groups * freqs * columns

    def kernel(place_ref, *refs):
        out, rows, points = refs[-3:]
        sets = [refs[: 1 + groups], refs[1 + groups : -3]]
        me = place_ref[0] // groups

        def copy(refs, s, way):
            s = s % refs[0].shape[1]
            for g in range(groups):
                for f in range(freqs):
                    at = pl.ds((g * freqs + f) * columns, columns)
                    if g == 0:
                        if way == 0:
                            rows[at] = refs[0][f, s]
                        else:
                            points[at] = refs[1][f, s]
                    elif way == 0:
                        rows[at] = refs[1 + g][f, s, :, :share]
                    else:
                        points[at] = refs[1 + g][f, s, :, share:]

        for s in range(subs):
            for way in range(2):
                mask = late_masks[way, s]
                if mask == 0:
                    copy(sets[0], s, way)
                else:
                    pl.when(jnp.logical_not(flag(mask, me)))(functools.partial(copy, sets[0], s, way))
                    pl.when(flag(mask, me))(functools.partial(copy, sets[1], s, way))
            out[s] = lax.dot_general(rows[...], points[...], TRANSPOSED_TIMES, preferred_element_type=F32) * scale

    vmem = pl.BlockSpec(memory_space=pltpu.VMEM)
    operands = [kept, back, *others]
    if late is not None:
        operands += [late[0], late[1], *late[2]]
    return pl.pallas_call(
        kernel,
        out_shape=jax.ShapeDtypeStruct((subs, share, width), F32),
        in_specs=[pl.BlockSpec(memory_space=pltpu.SMEM)] + [vmem] * len(operands),
        out_specs=vmem,
        scratch_shapes=[pltpu.VMEM((total, share), BF16), pltpu.VMEM((total, width), BF16)],
        compiler_params=pltpu.CompilerParams(vmem_limit_bytes=VMEM_LIMIT),
        name="image",
    )(place, *operands)


def choose_shots(shot_index, place, bank_size):
    def kernel(_, index_ref, out_ref):
        rows = lax.broadcasted_iota(jnp.int32, out_ref.shape, 0)
        out_ref[...] = (rows == index_ref[...]).astype(F32).astype(BF16)

    return pl.pallas_call(
        kernel,
        out_shape=jax.ShapeDtypeStruct((bank_size, shot_index.shape[0]), BF16),
        in_specs=[pl.BlockSpec(memory_space=pltpu.SMEM), pl.BlockSpec(memory_space=pltpu.VMEM)],
        out_specs=pl.BlockSpec(memory_space=pltpu.VMEM),
        name="shots",
    )(place, shot_index[None, :])


def pick_shots(table, chooser):
    freqs, subs, width, _, _ = table.shape
    picked = jnp.einsum("fsxcb,bn->fscnx", table, chooser, preferred_element_type=F32)
    return picked.astype(BF16).reshape(freqs, subs, -1, width)


def make_image(finished, last, place, maps, shots, groups, scale):
    subs = maps.shape[1]
    late_masks = {(way, s): bits([d for d, slot in last[way] if slot == s]) for way in range(2) for s in range(subs)}
    early_fronts, late_fronts = {}, {}
    for (way, f, s), found in finished.items():
        mask = late_masks[way, s]
        for array, part, devices in found:
            if devices & ~mask:
                early_fronts.setdefault((way, f, s), []).append((array, part, devices & ~mask))
            if devices & mask:
                late_fronts.setdefault((way, f, s), []).append((array, part, devices & mask))
    kept, back, sent = interior_step(early_fronts, place, maps, shots, groups, "interior")
    early = kept, back, exchange(sent, groups)
    late = None
    if late_fronts:
        kept, back, sent = interior_step(late_fronts, place, maps, shots, groups, "interior_last")
        late = kept, back, exchange(sent, groups)
    return image_step(early, late, late_masks, place, scale)


def per_device(trace_map, interior_map, excitation, receiver_data, shot_index):
    freq_local, sub_local = trace_map.shape[:2]
    shots = shot_index.shape[0]
    bank_size = excitation.shape[4]
    grid = Grid(sub_local * lax.axis_size("sub"), sub_local)
    groups = lax.axis_size("freq")
    place = (lax.axis_index("sub") * groups + lax.axis_index("freq")).astype(jnp.int32).reshape(1)
    chooser = choose_shots(shot_index, place, bank_size)
    origins = (pick_shots(excitation, chooser), pick_shots(receiver_data, chooser))
    scale = (2.0 * shots * freq_local * groups) ** (-0.5)
    deepest = grid.rows + GY - 2
    last = [[], []]
    if deepest <= TICKS:
        for way in range(2):
            last[way] = [grid.place(g) for g in range(grid.total) if grid.depth(way, g) == deepest]
        chunks, program = choose_program(grid, freq_local)
        finished = sweep(program, chunks, grid, place, groups, trace_map, origins, shots)
    else:
        finished = jacobi(grid, place // groups, trace_map, origins, shots)
    return make_image(finished, last, place, interior_map, shots, groups, scale)


def choose_program(grid, freqs):
    if (grid.rows, grid.devices, freqs % CHUNKS_OF_4X4) != (4, 8, 0):
        return 1, tick_program(grid, 1)
    kinds = ("send", "compute")
    return CHUNKS_OF_4X4, [(kinds[kind], *body) for kind, *body in PROGRAM_OF_4X4]


def jacobi(grid, device, maps, origins, shots):
    chunks, subs = maps.shape[:2]
    reach = GY // subs
    count = grid.devices
    places = (device[0] * subs + jnp.arange(subs, dtype=jnp.int32) + GY + 1) % grid.total
    column, row = places % GY, places // GY

    def move(x, by):
        return lax.ppermute(x, "sub", [(i, (i + by) % count) for i in range(count)])

    def mask(flags):
        return flags.astype(F32)[None, :, None, None]

    forward, adjoint = origins
    for _ in range(TICKS):
        left = jnp.concatenate([move(forward[:, subs - 1 :], 1), forward[:, : subs - 1]], axis=1)
        above = move(forward, reach)
        right = jnp.concatenate([adjoint[:, 1:], move(adjoint[:, :1], -1)], axis=1)
        below = move(adjoint, -reach)
        forward_in = left.astype(F32) * mask(column != 0) + above.astype(F32) * mask(row != 0)
        adjoint_in = right.astype(F32) * mask(column != GY - 1) + below.astype(F32) * mask(row != grid.rows - 1)
        fronts = []
        for way, total in enumerate((forward_in, adjoint_in)):
            dims = "fsnm,fsckm->fscnk" if way == 0 else "fsnk,fsckm->fscnm"
            product = jnp.einsum(dims, total.astype(BF16), maps, preferred_element_type=F32)
            real, imag = product[:, :, 0], product[:, :, 1]
            sign = 1.0 if way == 0 else -1.0
            moved = jnp.concatenate(
                [
                    real[:, :, :shots] - sign * imag[:, :, shots:],
                    real[:, :, shots:] + sign * imag[:, :, :shots],
                ],
                axis=2,
            )
            fronts.append((origins[way].astype(F32) + moved).astype(BF16))
        forward, adjoint = fronts
    everyone = bits(range(count))
    return {
        (way, f, s): [(front[:, s], f, everyone)]
        for way, front in enumerate((forward, adjoint))
        for f in range(chunks)
        for s in range(subs)
    }


def solution(mesh):
    placed = (
        P("freq", ("survey", "sub"), None, None, None),
        P("freq", ("survey", "sub"), None, None, None),
        P("freq", ("survey", "sub"), None, None, None),
        P("freq", ("survey", "sub"), None, None, None),
        P("survey"),
    )
    return jax.shard_map(
        per_device,
        mesh=mesh,
        in_specs=placed,
        out_specs=P(("survey", "sub"), "freq", None),
        check_vma=False,
    )
```

time: 136 us -> 124 us (0.912)
  waiting for transfers between devices: 86.4 us -> 60.8 us
  starting transfers between devices: 26.3 us -> 38.9 us
  Pallas kernels: 12.4 us -> 14.7 us
  local copies, waits for them, and re-layouts: 8.09 us -> 5.82 us
    ppermute x24 -> x29, waiting for transfers between devices: 84.7 us -> 59.2 us  [sweep(): lax.ppermute(payload, 'sub', sorted(((m[3], m[4]) for m in messages)))]
    ppermute x2, starting transfers between devices: 1.1 us -> 12.5 us  [exchange(): received.append(lax.ppermute(sent[shift - 1], 'freq', ring))]
    pallas_call x1 -> x10, Pallas kernels: 5.27 us -> 9.01 us  [the longest x2 7.43 us: interior_step(): pl.pallas_call(kernel, out_shape=[jax.ShapeDtypeStruct((freqs, slots, col...]
    pallas_call x12 -> x24, Pallas kernels: 4.94 us -> 2.94 us  [compute_step(): pl.pallas_call(kernel, out_shape=[jax.ShapeDtypeStruct(shape, BF16)] * le...]
    ppermute x24 -> x29, starting transfers between devices: 25.2 us -> 26.4 us  [sweep(): lax.ppermute(payload, 'sub', sorted(((m[3], m[4]) for m in messages)))]
    unnamed x16 -> x20, local copies, waits for them, and re-layouts: 5.99 us -> 5.77 us
  transfers between devices with their start and end apart: 26 -> 31, of which waited for: 6 -> 7; matrix products, arithmetic and copies ran while one was open for 2% -> 1% of each run, Pallas kernels for 2% -> 9%
where the time goes in v3:
time: 124 us; the launch traced here: 123 us
  waiting for transfers between devices  60.8 us (49%)
  starting transfers between devices  38.9 us (31%)
  Pallas kernels  14.7 us (12%)
  local copies, waits for them, and re-layouts  5.82 us (5%)
  matrix products  2.24 us (2%)
    ppermute x29, waiting for transfers between devices, sweep(): lax.ppermute(payload, 'sub', sorted(((m[3], m[4]) for m in messages)))  59.2 us
    ppermute x29, starting transfers between devices, sweep(): lax.ppermute(payload, 'sub', sorted(((m[3], m[4]) for m in messages)))  26.4 us
    ppermute x2, starting transfers between devices, exchange(): received.append(lax.ppermute(sent[shift - 1], 'freq', ring))  12.5 us
    pallas_call x2, Pallas kernels, interior_step(): pl.pallas_call(kernel, out_shape=[jax.ShapeDtypeStruct((freqs, slots, col...  7.43 us
    unnamed x20, local copies, waits for them, and re-layouts  5.77 us
    pallas_call x24, Pallas kernels, compute_step(): pl.pallas_call(kernel, out_shape=[jax.ShapeDtypeStruct(shape, BF16)] * le...  2.94 us
    pallas_call x1, Pallas kernels, image_step(): pl.pallas_call(kernel, out_shape=jax.ShapeDtypeStruct((subs, share, width...  2.71 us
  transfers between devices with their start and end apart: 31, of which 7 were waited for; matrix products, arithmetic and copies ran while one was open for 1% of the time, Pallas kernels for 9%

profile of v3, /device:TPU:21, one launch (start us, length us, event | category | flops | bytes accessed | tf_op | source)
XLA Modules:
  0.0 123.2 jit_solution(15054588789395746708)
XLA Ops:
  0.0 1.4 %shots.1 = bf16[128,64]{1,0:T(8,128)(2,1)} custom-call(s32[1]{0:T(128)} %bitcast._.place_ref, s32[1,64]{1,0:T(1,128)} %bitcast.52), custom_call_target="tpu_custom_call" | custom-call | tf_op jit(solution)/shard_map/shots/pallas_call | solution.py:466
  1.4 1.6 %fusion.7 = bf16[64,2,2,768,2]{3,0,4,2,1:T(8,128)(2,1)S(1)} fusion(bf16[2,2,768,2,128]{4,3,2,1,0:T(2,128)(2,1)S(1)} %copy-done, bf16[128,64]{1,0:T(8,128)(2,1)} %shots.1), kind=kOutput, calls=%fused_computation.5 | convolution fusion | flops 101056512 | bytes 2375680 | tf_op jit(solution)/shard_map/fsxcb,bn->fscnx/dot_general | solution.py:477
  3.0 2.2 %collective-permute-start = (bf16[2,128,768]{2,1,0:T(8,128)(2,1)S(1)}, bf16[2,128,768]{2,1,0:T(8,128)(2,1)S(1)}, u32[]{:S(2)}, u32[]{:S(2)}) collective-permute-start(bf16[2,128,768]{2,1,0:T(8,128)(2,1)S(1)} %slice_bitcast_fusion.refs_25_), channel_id=1, source_target_pairs={{10,8},{11,9},{26,24},{27,25}} | collective-permute-start | bytes 1179656 | tf_op jit(solution)/shard_map/ppermute | solution.py:276
  5.9 1.7 %collective-permute-start.1 = (bf16[2,128,768]{2,1,0:T(8,128)(2,1)S(1)}, bf16[2,128,768]{2,1,0:T(8,128)(2,1)S(1)}, u32[]{:S(2)}, u32[]{:S(2)}) collective-permute-start(bf16[2,128,768]{2,1,0:T(8,128)(2,1)S(1)} %slice_bitcast_fusion.1.refs_0_), channel_id=1, source_target_pairs={{10,12},{11,13},{26,28},{27,29}} | collective-permute-start | bytes 1179656 | tf_op jit(solution)/shard_map/ppermute | solution.py:276
  7.6 1.3 %collective-permute-start.2 = (bf16[2,128,768]{2,1,0:T(8,128)(2,1)S(1)}, bf16[2,128,768]{2,1,0:T(8,128)(2,1)S(1)}, u32[]{:S(2)}, u32[]{:S(2)}) collective-permute-start(bf16[2,128,768]{2,1,0:T(8,128)(2,1)S(1)} %slice_bitcast_fusion.refs_25_), channel_id=1, source_target_pairs={{10,6},{11,7},{26,22},{27,23}} | collective-permute-start | bytes 1179656 | tf_op jit(solution)/shard_map/ppermute | solution.py:276
  9.0 1.3 %collective-permute-start.3 = (bf16[2,128,768]{2,1,0:T(8,128)(2,1)S(1)}, bf16[2,128,768]{2,1,0:T(8,128)(2,1)S(1)}, u32[]{:S(2)}, u32[]{:S(2)}) collective-permute-start(bf16[2,128,768]{2,1,0:T(8,128)(2,1)S(1)} %slice_bitcast_fusion.1.refs_0_), channel_id=1, source_target_pairs={{10,14},{11,15},{26,30},{27,31}} | collective-permute-start | bytes 1179656 | tf_op jit(solution)/shard_map/ppermute | solution.py:276
  10.3 2.6 %collective-permute-done.refs_0_ = bf16[2,128,768]{2,1,0:T(8,128)(2,1)S(1)} collective-permute-done((bf16[2,128,768]{2,1,0:T(8,128)(2,1)S(1)}, bf16[2,128,768]{2,1,0:T(8,128)(2,1)S(1)}, u32[]{:S(2)}, u32[]{:S(2)}) %collective-permute-start) | collective-permute-done | bytes 393248 | tf_op jit(solution)/shard_map/ppermute | solution.py:276
  12.9 3.7 %copy-done.1 = bf16[2,2,2,768,768]{4,3,2,1,0:T(8,128)(2,1)S(1)} copy-done((bf16[2,2,2,768,768]{4,3,2,1,0:T(8,128)(2,1)S(1)}, bf16[2,2,2,768,768]{4,3,2,1,0:T(8,128)(2,1)}, u32[]{:S(2)}) %copy-start.1) | copy-done | bytes 9437208
  17.5 6.3 %collective-permute-done.3.refs_0_ = bf16[2,128,768]{2,1,0:T(8,128)(2,1)S(1)} collective-permute-done((bf16[2,128,768]{2,1,0:T(8,128)(2,1)S(1)}, bf16[2,128,768]{2,1,0:T(8,128)(2,1)S(1)}, u32[]{:S(2)}, u32[]{:S(2)}) %collective-permute-start.3) | collective-permute-done | bytes 393248 | tf_op jit(solution)/shard_map/ppermute | solution.py:276
  36.5 1.3 %collective-permute-start.23 = (bf16[2,128,768]{2,1,0:T(8,128)(2,1)S(1)}, bf16[2,128,768]{2,1,0:T(8,128)(2,1)S(1)}, u32[]{:S(2)}, u32[]{:S(2)}) collective-permute-start(bf16[2,128,768]{2,1,0:T(8,128)(2,1)S(1)} %choose.12), channel_id=1, source_target_pairs={{2,6},{4,8},{12,10},{3,7},{5,9},{13,11},{18,22},{20,24},{28,26},{1... | collective-permute-start | bytes 1179656 | tf_op jit(solution)/shard_map/ppermute | solution.py:276
  40.0 38.6 %collective-permute-done.23.refs_1_.refs_0_ = bf16[2,128,768]{2,1,0:T(8,128)(2,1)S(1)} collective-permute-done((bf16[2,128,768]{2,1,0:T(8,128)(2,1)S(1)}, bf16[2,128,768]{2,1,0:T(8,128)(2,1)S(1)}, u32[]{:S(2)}, u32[]{:S(2)}) %collective-permute-start.23) | collective-permute-done | bytes 393248 | tf_op jit(solution)/shard_map/ppermute | solution.py:276
  78.5 1.3 %collective-permute-start.29 = (bf16[2,128,768]{2,1,0:T(8,128)(2,1)S(1)}, bf16[2,128,768]{2,1,0:T(8,128)(2,1)S(1)}, u32[]{:S(2)}, u32[]{:S(2)}) collective-permute-start(bf16[2,128,768]{2,1,0:T(8,128)(2,1)S(1)} %front_0_0.20._.refs_11_), channel_id=1, source_target_pairs={{6,10},{7,11},{22,26},{23,27}} | collective-permute-start | bytes 1179656 | tf_op jit(solution)/shard_map/ppermute | solution.py:276
  79.9 1.3 %collective-permute-start.27 = (bf16[2,128,768]{2,1,0:T(8,128)(2,1)S(1)}, bf16[2,128,768]{2,1,0:T(8,128)(2,1)S(1)}, u32[]{:S(2)}, u32[]{:S(2)}) collective-permute-start(bf16[2,128,768]{2,1,0:T(8,128)(2,1)S(1)} %front_1_0.22._.refs_14_), channel_id=1, source_target_pairs={{14,10},{15,11},{30,26},{31,27}} | collective-permute-start | bytes 1179656 | tf_op jit(solution)/shard_map/ppermute | solution.py:276
  81.3 1.6 %collective-permute-start.28 = (bf16[2,128,768]{2,1,0:T(8,128)(2,1)S(1)}, bf16[2,128,768]{2,1,0:T(8,128)(2,1)S(1)}, u32[]{:S(2)}, u32[]{:S(2)}) collective-permute-start(bf16[2,128,768]{2,1,0:T(8,128)(2,1)S(1)} %front_0_0.22.refs_6_._), channel_id=1, source_target_pairs={{8,10},{9,11},{24,26},{25,27}} | collective-permute-start | bytes 1179656 | tf_op jit(solution)/shard_map/ppermute | solution.py:276
  83.3 1.3 %slice-done.4 = s8[4194304]{0:T(1024)(128)(4,1)S(1)} async-done(((s8[9437184]{0:T(1024)(128)(4,1)}), s8[4194304]{0:T(1024)(128)(4,1)S(1)}, s32[]{:S(2)}) %slice-start.4) | async-done | bytes 4194328
  84.9 4.3 %interior.1 = (bf16[2,2,128,384]{3,2,1,0:T(8,128)(2,1)S(1)}, bf16[2,2,128,768]{3,2,1,0:T(8,128)(2,1)S(1)}, bf16[1,2,2,128,1152]{4,3,2,1,0:T(8,128)(2,1)S(1)}) custom-call(s32[1]{0:T(128)} %bitcast._.place_ref, bf16[2,2,2,768,768]{4,3,2,1,0:T(8,128)(2,1)S(1)} %bitcast.49, bf16[2,128,768]{2,1,0:T(8,128)(2,1)S(1)} %slice_bitcast_fusion.1.refs_0_, ...), custom_call_target="tpu_custom_call" | custom-call | flops 2415919104 | bytes 16777216 | tf_op jit(solution)/shard_map/interior/pallas_call | solution.py:383
  89.1 8.9 %collective-permute-start.26 = (bf16[2,2,128,1152]{3,2,1,0:T(8,128)(2,1)S(1)}, bf16[2,2,128,1152]{3,2,1,0:T(8,128)(2,1)S(1)}, u32[]{:S(2)}, u32[]{:S(2)}) collective-permute-start(bf16[2,2,128,1152]{3,2,1,0:T(8,128)(2,1)S(1)} %bitcast.50), channel_id=1, source_target_pairs={{0,1},{1,0},{2,3},{3,2},{4,5},{5,4},{6,7},{7,6},{8,9},{9,8},{10,11... | collective-permute-start | bytes 3538952 | tf_op jit(solution)/shard_map/ppermute | solution.py:405
  98.0 1.8 %collective-permute-done.27.refs_1_ = bf16[2,128,768]{2,1,0:T(8,128)(2,1)S(1)} collective-permute-done((bf16[2,128,768]{2,1,0:T(8,128)(2,1)S(1)}, bf16[2,128,768]{2,1,0:T(8,128)(2,1)S(1)}, u32[]{:S(2)}, u32[]{:S(2)}) %collective-permute-start.27) | collective-permute-done | bytes 393248 | tf_op jit(solution)/shard_map/ppermute | solution.py:276
  100.7 9.7 %collective-permute-done.28.refs_0_ = bf16[2,128,768]{2,1,0:T(8,128)(2,1)S(1)} collective-permute-done((bf16[2,128,768]{2,1,0:T(8,128)(2,1)S(1)}, bf16[2,128,768]{2,1,0:T(8,128)(2,1)S(1)}, u32[]{:S(2)}, u32[]{:S(2)}) %collective-permute-start.28) | collective-permute-done | bytes 393248 | tf_op jit(solution)/shard_map/ppermute | solution.py:276
  110.4 1.7 %front_0_0.23.refs_0_ = bf16[2,128,768]{2,1,0:T(8,128)(2,1)S(1)} custom-call(s32[1]{0:T(128)} %bitcast._.place_ref, bf16[2,2,2,768,768]{4,3,2,1,0:T(8,128)(2,1)S(1)} %bitcast.21, bf16[2,2,128,768]{3,2,1,0:T(8,128)(2,1)S(1)} %bitcast.47, bf16[2,128,768]{2,1,0:T(8,128)(2,1)S(1)} %front_1_0.23._.refs_1_, ...), custom_call_target="tpu_custom_call" | custom-call | flops 301989888 | bytes 1048576 | tf_op jit(solution)/shard_map/front_0_0/pallas_call | solution.py:201
  112.0 3.2 %interior_last.1 = (bf16[2,1,128,384]{3,2,1,0:T(8,128)(2,1)S(1)}, bf16[2,1,128,768]{3,2,1,0:T(8,128)(2,1)S(1)}, bf16[1,2,1,128,1152]{4,3,2,1,0:T(8,128)(2,1)S(1)}) custom-call(s32[1]{0:T(128)} %bitcast._.place_ref, bf16[2,2,2,768,768]{4,3,2,1,0:T(8,128)(2,1)S(1)} %bitcast.49, bf16[2,128,768]{2,1,0:T(8,128)(2,1)S(1)} %front_0_0.23.refs_0_, ...), custom_call_target="tpu_custom_call" | custom-call | flops 2415919104 | bytes 16777216 | tf_op jit(solution)/shard_map/interior_last/pallas_call | solution.py:383
  115.2 3.6 %collective-permute-start.30 = (bf16[2,1,128,1152]{3,2,1,0:T(8,128)(2,1)S(1)}, bf16[2,1,128,1152]{3,2,1,0:T(8,128)(2,1)S(1)}, u32[]{:S(2)}, u32[]{:S(2)}) collective-permute-start(bf16[2,1,128,1152]{3,2,1,0:T(8,128)(2,1)S(1)} %bitcast.51), channel_id=1, source_target_pairs={{0,1},{1,0},{2,3},{3,2},{4,5},{5,4},{6,7},{7,6},{8,9},{9,8},{10,11... | collective-permute-start | bytes 1769480 | tf_op jit(solution)/shard_map/ppermute | solution.py:405
  118.8 1.6 %collective-permute-done.30.refs_5_ = bf16[2,1,128,1152]{3,2,1,0:T(8,128)(2,1)S(1)} collective-permute-done((bf16[2,1,128,1152]{3,2,1,0:T(8,128)(2,1)S(1)}, bf16[2,1,128,1152]{3,2,1,0:T(8,128)(2,1)S(1)}, u32[]{:S(2)}, u32[]{:S(2)}) %collective-permute-start.30) | collective-permute-done | bytes 589856 | tf_op jit(solution)/shard_map/ppermute | solution.py:405
  120.4 2.7 %image.1 = f32[2,384,768]{2,1,0:T(8,128)} custom-call(s32[1]{0:T(128)} %bitcast._.place_ref, bf16[2,2,128,384]{3,2,1,0:T(8,128)(2,1)S(1)} %get-tuple-element.19.refs_0_, bf16[2,2,128,768]{3,2,1,0:T(8,128)(2,1)S(1)} %get-tuple-element.20.refs_1_, bf16[2,2,128,1152]{3,2,1,0:T(8,128)(2,1)S(1)} %collective-permute-done.26.refs_2_, ...), custom_call_target="tpu_custom_call" | custom-call | tf_op jit(solution)/shard_map/image/pallas_call | solution.py:450
  (99 shorter events, 17.7 us)
Async XLA Ops:
  3.0 9.9 %collective-permute-start = (bf16[2,128,768]{2,1,0:T(8,128)(2,1)S(1)}, bf16[2,128,768]{2,1,0:T(8,128)(2,1)S(1)}, u32[]{:S(2)}, u32[]{:S(2)}) collective-permute-start(bf16[2,128,768]{2,1,0:T(8,128)(2,1)S(1)} %slice_bitcast_fusion.refs_25_), channel_id=1, source_target_pairs={{10,8},{11,9},{26,24},{27,25}} | collective-permute-start | bytes 1179656 | tf_op jit(solution)/shard_map/ppermute | solution.py:276
  5.9 10.7 %collective-permute-start.1 = (bf16[2,128,768]{2,1,0:T(8,128)(2,1)S(1)}, bf16[2,128,768]{2,1,0:T(8,128)(2,1)S(1)}, u32[]{:S(2)}, u32[]{:S(2)}) collective-permute-start(bf16[2,128,768]{2,1,0:T(8,128)(2,1)S(1)} %slice_bitcast_fusion.1.refs_0_), channel_id=1, source_target_pairs={{10,12},{11,13},{26,28},{27,29}} | collective-permute-start | bytes 1179656 | tf_op jit(solution)/shard_map/ppermute | solution.py:276
  7.6 9.1 %collective-permute-start.2 = (bf16[2,128,768]{2,1,0:T(8,128)(2,1)S(1)}, bf16[2,128,768]{2,1,0:T(8,128)(2,1)S(1)}, u32[]{:S(2)}, u32[]{:S(2)}) collective-permute-start(bf16[2,128,768]{2,1,0:T(8,128)(2,1)S(1)} %slice_bitcast_fusion.refs_25_), channel_id=1, source_target_pairs={{10,6},{11,7},{26,22},{27,23}} | collective-permute-start | bytes 1179656 | tf_op jit(solution)/shard_map/ppermute | solution.py:276
  9.0 14.8 %collective-permute-start.3 = (bf16[2,128,768]{2,1,0:T(8,128)(2,1)S(1)}, bf16[2,128,768]{2,1,0:T(8,128)(2,1)S(1)}, u32[]{:S(2)}, u32[]{:S(2)}) collective-permute-start(bf16[2,128,768]{2,1,0:T(8,128)(2,1)S(1)} %slice_bitcast_fusion.1.refs_0_), channel_id=1, source_target_pairs={{10,14},{11,15},{26,30},{27,31}} | collective-permute-start | bytes 1179656 | tf_op jit(solution)/shard_map/ppermute | solution.py:276
  16.7 9.2 %collective-permute-start.4 = (bf16[2,128,768]{2,1,0:T(8,128)(2,1)S(1)}, bf16[2,128,768]{2,1,0:T(8,128)(2,1)S(1)}, u32[]{:S(2)}, u32[]{:S(2)}) collective-permute-start(bf16[2,128,768]{2,1,0:T(8,128)(2,1)S(1)} %front_1_0.13._.refs_0_.refs_24_), channel_id=1, source_target_pairs={{6,2},{7,3},{22,18},{23,19}} | collective-permute-start | bytes 1179656 | tf_op jit(solution)/shard_map/ppermute | solution.py:276
  23.8 3.6 %collective-permute-start.5 = (bf16[2,128,768]{2,1,0:T(8,128)(2,1)S(1)}, bf16[2,128,768]{2,1,0:T(8,128)(2,1)S(1)}, u32[]{:S(2)}, u32[]{:S(2)}) collective-permute-start(bf16[2,128,768]{2,1,0:T(8,128)(2,1)S(1)} %front_0_0.13._.refs_2_), channel_id=1, source_target_pairs={{14,2},{15,3},{30,18},{31,19}} | collective-permute-start | bytes 1179656 | tf_op jit(solution)/shard_map/ppermute | solution.py:276
  24.5 2.9 %collective-permute-start.6 = (bf16[2,128,768]{2,1,0:T(8,128)(2,1)S(1)}, bf16[2,128,768]{2,1,0:T(8,128)(2,1)S(1)}, u32[]{:S(2)}, u32[]{:S(2)}) collective-permute-start(bf16[2,128,768]{2,1,0:T(8,128)(2,1)S(1)} %choose.7), channel_id=1, source_target_pairs={{6,4},{12,14},{7,5},{13,15},{22,20},{28,30},{23,21},{29,31}} | collective-permute-start | bytes 1179656 | tf_op jit(solution)/shard_map/ppermute | solution.py:276
  27.5 3.5 %collective-permute-start.11 = (bf16[2,128,768]{2,1,0:T(8,128)(2,1)S(1)}, bf16[2,128,768]{2,1,0:T(8,128)(2,1)S(1)}, u32[]{:S(2)}, u32[]{:S(2)}) collective-permute-start(bf16[2,128,768]{2,1,0:T(8,128)(2,1)S(1)} %front_1_0.15._.refs_0_.refs_17_), channel_id=1, source_target_pairs={{4,0},{5,1},{20,16},{21,17}} | collective-permute-start | bytes 1179656 | tf_op jit(solution)/shard_map/ppermute | solution.py:276
  28.1 2.9 %collective-permute-start.10 = (bf16[2,128,768]{2,1,0:T(8,128)(2,1)S(1)}, bf16[2,128,768]{2,1,0:T(8,128)(2,1)S(1)}, u32[]{:S(2)}, u32[]{:S(2)}) collective-permute-start(bf16[2,128,768]{2,1,0:T(8,128)(2,1)S(1)} %front_1_0.14._.refs_22_), channel_id=1, source_target_pairs={{2,0},{3,1},{18,16},{19,17}} | collective-permute-start | bytes 1179656 | tf_op jit(solution)/shard_map/ppermute | solution.py:276
  28.9 2.9 %collective-permute-start.13 = (bf16[2,128,768]{2,1,0:T(8,128)(2,1)S(1)}, bf16[2,128,768]{2,1,0:T(8,128)(2,1)S(1)}, u32[]{:S(2)}, u32[]{:S(2)}) collective-permute-start(bf16[2,128,768]{2,1,0:T(8,128)(2,1)S(1)} %front_1_0.17._.refs_23_), channel_id=1, source_target_pairs={{4,0},{5,1},{20,16},{21,17}} | collective-permute-start | bytes 1179656 | tf_op jit(solution)/shard_map/ppermute | solution.py:276
  29.6 2.9 %collective-permute-start.12 = (bf16[2,128,768]{2,1,0:T(8,128)(2,1)S(1)}, bf16[2,128,768]{2,1,0:T(8,128)(2,1)S(1)}, u32[]{:S(2)}, u32[]{:S(2)}) collective-permute-start(bf16[2,128,768]{2,1,0:T(8,128)(2,1)S(1)} %collective-permute-done.9.refs_1_), channel_id=1, source_target_pairs={{4,6},{5,7},{20,22},{21,23}} | collective-permute-start | bytes 1179656 | tf_op jit(solution)/shard_map/ppermute | solution.py:276
  30.3 3.1 %collective-permute-start.14 = (bf16[2,128,768]{2,1,0:T(8,128)(2,1)S(1)}, bf16[2,128,768]{2,1,0:T(8,128)(2,1)S(1)}, u32[]{:S(2)}, u32[]{:S(2)}) collective-permute-start(bf16[2,128,768]{2,1,0:T(8,128)(2,1)S(1)} %collective-permute-done.5.refs_0_), channel_id=1, source_target_pairs={{2,0},{3,1},{18,16},{19,17}} | collective-permute-start | bytes 1179656 | tf_op jit(solution)/shard_map/ppermute | solution.py:276
  31.8 3.1 %collective-permute-start.16 = (bf16[2,128,768]{2,1,0:T(8,128)(2,1)S(1)}, bf16[2,128,768]{2,1,0:T(8,128)(2,1)S(1)}, u32[]{:S(2)}, u32[]{:S(2)}) collective-permute-start(bf16[2,128,768]{2,1,0:T(8,128)(2,1)S(1)} %choose.9), channel_id=1, source_target_pairs={{0,2},{12,0},{14,12},{1,3},{13,1},{15,13},{16,18},{28,16},{30,28},... | collective-permute-start | bytes 1179656 | tf_op jit(solution)/shard_map/ppermute | solution.py:276
  32.7 3.6 %collective-permute-start.17 = (bf16[2,128,768]{2,1,0:T(8,128)(2,1)S(1)}, bf16[2,128,768]{2,1,0:T(8,128)(2,1)S(1)}, u32[]{:S(2)}, u32[]{:S(2)}) collective-permute-start(bf16[2,128,768]{2,1,0:T(8,128)(2,1)S(1)} %front_1_0.19._.refs_18_), channel_id=1, source_target_pairs={{0,12},{6,2},{1,13},{7,3},{16,28},{22,18},{17,29},{23,19}} | collective-permute-start | bytes 1179656 | tf_op jit(solution)/shard_map/ppermute | solution.py:276
  33.5 2.9 %collective-permute-start.18 = (bf16[2,128,768]{2,1,0:T(8,128)(2,1)S(1)}, bf16[2,128,768]{2,1,0:T(8,128)(2,1)S(1)}, u32[]{:S(2)}, u32[]{:S(2)}) collective-permute-start(bf16[2,128,768]{2,1,0:T(8,128)(2,1)S(1)} %choose.10), channel_id=1, source_target_pairs={{6,4},{14,2},{7,5},{15,3},{22,20},{30,18},{23,21},{31,19}} | collective-permute-start | bytes 1179656 | tf_op jit(solution)/shard_map/ppermute | solution.py:276
  36.5 42.0 %collective-permute-start.23 = (bf16[2,128,768]{2,1,0:T(8,128)(2,1)S(1)}, bf16[2,128,768]{2,1,0:T(8,128)(2,1)S(1)}, u32[]{:S(2)}, u32[]{:S(2)}) collective-permute-start(bf16[2,128,768]{2,1,0:T(8,128)(2,1)S(1)} %choose.12), channel_id=1, source_target_pairs={{2,6},{4,8},{12,10},{3,7},{5,9},{13,11},{18,22},{20,24},{28,26},{1... | collective-permute-start | bytes 1179656 | tf_op jit(solution)/shard_map/ppermute | solution.py:276
  37.9 40.7 %collective-permute-start.22 = (bf16[2,128,768]{2,1,0:T(8,128)(2,1)S(1)}, bf16[2,128,768]{2,1,0:T(8,128)(2,1)S(1)}, u32[]{:S(2)}, u32[]{:S(2)}) collective-permute-start(bf16[2,128,768]{2,1,0:T(8,128)(2,1)S(1)} %choose.11), channel_id=1, source_target_pairs={{4,6},{12,14},{5,7},{13,15},{20,22},{28,30},{21,23},{29,31}} | collective-permute-start | bytes 1179656 | tf_op jit(solution)/shard_map/ppermute | solution.py:276
  38.6 41.2 %collective-permute-start.24 = (bf16[2,128,768]{2,1,0:T(8,128)(2,1)S(1)}, bf16[2,128,768]{2,1,0:T(8,128)(2,1)S(1)}, u32[]{:S(2)}, u32[]{:S(2)}) collective-permute-start(bf16[2,128,768]{2,1,0:T(8,128)(2,1)S(1)} %choose.13), channel_id=1, source_target_pairs={{2,14},{6,8},{3,15},{7,9},{18,30},{22,24},{19,31},{23,25}} | collective-permute-start | bytes 1179656 | tf_op jit(solution)/shard_map/ppermute | solution.py:276
  39.3 41.9 %collective-permute-start.25 = (bf16[2,128,768]{2,1,0:T(8,128)(2,1)S(1)}, bf16[2,128,768]{2,1,0:T(8,128)(2,1)S(1)}, u32[]{:S(2)}, u32[]{:S(2)}) collective-permute-start(bf16[2,128,768]{2,1,0:T(8,128)(2,1)S(1)} %front_0_0.19.refs_0_._.refs_5_), channel_id=1, source_target_pairs={{4,8},{5,9},{20,24},{21,25}} | collective-permute-start | bytes 1179656 | tf_op jit(solution)/shard_map/ppermute | solution.py:276
  78.5 31.8 %collective-permute-start.29 = (bf16[2,128,768]{2,1,0:T(8,128)(2,1)S(1)}, bf16[2,128,768]{2,1,0:T(8,128)(2,1)S(1)}, u32[]{:S(2)}, u32[]{:S(2)}) collective-permute-start(bf16[2,128,768]{2,1,0:T(8,128)(2,1)S(1)} %front_0_0.20._.refs_11_), channel_id=1, source_target_pairs={{6,10},{7,11},{22,26},{23,27}} | collective-permute-start | bytes 1179656 | tf_op jit(solution)/shard_map/ppermute | solution.py:276
  79.9 20.0 %collective-permute-start.27 = (bf16[2,128,768]{2,1,0:T(8,128)(2,1)S(1)}, bf16[2,128,768]{2,1,0:T(8,128)(2,1)S(1)}, u32[]{:S(2)}, u32[]{:S(2)}) collective-permute-start(bf16[2,128,768]{2,1,0:T(8,128)(2,1)S(1)} %front_1_0.22._.refs_14_), channel_id=1, source_target_pairs={{14,10},{15,11},{30,26},{31,27}} | collective-permute-start | bytes 1179656 | tf_op jit(solution)/shard_map/ppermute | solution.py:276
  81.3 29.1 %collective-permute-start.28 = (bf16[2,128,768]{2,1,0:T(8,128)(2,1)S(1)}, bf16[2,128,768]{2,1,0:T(8,128)(2,1)S(1)}, u32[]{:S(2)}, u32[]{:S(2)}) collective-permute-start(bf16[2,128,768]{2,1,0:T(8,128)(2,1)S(1)} %front_0_0.22.refs_6_._), channel_id=1, source_target_pairs={{8,10},{9,11},{24,26},{25,27}} | collective-permute-start | bytes 1179656 | tf_op jit(solution)/shard_map/ppermute | solution.py:276
  89.1 31.3 %collective-permute-start.26 = (bf16[2,2,128,1152]{3,2,1,0:T(8,128)(2,1)S(1)}, bf16[2,2,128,1152]{3,2,1,0:T(8,128)(2,1)S(1)}, u32[]{:S(2)}, u32[]{:S(2)}) collective-permute-start(bf16[2,2,128,1152]{3,2,1,0:T(8,128)(2,1)S(1)} %bitcast.50), channel_id=1, source_target_pairs={{0,1},{1,0},{2,3},{3,2},{4,5},{5,4},{6,7},{7,6},{8,9},{9,8},{10,11... | collective-permute-start | bytes 3538952 | tf_op jit(solution)/shard_map/ppermute | solution.py:405
  115.2 5.2 %collective-permute-start.30 = (bf16[2,1,128,1152]{3,2,1,0:T(8,128)(2,1)S(1)}, bf16[2,1,128,1152]{3,2,1,0:T(8,128)(2,1)S(1)}, u32[]{:S(2)}, u32[]{:S(2)}) collective-permute-start(bf16[2,1,128,1152]{3,2,1,0:T(8,128)(2,1)S(1)} %bitcast.51), channel_id=1, source_target_pairs={{0,1},{1,0},{2,3},{3,2},{4,5},{5,4},{6,7},{7,6},{8,9},{9,8},{10,11... | collective-permute-start | bytes 1769480 | tf_op jit(solution)/shard_map/ppermute | solution.py:405
  (17 other events, 65.1 us)

commit v4 on v3

--- a/solution.py
+++ b/solution.py
@@ -18,56 +18,61 @@
 VMEM_LIMIT = 12 * 1024 * 1024
 CHUNKS_OF_4X4 = 1
 PROGRAM_OF_4X4 = (
+    (0, ((1, 0, 15, 5, 3),)),
     (0, ((1, 0, 15, 5, 4),)),
-    (0, ((1, 0, 15, 5, 3),)),
     (0, ((0, 0, 0, 5, 6),)),
+    (1, 1, 0, ((11, 3),)),
+    (0, ((1, 0, 11, 3, 2), (0, 0, 0, 5, 7))),
+    (0, ((1, 0, 11, 3, 1),)),
     (1, 1, 0, ((14, 4),)),
     (0, ((1, 0, 14, 4, 2),)),
-    (0, ((0, 0, 0, 5, 7),)),
-    (1, 0, 0, ((1, 6), (2, 6))),
-    (1, 1, 0, ((11, 3),)),
-    (0, ((1, 0, 11, 3, 2), (0, 0, 2, 6, 7))),
-    (0, ((1, 0, 11, 3, 1),)),
+    (1, 1, 0, ((13, 4),)),
+    (1, 0, 0, ((1, 6),)),
     (1, 0, 0, ((4, 7),)),
-    (0, ((0, 0, 4, 7, 1),)),
-    (1, 1, 0, ((7, 1), (13, 4))),
+    (0, ((1, 0, 13, 4, 2), (0, 0, 4, 7, 1))),
+    (1, 1, 0, ((7, 1),)),
     (0, ((1, 0, 7, 1, 0),)),
-    (0, ((1, 0, 7, 1, 7),)),
-    (1, 0, 0, ((8, 1),)),
-    (0, ((1, 0, 13, 4, 2),)),
     (1, 1, 0, ((10, 2),)),
     (0, ((1, 0, 10, 2, 0),)),
-    (1, 1, 0, ((3, 7),)),
-    (0, ((1, 0, 13, 2, 3),)),
+    (0, ((1, 0, 7, 1, 7),)),
+    (1, 0, 0, ((2, 6),)),
     (1, 1, 0, ((9, 2),)),
     (0, ((1, 0, 9, 2, 0),)),
-    (0, ((0, 0, 4, 1, 0),)),
+    (0, ((1, 0, 13, 2, 3),)),
     (1, 1, 0, ((6, 0),)),
-    (0, ((0, 0, 1, 6, 0), (1, 0, 6, 0, 6), (0, 0, 8, 1, 3))),
+    (1, 0, 0, ((8, 1),)),
+    (0, ((0, 0, 8, 1, 3),)),
+    (0, ((0, 0, 4, 1, 0), (1, 0, 6, 0, 6), (0, 0, 2, 6, 7))),
+    (1, 1, 0, ((3, 7),)),
+    (0, ((0, 0, 1, 6, 0),)),
     (1, 1, 0, ((12, 3), (5, 0))),
-    (0, ((1, 0, 5, 0, 6), (1, 0, 12, 3, 1))),
-    (0, ((1, 0, 9, 0, 1), (0, 0, 2, 6, 0), (1, 0, 3, 7, 6))),
-    (1, 0, 0, ((3, 7), (5, 0))),
+    (0, ((0, 0, 2, 6, 0), (1, 0, 5, 0, 6), (1, 0, 12, 3, 1), (0, 0, 8, 1, 2))),
+    (0, ((1, 0, 9, 0, 1),)),
+    (1, 0, 0, ((12, 3),)),
+    (1, 0, 0, ((5, 0),)),
     (0, ((0, 0, 5, 0, 2),)),
-    (0, ((0, 0, 8, 3, 2), (0, 0, 3, 7, 1))),
-    (1, 0, 0, ((12, 3), (6, 0))),
-    (0, ((0, 0, 6, 0, 2),)),
+    (0, ((1, 0, 3, 7, 6),)),
+    (1, 0, 0, ((3, 7),)),
+    (1, 0, 0, ((6, 0),)),
+    (0, ((0, 0, 3, 7, 1), (0, 0, 6, 0, 2))),
     (0, ((0, 0, 6, 0, 1),)),
     (1, 1, 0, ((8, 1),)),
-    (1, 1, 0, ((2, 6), (1, 6))),
     (0, ((1, 0, 8, 1, 7), (0, 0, 12, 3, 4))),
     (1, 0, 0, ((9, 2),)),
-    (1, 0, 0, ((7, 1),)),
-    (0, ((0, 0, 7, 1, 3), (1, 0, 1, 6, 5), (0, 0, 9, 2, 4))),
+    (0, ((1, 0, 5, 6, 7), (0, 0, 9, 2, 4))),
+    (1, 1, 0, ((2, 6),)),
+    (1, 1, 0, ((1, 6),)),
     (1, 0, 0, ((10, 2),)),
     (0, ((0, 0, 10, 2, 4),)),
-    (0, ((0, 0, 10, 2, 3), (1, 0, 5, 6, 7))),
-    (1, 0, 0, ((11, 3),)),
+    (0, ((0, 0, 10, 2, 3),)),
+    (1, 0, 0, ((7, 1),)),
+    (0, ((0, 0, 7, 1, 3),)),
+    (1, 1, 0, ((4, 7),)),
+    (0, ((1, 0, 4, 7, 5),)),
+    (0, ((1, 0, 1, 6, 5),)),
+    (1, 0, 0, ((13, 4),)),
+    (1, 0, 0, ((11, 3), (14, 4))),
     (0, ((0, 0, 11, 3, 5),)),
-    (1, 1, 0, ((4, 7),)),
-    (1, 0, 0, ((13, 4),)),
-    (1, 0, 0, ((14, 4),)),
-    (0, ((1, 0, 4, 7, 5),)),
     (0, ((0, 0, 14, 4, 5),)),
     (1, 1, 0, ((0, 5),)),
     (1, 0, 0, ((15, 5),)),
@@ -136,13 +141,44 @@
     return ((mask >> device) & 1) == 1
 
 
-def apply_map(way, front, real_map, imag_map, shots):
-    dims = TIMES_TRANSPOSED if way == 0 else TIMES
-    by_real = lax.dot_general(front, real_map, dims, preferred_element_type=F32)
-    by_imag = lax.dot_general(front, imag_map, dims, preferred_element_type=F32)
-    if way == 0:
-        return by_real[:shots] - by_imag[shots:], by_real[shots:] + by_imag[:shots]
-    return by_real[:shots] + by_imag[shots:], by_real[shots:] - by_imag[:shots]
+def turn(front, shots):
+    blocks = [front[at : at + shots] for at in range(0, front.shape[0], shots)]
+    return jnp.concatenate([part for re, im in zip(blocks[::2], blocks[1::2]) for part in (-im, re)], axis=0)
+
+
+def times_map(front, real_map, imag_map, shots):
+    moved = lax.dot_general(real_map, front, TIMES_TRANSPOSED, preferred_element_type=F32)
+    moved += lax.dot_general(imag_map, turn(front, shots), TIMES_TRANSPOSED, preferred_element_type=F32)
+    return moved.T
+
+
+def times_turned_map(front, real_map, imag_map, shots):
+    by_real = lax.dot_general(front, real_map, TIMES, preferred_element_type=F32)
+    return by_real + lax.dot_general(turn(front, shots), imag_map, TIMES, preferred_element_type=F32)
+
+
+def times_adjoint(front, real_map, imag_map, shots):
+    by_real = lax.dot_general(front, real_map, TIMES, preferred_element_type=F32)
+    by_imag = lax.dot_general(turn(front, shots), imag_map, TIMES, preferred_element_type=F32)
+    return by_real - by_imag
+
+
+def transpose_step(maps):
+    def kernel(maps_ref, out_ref):
+        for f in range(maps.shape[0]):
+            for s in range(maps.shape[1]):
+                for c in range(maps.shape[2]):
+                    out_ref[f, s, c] = maps_ref[f, s, c].T
+
+    vmem = pl.BlockSpec(memory_space=pltpu.VMEM)
+    return pl.pallas_call(
+        kernel,
+        out_shape=jax.ShapeDtypeStruct(maps.shape, BF16),
+        in_specs=[vmem],
+        out_specs=vmem,
+        compiler_params=pltpu.CompilerParams(vmem_limit_bytes=2 * VMEM_LIMIT),
+        name="transpose",
+    )(maps)
 
 
 def compute_step(way, chunk, steps, place, groups, maps, origin, arrays, before, shots):
@@ -192,10 +228,9 @@
                     for s in range(1, origin_ref.shape[1]):
                         slot += s * ((bits([d for d, own in step["slot"].items() if own == s]) >> me) & 1)
                     for i, f in enumerate(chunk):
-                        real_part, imag_part = apply_map(way, front[i], maps_ref[f, slot, 0], maps_ref[f, slot, 1], shots)
-                        start = origin_ref[f, slot].astype(F32)
-                        out[i, :shots] = (start[:shots] + real_part).astype(BF16)
-                        out[i, shots:] = (start[shots:] + imag_part).astype(BF16)
+                        apply = times_adjoint if way else times_turned_map
+                        moved = apply(front[i], maps_ref[f, slot, 0], maps_ref[f, slot, 1], shots)
+                        out[i] = (origin_ref[f, slot].astype(F32) + moved).astype(BF16)
 
     vmem = pl.BlockSpec(memory_space=pltpu.VMEM)
     return pl.pallas_call(
@@ -234,7 +269,9 @@
 def sweep(program, chunks, grid, place, groups, maps, origins, shots):
     per_chunk = maps.shape[0] // chunks
     arrays, where = [], {}
+    done = 0
     before = place
+    before = turned = transpose_step(maps)
 
     def keep(value):
         arrays.append(value)
@@ -305,10 +342,11 @@
                     step["arrays"][index] = step["arrays"].get(index, 0) | 1 << dev
             made[value, dev] = position
         results = compute_step(
-            way, range(chunk * per_chunk, (chunk + 1) * per_chunk), steps, place, groups, maps, origins[way],
+            way, range(chunk * per_chunk, (chunk + 1) * per_chunk), steps, place, groups, maps if way else turned, origins[way],
             [arrays[i] for i in operands], before, shots
         )
-        before = results[0]
+        done += 1
+        before = turned if done == 0 else results[0]
         kept = [keep(r) for r in results]
         for (value, dev), position in made.items():
             where[way, chunk, value, dev] = kept[position], 0
@@ -358,26 +396,20 @@
                             both[at : at + columns] = ins[i][part]
 
                     front = both[: len(ways) * columns]
-                    by_real = lax.dot_general(front, maps_ref[f, s, 0], TIMES_TRANSPOSED, preferred_element_type=F32)
-                    by_imag = lax.dot_general(front, maps_ref[f, s, 1], TIMES_TRANSPOSED, preferred_element_type=F32)
+                    moved = times_map(front, maps_ref[f, s, 0], maps_ref[f, s, 1], shots).astype(BF16)
                     for at, way in enumerate(ways):
-                        a, b = at * columns, at * columns + shots
-                        real_part = (by_real[a : a + shots] - by_imag[b : b + shots]).astype(BF16)
-                        imag_part = (by_real[b : b + shots] + by_imag[a : a + shots]).astype(BF16)
+                        part = moved[at * columns : (at + 1) * columns]
                         if way == 0:
-                            wave[:shots] = real_part
-                            wave[shots:] = imag_part
+                            wave[...] = part
                             kept[f, s % slots] = wave[:, pl.ds(pl.multiple_of(core * share, share), share)]
                             for shift in range(1, groups):
                                 owner = lax.rem(core + shift, groups)
                                 rows = wave[:, pl.ds(pl.multiple_of(owner * share, share), share)]
                                 sent[shift - 1, f, s % slots, :, :share] = rows
                         else:
-                            back[f, s % slots, :shots] = real_part
-                            back[f, s % slots, shots:] = imag_part
+                            back[f, s % slots] = part
                             for shift in range(1, groups):
-                                sent[shift - 1, f, s % slots, :shots, share:] = real_part
-                                sent[shift - 1, f, s % slots, shots:, share:] = imag_part
+                                sent[shift - 1, f, s % slots, :, share:] = part
 
     vmem = pl.BlockSpec(memory_space=pltpu.VMEM)
     return pl.pallas_call(

time: 124 us -> 113 us (0.911)
  waiting for transfers between devices: 60.8 us -> 48.1 us
  Pallas kernels: 14.7 us -> 18.1 us
    ppermute x29 -> x30, waiting for transfers between devices: 59.2 us -> 46.4 us  [sweep(): lax.ppermute(payload, 'sub', sorted(((m[3], m[4]) for m in messages)))]
    pallas_call x0 -> x1, Pallas kernels: none -> 2.47 us  [transpose_step(): pl.pallas_call(kernel, out_shape=jax.ShapeDtypeStruct(maps.shape, BF16),...]
    pallas_call x2, Pallas kernels: 7.43 us -> 8.91 us  [interior_step(): pl.pallas_call(kernel, out_shape=[jax.ShapeDtypeStruct((freqs, slots, col...]
    pallas_call x24 -> x28, Pallas kernels: 2.94 us -> 2.42 us  [compute_step(): pl.pallas_call(kernel, out_shape=[jax.ShapeDtypeStruct(shape, BF16)] * le...]
    unnamed x20 -> x18, local copies, waits for them, and re-layouts: 5.77 us -> 5.35 us
    ppermute x29 -> x30, starting transfers between devices: 26.4 us -> 26.8 us  [sweep(): lax.ppermute(payload, 'sub', sorted(((m[3], m[4]) for m in messages)))]
  transfers between devices with their start and end apart: 31 -> 32, of which waited for: 7 -> 5; matrix products, arithmetic and copies ran while one was open for 1% -> 1% of each run, Pallas kernels for 9% -> 12%
where the time goes in v4:
time: 113 us
  waiting for transfers between devices  48.1 us (43%)
  starting transfers between devices  38.1 us (34%)
  Pallas kernels  18.1 us (16%)
  local copies, waits for them, and re-layouts  5.41 us (5%)
  matrix products  2.24 us (2%)
    ppermute x30, waiting for transfers between devices, sweep(): lax.ppermute(payload, 'sub', sorted(((m[3], m[4]) for m in messages)))  46.4 us
    ppermute x30, starting transfers between devices, sweep(): lax.ppermute(payload, 'sub', sorted(((m[3], m[4]) for m in messages)))  26.8 us
    ppermute x2, starting transfers between devices, exchange(): received.append(lax.ppermute(sent[shift - 1], 'freq', ring))  11.3 us
    pallas_call x2, Pallas kernels, interior_step(): pl.pallas_call(kernel, out_shape=[jax.ShapeDtypeStruct((freqs, slots, col...  8.91 us
    unnamed x18, local copies, waits for them, and re-layouts  5.35 us
    pallas_call x1, Pallas kernels, image_step(): pl.pallas_call(kernel, out_shape=jax.ShapeDtypeStruct((subs, share, width...  2.71 us
    pallas_call x1, Pallas kernels, transpose_step(): pl.pallas_call(kernel, out_shape=jax.ShapeDtypeStruct(maps.shape, BF16),...  2.47 us
    pallas_call x28, Pallas kernels, compute_step(): pl.pallas_call(kernel, out_shape=[jax.ShapeDtypeStruct(shape, BF16)] * le...  2.42 us
  transfers between devices with their start and end apart: 32, of which 5 were waited for; matrix products, arithmetic and copies ran while one was open for 1% of the time, Pallas kernels for 12%

profile of v4, /device:TPU:21, one launch (start us, length us, event | category | flops | bytes accessed | tf_op | source)
XLA Modules:
  0.0 112.7 jit_solution(14573171733152669338)
XLA Ops:
  0.0 1.4 %shots.1 = bf16[128,64]{1,0:T(8,128)(2,1)} custom-call(s32[1]{0:T(128)} %bitcast._.place_ref, s32[1,64]{1,0:T(1,128)} %bitcast.54), custom_call_target="tpu_custom_call" | custom-call | tf_op jit(solution)/shard_map/shots/pallas_call | solution.py:498
  1.4 1.6 %fusion.7 = bf16[64,2,2,768,2]{3,0,4,2,1:T(8,128)(2,1)S(1)} fusion(bf16[2,2,768,2,128]{4,3,2,1,0:T(2,128)(2,1)S(1)} %copy-done, bf16[128,64]{1,0:T(8,128)(2,1)} %shots.1), kind=kOutput, calls=%fused_computation.5 | convolution fusion | flops 101056512 | bytes 2375680 | tf_op jit(solution)/shard_map/fsxcb,bn->fscnx/dot_general | solution.py:509
  3.0 2.1 %collective-permute-start = (bf16[2,128,768]{2,1,0:T(8,128)(2,1)S(1)}, bf16[2,128,768]{2,1,0:T(8,128)(2,1)S(1)}, u32[]{:S(2)}, u32[]{:S(2)}) collective-permute-start(bf16[2,128,768]{2,1,0:T(8,128)(2,1)S(1)} %slice_bitcast_fusion.refs_27_), channel_id=1, source_target_pairs={{10,6},{11,7},{26,22},{27,23}} | collective-permute-start | bytes 1179656 | tf_op jit(solution)/shard_map/ppermute | solution.py:313
  5.1 1.3 %collective-permute-start.1 = (bf16[2,128,768]{2,1,0:T(8,128)(2,1)S(1)}, bf16[2,128,768]{2,1,0:T(8,128)(2,1)S(1)}, u32[]{:S(2)}, u32[]{:S(2)}) collective-permute-start(bf16[2,128,768]{2,1,0:T(8,128)(2,1)S(1)} %slice_bitcast_fusion.refs_27_), channel_id=1, source_target_pairs={{10,8},{11,9},{26,24},{27,25}} | collective-permute-start | bytes 1179656 | tf_op jit(solution)/shard_map/ppermute | solution.py:313
  7.2 1.3 %collective-permute-start.2 = (bf16[2,128,768]{2,1,0:T(8,128)(2,1)S(1)}, bf16[2,128,768]{2,1,0:T(8,128)(2,1)S(1)}, u32[]{:S(2)}, u32[]{:S(2)}) collective-permute-start(bf16[2,128,768]{2,1,0:T(8,128)(2,1)S(1)} %slice_bitcast_fusion.1.refs_1_.refs_0_), channel_id=1, source_target_pairs={{10,12},{11,13},{26,28},{27,29}} | collective-permute-start | bytes 1179656 | tf_op jit(solution)/shard_map/ppermute | solution.py:313
  8.5 3.7 %copy-done.2 = bf16[2,2,2,768,768]{4,3,2,1,0:T(8,128)(2,1)S(1)} copy-done((bf16[2,2,2,768,768]{4,3,2,1,0:T(8,128)(2,1)S(1)}, bf16[2,2,2,768,768]{4,3,2,1,0:T(8,128)(2,1)}, u32[]{:S(2)}) %copy-start.2) | copy-done | bytes 9437208
  12.2 2.5 %transpose.9._.maps_ref = bf16[2,2,2,768,768]{4,3,2,1,0:T(8,128)(2,1)S(1)} custom-call(bf16[2,2,2,768,768]{4,3,2,1,0:T(8,128)(2,1)S(1)} %copy-done.2), custom_call_target="tpu_custom_call" | custom-call | tf_op jit(solution)/shard_map/transpose/pallas_call | solution.py:174
  14.7 1.2 %copy-done.3 = bf16[2,2,2,768,768]{4,3,2,1,0:T(8,128)(2,1)S(1)} copy-done((bf16[2,2,2,768,768]{4,3,2,1,0:T(8,128)(2,1)S(1)}, bf16[2,2,2,768,768]{4,3,2,1,0:T(8,128)(2,1)}, u32[]{:S(2)}) %copy-start.3) | copy-done | bytes 9437208
  15.9 1.3 %collective-permute-start.3 = (bf16[2,128,768]{2,1,0:T(8,128)(2,1)S(1)}, bf16[2,128,768]{2,1,0:T(8,128)(2,1)S(1)}, u32[]{:S(2)}, u32[]{:S(2)}) collective-permute-start(bf16[2,128,768]{2,1,0:T(8,128)(2,1)S(1)} %choose.7), channel_id=1, source_target_pairs={{6,4},{10,14},{7,5},{11,15},{22,20},{26,30},{23,21},{27,31}} | collective-permute-start | bytes 1179656 | tf_op jit(solution)/shard_map/ppermute | solution.py:313
  18.7 6.3 %collective-permute-done.3.refs_0_ = bf16[2,128,768]{2,1,0:T(8,128)(2,1)S(1)} collective-permute-done((bf16[2,128,768]{2,1,0:T(8,128)(2,1)S(1)}, bf16[2,128,768]{2,1,0:T(8,128)(2,1)S(1)}, u32[]{:S(2)}, u32[]{:S(2)}) %collective-permute-start.3) | collective-permute-done | bytes 393248 | tf_op jit(solution)/shard_map/ppermute | solution.py:313
  39.8 1.3 %collective-permute-start.27 = (bf16[2,128,768]{2,1,0:T(8,128)(2,1)S(1)}, bf16[2,128,768]{2,1,0:T(8,128)(2,1)S(1)}, u32[]{:S(2)}, u32[]{:S(2)}) collective-permute-start(bf16[2,128,768]{2,1,0:T(8,128)(2,1)S(1)} %front_1_0.25._.refs_21_), channel_id=1, source_target_pairs={{12,10},{13,11},{28,26},{29,27}} | collective-permute-start | bytes 1179656 | tf_op jit(solution)/shard_map/ppermute | solution.py:313
  41.4 1.3 %collective-permute-start.28 = (bf16[2,128,768]{2,1,0:T(8,128)(2,1)S(1)}, bf16[2,128,768]{2,1,0:T(8,128)(2,1)S(1)}, u32[]{:S(2)}, u32[]{:S(2)}) collective-permute-start(bf16[2,128,768]{2,1,0:T(8,128)(2,1)S(1)} %front_1_0.26._.refs_15_), channel_id=1, source_target_pairs={{14,10},{15,11},{30,26},{31,27}} | collective-permute-start | bytes 1179656 | tf_op jit(solution)/shard_map/ppermute | solution.py:313
  42.8 1.6 %collective-permute-start.29 = (bf16[2,128,768]{2,1,0:T(8,128)(2,1)S(1)}, bf16[2,128,768]{2,1,0:T(8,128)(2,1)S(1)}, u32[]{:S(2)}, u32[]{:S(2)}) collective-permute-start(bf16[2,128,768]{2,1,0:T(8,128)(2,1)S(1)} %front_0_0.26.refs_7_._), channel_id=1, source_target_pairs={{8,10},{9,11},{24,26},{25,27}} | collective-permute-start | bytes 1179656 | tf_op jit(solution)/shard_map/ppermute | solution.py:313
  44.4 1.6 %collective-permute-start.30 = (bf16[2,128,768]{2,1,0:T(8,128)(2,1)S(1)}, bf16[2,128,768]{2,1,0:T(8,128)(2,1)S(1)}, u32[]{:S(2)}, u32[]{:S(2)}) collective-permute-start(bf16[2,128,768]{2,1,0:T(8,128)(2,1)S(1)} %front_0_0.26.refs_7_._), channel_id=1, source_target_pairs={{6,10},{7,11},{22,26},{23,27}} | collective-permute-start | bytes 1179656 | tf_op jit(solution)/shard_map/ppermute | solution.py:313
  46.4 6.2 %interior.1 = (bf16[2,2,128,384]{3,2,1,0:T(8,128)(2,1)S(1)}, bf16[2,2,128,768]{3,2,1,0:T(8,128)(2,1)S(1)}, bf16[1,2,2,128,1152]{4,3,2,1,0:T(8,128)(2,1)S(1)}) custom-call(s32[1]{0:T(128)} %bitcast._.place_ref, bf16[2,2,2,768,768]{4,3,2,1,0:T(8,128)(2,1)S(1)} %bitcast.51, bf16[2,128,768]{2,1,0:T(8,128)(2,1)S(1)} %slice_bitcast_fusion.1.refs_1_.refs_0_, ...), custom_call_target="tpu_custom_call" | custom-call | flops 2415919104 | bytes 16777216 | tf_op jit(solution)/shard_map/interior/pallas_call | solution.py:415
  52.6 1.6 %collective-permute-start.26 = (bf16[2,2,128,1152]{3,2,1,0:T(8,128)(2,1)S(1)}, bf16[2,2,128,1152]{3,2,1,0:T(8,128)(2,1)S(1)}, u32[]{:S(2)}, u32[]{:S(2)}) collective-permute-start(bf16[2,2,128,1152]{3,2,1,0:T(8,128)(2,1)S(1)} %bitcast.52), channel_id=1, source_target_pairs={{0,1},{1,0},{2,3},{3,2},{4,5},{5,4},{6,7},{7,6},{8,9},{9,8},{10,11... | collective-permute-start | bytes 3538952 | tf_op jit(solution)/shard_map/ppermute | solution.py:437
  54.2 22.4 %collective-permute-done.27.refs_0_ = bf16[2,128,768]{2,1,0:T(8,128)(2,1)S(1)} collective-permute-done((bf16[2,128,768]{2,1,0:T(8,128)(2,1)S(1)}, bf16[2,128,768]{2,1,0:T(8,128)(2,1)S(1)}, u32[]{:S(2)}, u32[]{:S(2)}) %collective-permute-start.27) | collective-permute-done | bytes 393248 | tf_op jit(solution)/shard_map/ppermute | solution.py:313
  76.6 9.3 %collective-permute-done.28.refs_1_ = bf16[2,128,768]{2,1,0:T(8,128)(2,1)S(1)} collective-permute-done((bf16[2,128,768]{2,1,0:T(8,128)(2,1)S(1)}, bf16[2,128,768]{2,1,0:T(8,128)(2,1)S(1)}, u32[]{:S(2)}, u32[]{:S(2)}) %collective-permute-start.28) | collective-permute-done | bytes 393248 | tf_op jit(solution)/shard_map/ppermute | solution.py:313
  85.8 0.8 front_1_0.27._.refs_1_
  86.7 8.5 %collective-permute-done.29.refs_0_ = bf16[2,128,768]{2,1,0:T(8,128)(2,1)S(1)} collective-permute-done((bf16[2,128,768]{2,1,0:T(8,128)(2,1)S(1)}, bf16[2,128,768]{2,1,0:T(8,128)(2,1)S(1)}, u32[]{:S(2)}, u32[]{:S(2)}) %collective-permute-start.29) | collective-permute-done | bytes 393248 | tf_op jit(solution)/shard_map/ppermute | solution.py:313
  95.9 2.7 %interior_last.1 = (bf16[2,1,128,384]{3,2,1,0:T(8,128)(2,1)S(1)}, bf16[2,1,128,768]{3,2,1,0:T(8,128)(2,1)S(1)}, bf16[1,2,1,128,1152]{4,3,2,1,0:T(8,128)(2,1)S(1)}) custom-call(s32[1]{0:T(128)} %bitcast._.place_ref, bf16[2,2,2,768,768]{4,3,2,1,0:T(8,128)(2,1)S(1)} %bitcast.51, bf16[2,128,768]{2,1,0:T(8,128)(2,1)S(1)} %front_0_0.27.refs_0_, ...), custom_call_target="tpu_custom_call" | custom-call | flops 2415919104 | bytes 16777216 | tf_op jit(solution)/shard_map/interior_last/pallas_call | solution.py:415
  98.7 9.7 %collective-permute-start.31 = (bf16[2,1,128,1152]{3,2,1,0:T(8,128)(2,1)S(1)}, bf16[2,1,128,1152]{3,2,1,0:T(8,128)(2,1)S(1)}, u32[]{:S(2)}, u32[]{:S(2)}) collective-permute-start(bf16[2,1,128,1152]{3,2,1,0:T(8,128)(2,1)S(1)} %bitcast.53), channel_id=1, source_target_pairs={{0,1},{1,0},{2,3},{3,2},{4,5},{5,4},{6,7},{7,6},{8,9},{9,8},{10,11... | collective-permute-start | bytes 1769480 | tf_op jit(solution)/shard_map/ppermute | solution.py:437
  108.4 1.6 %collective-permute-done.31.refs_5_ = bf16[2,1,128,1152]{3,2,1,0:T(8,128)(2,1)S(1)} collective-permute-done((bf16[2,1,128,1152]{3,2,1,0:T(8,128)(2,1)S(1)}, bf16[2,1,128,1152]{3,2,1,0:T(8,128)(2,1)S(1)}, u32[]{:S(2)}, u32[]{:S(2)}) %collective-permute-start.31) | collective-permute-done | bytes 589856 | tf_op jit(solution)/shard_map/ppermute | solution.py:437
  110.0 2.7 %image.1 = f32[2,384,768]{2,1,0:T(8,128)} custom-call(s32[1]{0:T(128)} %bitcast._.place_ref, bf16[2,2,128,384]{3,2,1,0:T(8,128)(2,1)S(1)} %get-tuple-element.11.refs_0_, bf16[2,2,128,768]{3,2,1,0:T(8,128)(2,1)S(1)} %get-tuple-element.12.refs_1_, bf16[2,2,128,1152]{3,2,1,0:T(8,128)(2,1)S(1)} %collective-permute-done.26.refs_2_, ...), custom_call_target="tpu_custom_call" | custom-call | tf_op jit(solution)/shard_map/image/pallas_call | solution.py:482
  (103 shorter events, 18.1 us)
Async XLA Ops:
  3.0 11.7 %collective-permute-start = (bf16[2,128,768]{2,1,0:T(8,128)(2,1)S(1)}, bf16[2,128,768]{2,1,0:T(8,128)(2,1)S(1)}, u32[]{:S(2)}, u32[]{:S(2)}) collective-permute-start(bf16[2,128,768]{2,1,0:T(8,128)(2,1)S(1)} %slice_bitcast_fusion.refs_27_), channel_id=1, source_target_pairs={{10,6},{11,7},{26,22},{27,23}} | collective-permute-start | bytes 1179656 | tf_op jit(solution)/shard_map/ppermute | solution.py:313
  5.1 12.8 %collective-permute-start.1 = (bf16[2,128,768]{2,1,0:T(8,128)(2,1)S(1)}, bf16[2,128,768]{2,1,0:T(8,128)(2,1)S(1)}, u32[]{:S(2)}, u32[]{:S(2)}) collective-permute-start(bf16[2,128,768]{2,1,0:T(8,128)(2,1)S(1)} %slice_bitcast_fusion.refs_27_), channel_id=1, source_target_pairs={{10,8},{11,9},{26,24},{27,25}} | collective-permute-start | bytes 1179656 | tf_op jit(solution)/shard_map/ppermute | solution.py:313
  7.2 11.5 %collective-permute-start.2 = (bf16[2,128,768]{2,1,0:T(8,128)(2,1)S(1)}, bf16[2,128,768]{2,1,0:T(8,128)(2,1)S(1)}, u32[]{:S(2)}, u32[]{:S(2)}) collective-permute-start(bf16[2,128,768]{2,1,0:T(8,128)(2,1)S(1)} %slice_bitcast_fusion.1.refs_1_.refs_0_), channel_id=1, source_target_pairs={{10,12},{11,13},{26,28},{27,29}} | collective-permute-start | bytes 1179656 | tf_op jit(solution)/shard_map/ppermute | solution.py:313
  15.9 9.1 %collective-permute-start.3 = (bf16[2,128,768]{2,1,0:T(8,128)(2,1)S(1)}, bf16[2,128,768]{2,1,0:T(8,128)(2,1)S(1)}, u32[]{:S(2)}, u32[]{:S(2)}) collective-permute-start(bf16[2,128,768]{2,1,0:T(8,128)(2,1)S(1)} %choose.7), channel_id=1, source_target_pairs={{6,4},{10,14},{7,5},{11,15},{22,20},{26,30},{23,21},{27,31}} | collective-permute-start | bytes 1179656 | tf_op jit(solution)/shard_map/ppermute | solution.py:313
  17.3 8.4 %collective-permute-start.4 = (bf16[2,128,768]{2,1,0:T(8,128)(2,1)S(1)}, bf16[2,128,768]{2,1,0:T(8,128)(2,1)S(1)}, u32[]{:S(2)}, u32[]{:S(2)}) collective-permute-start(bf16[2,128,768]{2,1,0:T(8,128)(2,1)S(1)} %front_1_0.14._.refs_0_.refs_25_), channel_id=1, source_target_pairs={{6,2},{7,3},{22,18},{23,19}} | collective-permute-start | bytes 1179656 | tf_op jit(solution)/shard_map/ppermute | solution.py:313
  18.0 7.7 %collective-permute-start.5 = (bf16[2,128,768]{2,1,0:T(8,128)(2,1)S(1)}, bf16[2,128,768]{2,1,0:T(8,128)(2,1)S(1)}, u32[]{:S(2)}, u32[]{:S(2)}) collective-permute-start(bf16[2,128,768]{2,1,0:T(8,128)(2,1)S(1)} %front_1_0.15._.refs_0_.refs_20_), channel_id=1, source_target_pairs={{8,4},{9,5},{24,20},{25,21}} | collective-permute-start | bytes 1179656 | tf_op jit(solution)/shard_map/ppermute | solution.py:313
  25.7 3.5 %collective-permute-start.8 = (bf16[2,128,768]{2,1,0:T(8,128)(2,1)S(1)}, bf16[2,128,768]{2,1,0:T(8,128)(2,1)S(1)}, u32[]{:S(2)}, u32[]{:S(2)}) collective-permute-start(bf16[2,128,768]{2,1,0:T(8,128)(2,1)S(1)} %front_1_0.18._.refs_0_.refs_18_), channel_id=1, source_target_pairs={{4,0},{5,1},{20,16},{21,17}} | collective-permute-start | bytes 1179656 | tf_op jit(solution)/shard_map/ppermute | solution.py:313
  27.1 3.8 %collective-permute-start.9 = (bf16[2,128,768]{2,1,0:T(8,128)(2,1)S(1)}, bf16[2,128,768]{2,1,0:T(8,128)(2,1)S(1)}, u32[]{:S(2)}, u32[]{:S(2)}) collective-permute-start(bf16[2,128,768]{2,1,0:T(8,128)(2,1)S(1)} %front_1_0.17._.refs_23_), channel_id=1, source_target_pairs={{2,14},{3,15},{18,30},{19,31}} | collective-permute-start | bytes 1179656 | tf_op jit(solution)/shard_map/ppermute | solution.py:313
  27.9 3.8 %collective-permute-start.11 = (bf16[2,128,768]{2,1,0:T(8,128)(2,1)S(1)}, bf16[2,128,768]{2,1,0:T(8,128)(2,1)S(1)}, u32[]{:S(2)}, u32[]{:S(2)}) collective-permute-start(bf16[2,128,768]{2,1,0:T(8,128)(2,1)S(1)} %front_1_0.19._.refs_24_), channel_id=1, source_target_pairs={{4,0},{5,1},{20,16},{21,17}} | collective-permute-start | bytes 1179656 | tf_op jit(solution)/shard_map/ppermute | solution.py:313
  29.5 3.6 %collective-permute-start.12 = (bf16[2,128,768]{2,1,0:T(8,128)(2,1)S(1)}, bf16[2,128,768]{2,1,0:T(8,128)(2,1)S(1)}, u32[]{:S(2)}, u32[]{:S(2)}) collective-permute-start(bf16[2,128,768]{2,1,0:T(8,128)(2,1)S(1)} %front_0_0.17._.refs_2_.refs_4_), channel_id=1, source_target_pairs={{2,6},{3,7},{18,22},{19,23}} | collective-permute-start | bytes 1179656 | tf_op jit(solution)/shard_map/ppermute | solution.py:313
  32.5 3.6 %collective-permute-start.16 = (bf16[2,128,768]{2,1,0:T(8,128)(2,1)S(1)}, bf16[2,128,768]{2,1,0:T(8,128)(2,1)S(1)}, u32[]{:S(2)}, u32[]{:S(2)}) collective-permute-start(bf16[2,128,768]{2,1,0:T(8,128)(2,1)S(1)} %collective-permute-done.11.refs_2_), channel_id=1, source_target_pairs={{0,2},{1,3},{16,18},{17,19}} | collective-permute-start | bytes 1179656 | tf_op jit(solution)/shard_map/ppermute | solution.py:313
  33.2 3.6 %collective-permute-start.17 = (bf16[2,128,768]{2,1,0:T(8,128)(2,1)S(1)}, bf16[2,128,768]{2,1,0:T(8,128)(2,1)S(1)}, u32[]{:S(2)}, u32[]{:S(2)}) collective-permute-start(bf16[2,128,768]{2,1,0:T(8,128)(2,1)S(1)} %front_0_0.19._.refs_0_.refs_10_), channel_id=1, source_target_pairs={{0,4},{1,5},{16,20},{17,21}} | collective-permute-start | bytes 1179656 | tf_op jit(solution)/shard_map/ppermute | solution.py:313
  33.9 3.7 %collective-permute-start.18 = (bf16[2,128,768]{2,1,0:T(8,128)(2,1)S(1)}, bf16[2,128,768]{2,1,0:T(8,128)(2,1)S(1)}, u32[]{:S(2)}, u32[]{:S(2)}) collective-permute-start(bf16[2,128,768]{2,1,0:T(8,128)(2,1)S(1)} %front_1_0.21._.refs_22_), channel_id=1, source_target_pairs={{14,12},{15,13},{30,28},{31,29}} | collective-permute-start | bytes 1179656 | tf_op jit(solution)/shard_map/ppermute | solution.py:313
  36.2 3.7 %collective-permute-start.22 = (bf16[2,128,768]{2,1,0:T(8,128)(2,1)S(1)}, bf16[2,128,768]{2,1,0:T(8,128)(2,1)S(1)}, u32[]{:S(2)}, u32[]{:S(2)}) collective-permute-start(bf16[2,128,768]{2,1,0:T(8,128)(2,1)S(1)} %choose.13), channel_id=1, source_target_pairs={{2,14},{6,8},{3,15},{7,9},{18,30},{22,24},{19,31},{23,25}} | collective-permute-start | bytes 1179656 | tf_op jit(solution)/shard_map/ppermute | solution.py:313
  36.9 4.2 %collective-permute-start.21 = (bf16[2,128,768]{2,1,0:T(8,128)(2,1)S(1)}, bf16[2,128,768]{2,1,0:T(8,128)(2,1)S(1)}, u32[]{:S(2)}, u32[]{:S(2)}) collective-permute-start(bf16[2,128,768]{2,1,0:T(8,128)(2,1)S(1)} %choose.12), channel_id=1, source_target_pairs={{4,8},{12,14},{5,9},{13,15},{20,24},{28,30},{21,25},{29,31}} | collective-permute-start | bytes 1179656 | tf_op jit(solution)/shard_map/ppermute | solution.py:313
  37.8 5.0 %collective-permute-start.24 = (bf16[2,128,768]{2,1,0:T(8,128)(2,1)S(1)}, bf16[2,128,768]{2,1,0:T(8,128)(2,1)S(1)}, u32[]{:S(2)}, u32[]{:S(2)}) collective-permute-start(bf16[2,128,768]{2,1,0:T(8,128)(2,1)S(1)} %front_0_0.24._.refs_11_), channel_id=1, source_target_pairs={{2,6},{3,7},{18,22},{19,23}} | collective-permute-start | bytes 1179656 | tf_op jit(solution)/shard_map/ppermute | solution.py:313
  38.4 4.3 %collective-permute-start.23 = (bf16[2,128,768]{2,1,0:T(8,128)(2,1)S(1)}, bf16[2,128,768]{2,1,0:T(8,128)(2,1)S(1)}, u32[]{:S(2)}, u32[]{:S(2)}) collective-permute-start(bf16[2,128,768]{2,1,0:T(8,128)(2,1)S(1)} %front_0_0.23._.refs_5_), channel_id=1, source_target_pairs={{4,6},{5,7},{20,22},{21,23}} | collective-permute-start | bytes 1179656 | tf_op jit(solution)/shard_map/ppermute | solution.py:313
  39.1 3.6 %collective-permute-start.25 = (bf16[2,128,768]{2,1,0:T(8,128)(2,1)S(1)}, bf16[2,128,768]{2,1,0:T(8,128)(2,1)S(1)}, u32[]{:S(2)}, u32[]{:S(2)}) collective-permute-start(bf16[2,128,768]{2,1,0:T(8,128)(2,1)S(1)} %front_0_0.23._.refs_5_), channel_id=1, source_target_pairs={{4,8},{5,9},{20,24},{21,25}} | collective-permute-start | bytes 1179656 | tf_op jit(solution)/shard_map/ppermute | solution.py:313
  39.8 36.7 %collective-permute-start.27 = (bf16[2,128,768]{2,1,0:T(8,128)(2,1)S(1)}, bf16[2,128,768]{2,1,0:T(8,128)(2,1)S(1)}, u32[]{:S(2)}, u32[]{:S(2)}) collective-permute-start(bf16[2,128,768]{2,1,0:T(8,128)(2,1)S(1)} %front_1_0.25._.refs_21_), channel_id=1, source_target_pairs={{12,10},{13,11},{28,26},{29,27}} | collective-permute-start | bytes 1179656 | tf_op jit(solution)/shard_map/ppermute | solution.py:313
  41.4 44.4 %collective-permute-start.28 = (bf16[2,128,768]{2,1,0:T(8,128)(2,1)S(1)}, bf16[2,128,768]{2,1,0:T(8,128)(2,1)S(1)}, u32[]{:S(2)}, u32[]{:S(2)}) collective-permute-start(bf16[2,128,768]{2,1,0:T(8,128)(2,1)S(1)} %front_1_0.26._.refs_15_), channel_id=1, source_target_pairs={{14,10},{15,11},{30,26},{31,27}} | collective-permute-start | bytes 1179656 | tf_op jit(solution)/shard_map/ppermute | solution.py:313
  42.8 52.3 %collective-permute-start.29 = (bf16[2,128,768]{2,1,0:T(8,128)(2,1)S(1)}, bf16[2,128,768]{2,1,0:T(8,128)(2,1)S(1)}, u32[]{:S(2)}, u32[]{:S(2)}) collective-permute-start(bf16[2,128,768]{2,1,0:T(8,128)(2,1)S(1)} %front_0_0.26.refs_7_._), channel_id=1, source_target_pairs={{8,10},{9,11},{24,26},{25,27}} | collective-permute-start | bytes 1179656 | tf_op jit(solution)/shard_map/ppermute | solution.py:313
  44.4 50.7 %collective-permute-start.30 = (bf16[2,128,768]{2,1,0:T(8,128)(2,1)S(1)}, bf16[2,128,768]{2,1,0:T(8,128)(2,1)S(1)}, u32[]{:S(2)}, u32[]{:S(2)}) collective-permute-start(bf16[2,128,768]{2,1,0:T(8,128)(2,1)S(1)} %front_0_0.26.refs_7_._), channel_id=1, source_target_pairs={{6,10},{7,11},{22,26},{23,27}} | collective-permute-start | bytes 1179656 | tf_op jit(solution)/shard_map/ppermute | solution.py:313
  52.6 57.5 %collective-permute-start.26 = (bf16[2,2,128,1152]{3,2,1,0:T(8,128)(2,1)S(1)}, bf16[2,2,128,1152]{3,2,1,0:T(8,128)(2,1)S(1)}, u32[]{:S(2)}, u32[]{:S(2)}) collective-permute-start(bf16[2,2,128,1152]{3,2,1,0:T(8,128)(2,1)S(1)} %bitcast.52), channel_id=1, source_target_pairs={{0,1},{1,0},{2,3},{3,2},{4,5},{5,4},{6,7},{7,6},{8,9},{9,8},{10,11... | collective-permute-start | bytes 3538952 | tf_op jit(solution)/shard_map/ppermute | solution.py:437
  98.7 11.3 %collective-permute-start.31 = (bf16[2,1,128,1152]{3,2,1,0:T(8,128)(2,1)S(1)}, bf16[2,1,128,1152]{3,2,1,0:T(8,128)(2,1)S(1)}, u32[]{:S(2)}, u32[]{:S(2)}) collective-permute-start(bf16[2,1,128,1152]{3,2,1,0:T(8,128)(2,1)S(1)} %bitcast.53), channel_id=1, source_target_pairs={{0,1},{1,0},{2,3},{3,2},{4,5},{5,4},{6,7},{7,6},{8,9},{9,8},{10,11... | collective-permute-start | bytes 1769480 | tf_op jit(solution)/shard_map/ppermute | solution.py:437
  (17 other events, 54.1 us)

commit v5 on v4

--- a/solution.py
+++ b/solution.py
@@ -18,62 +18,62 @@
 VMEM_LIMIT = 12 * 1024 * 1024
 CHUNKS_OF_4X4 = 1
 PROGRAM_OF_4X4 = (
+    (0, ((1, 0, 15, 5, 4),)),
     (0, ((1, 0, 15, 5, 3),)),
-    (0, ((1, 0, 15, 5, 4),)),
-    (0, ((0, 0, 0, 5, 6),)),
+    (1, 1, 0, ((14, 4),)),
+    (0, ((0, 0, 0, 5, 7), (1, 0, 14, 4, 2))),
+    (1, 1, 0, ((13, 4),)),
     (1, 1, 0, ((11, 3),)),
-    (0, ((1, 0, 11, 3, 2), (0, 0, 0, 5, 7))),
     (0, ((1, 0, 11, 3, 1),)),
-    (1, 1, 0, ((14, 4),)),
-    (0, ((1, 0, 14, 4, 2),)),
-    (1, 1, 0, ((13, 4),)),
-    (1, 0, 0, ((1, 6),)),
+    (0, ((1, 0, 11, 3, 2),)),
     (1, 0, 0, ((4, 7),)),
     (0, ((1, 0, 13, 4, 2), (0, 0, 4, 7, 1))),
     (1, 1, 0, ((7, 1),)),
     (0, ((1, 0, 7, 1, 0),)),
     (1, 1, 0, ((10, 2),)),
     (0, ((1, 0, 10, 2, 0),)),
+    (0, ((0, 0, 0, 5, 6),)),
     (0, ((1, 0, 7, 1, 7),)),
-    (1, 0, 0, ((2, 6),)),
     (1, 1, 0, ((9, 2),)),
     (0, ((1, 0, 9, 2, 0),)),
-    (0, ((1, 0, 13, 2, 3),)),
     (1, 1, 0, ((6, 0),)),
+    (0, ((0, 0, 4, 1, 0), (1, 0, 6, 0, 6), (1, 0, 13, 2, 3))),
+    (1, 0, 0, ((1, 6), (2, 6))),
     (1, 0, 0, ((8, 1),)),
     (0, ((0, 0, 8, 1, 3),)),
-    (0, ((0, 0, 4, 1, 0), (1, 0, 6, 0, 6), (0, 0, 2, 6, 7))),
     (1, 1, 0, ((3, 7),)),
-    (0, ((0, 0, 1, 6, 0),)),
-    (1, 1, 0, ((12, 3), (5, 0))),
-    (0, ((0, 0, 2, 6, 0), (1, 0, 5, 0, 6), (1, 0, 12, 3, 1), (0, 0, 8, 1, 2))),
-    (0, ((1, 0, 9, 0, 1),)),
+    (0, ((0, 0, 1, 6, 0), (1, 0, 3, 7, 6))),
+    (1, 1, 0, ((5, 0),)),
+    (0, ((1, 0, 5, 0, 6), (0, 0, 2, 6, 7))),
+    (0, ((0, 0, 2, 6, 0),)),
+    (1, 1, 0, ((12, 3),)),
+    (0, ((0, 0, 8, 1, 2), (1, 0, 12, 3, 1))),
     (1, 0, 0, ((12, 3),)),
     (1, 0, 0, ((5, 0),)),
     (0, ((0, 0, 5, 0, 2),)),
-    (0, ((1, 0, 3, 7, 6),)),
+    (0, ((1, 0, 9, 0, 1),)),
     (1, 0, 0, ((3, 7),)),
     (1, 0, 0, ((6, 0),)),
     (0, ((0, 0, 3, 7, 1), (0, 0, 6, 0, 2))),
-    (0, ((0, 0, 6, 0, 1),)),
+    (0, ((0, 0, 6, 0, 1), (0, 0, 12, 3, 4))),
+    (1, 0, 0, ((9, 2),)),
+    (0, ((1, 0, 5, 6, 7),)),
     (1, 1, 0, ((8, 1),)),
-    (0, ((1, 0, 8, 1, 7), (0, 0, 12, 3, 4))),
-    (1, 0, 0, ((9, 2),)),
-    (0, ((1, 0, 5, 6, 7), (0, 0, 9, 2, 4))),
-    (1, 1, 0, ((2, 6),)),
-    (1, 1, 0, ((1, 6),)),
+    (0, ((1, 0, 8, 1, 7), (0, 0, 9, 2, 4))),
     (1, 0, 0, ((10, 2),)),
     (0, ((0, 0, 10, 2, 4),)),
     (0, ((0, 0, 10, 2, 3),)),
     (1, 0, 0, ((7, 1),)),
     (0, ((0, 0, 7, 1, 3),)),
-    (1, 1, 0, ((4, 7),)),
+    (1, 1, 0, ((4, 7), (2, 6))),
     (0, ((1, 0, 4, 7, 5),)),
+    (1, 1, 0, ((1, 6),)),
     (0, ((1, 0, 1, 6, 5),)),
     (1, 0, 0, ((13, 4),)),
-    (1, 0, 0, ((11, 3), (14, 4))),
+    (1, 0, 0, ((14, 4),)),
+    (0, ((0, 0, 14, 4, 5),)),
+    (1, 0, 0, ((11, 3),)),
     (0, ((0, 0, 11, 3, 5),)),
-    (0, ((0, 0, 14, 4, 5),)),
     (1, 1, 0, ((0, 5),)),
     (1, 0, 0, ((15, 5),)),
 )

time: 113 us -> 110 us (0.973)
  waiting for transfers between devices: 48.1 us -> 41 us
  starting transfers between devices: 38.1 us -> 42.5 us
    ppermute x30, waiting for transfers between devices: 46.4 us -> 39.3 us  [sweep(): lax.ppermute(payload, 'sub', sorted(((m[3], m[4]) for m in messages)))]
    ppermute x2, starting transfers between devices: 11.3 us -> 15.7 us  [exchange(): received.append(lax.ppermute(sent[shift - 1], 'freq', ring))]
  transfers between devices with their start and end apart: 32 -> 32, of which waited for: 5 -> 6; matrix products, arithmetic and copies ran while one was open for 1% -> 1% of each run, Pallas kernels for 12% -> 13%
where the time goes in v5:
time: 110 us; the launch traced here: 109 us
  starting transfers between devices  42.5 us (39%)
  waiting for transfers between devices  41 us (37%)
  Pallas kernels  17.9 us (16%)
  local copies, waits for them, and re-layouts  5.16 us (5%)
  matrix products  2.12 us (2%)
    ppermute x30, waiting for transfers between devices, sweep(): lax.ppermute(payload, 'sub', sorted(((m[3], m[4]) for m in messages)))  39.3 us
    ppermute x30, starting transfers between devices, sweep(): lax.ppermute(payload, 'sub', sorted(((m[3], m[4]) for m in messages)))  26.9 us
    ppermute x2, starting transfers between devices, exchange(): received.append(lax.ppermute(sent[shift - 1], 'freq', ring))  15.7 us
    pallas_call x2, Pallas kernels, interior_step(): pl.pallas_call(kernel, out_shape=[jax.ShapeDtypeStruct((freqs, slots, col...  8.9 us
    unnamed x18, local copies, waits for them, and re-layouts  5.1 us
    pallas_call x1, Pallas kernels, image_step(): pl.pallas_call(kernel, out_shape=jax.ShapeDtypeStruct((subs, share, width...  2.71 us
    pallas_call x1, Pallas kernels, transpose_step(): pl.pallas_call(kernel, out_shape=jax.ShapeDtypeStruct(maps.shape, BF16),...  2.47 us
    pallas_call x28, Pallas kernels, compute_step(): pl.pallas_call(kernel, out_shape=[jax.ShapeDtypeStruct(shape, BF16)] * le...  2.21 us
  transfers between devices with their start and end apart: 32, of which 6 were waited for; matrix products, arithmetic and copies ran while one was open for 1% of the time, Pallas kernels for 13%

profile of v5, /device:TPU:21, one launch (start us, length us, event | category | flops | bytes accessed | tf_op | source)
XLA Modules:
  0.0 109.4 jit_solution(5723082696679950817)
XLA Ops:
  0.0 1.4 %shots.1 = bf16[128,64]{1,0:T(8,128)(2,1)} custom-call(s32[1]{0:T(128)} %bitcast._.place_ref, s32[1,64]{1,0:T(1,128)} %bitcast.54), custom_call_target="tpu_custom_call" | custom-call | tf_op jit(solution)/shard_map/shots/pallas_call | solution.py:498
  1.4 1.4 %fusion.7 = bf16[64,2,2,768,2]{3,0,4,2,1:T(8,128)(2,1)S(1)} fusion(bf16[2,2,768,2,128]{4,3,2,1,0:T(2,128)(2,1)S(1)} %copy-done, bf16[128,64]{1,0:T(8,128)(2,1)} %shots.1), kind=kOutput, calls=%fused_computation.5 | convolution fusion | flops 101056512 | bytes 2375680 | tf_op jit(solution)/shard_map/fsxcb,bn->fscnx/dot_general | solution.py:509
  2.9 2.2 %collective-permute-start = (bf16[2,128,768]{2,1,0:T(8,128)(2,1)S(1)}, bf16[2,128,768]{2,1,0:T(8,128)(2,1)S(1)}, u32[]{:S(2)}, u32[]{:S(2)}) collective-permute-start(bf16[2,128,768]{2,1,0:T(8,128)(2,1)S(1)} %slice_bitcast_fusion.refs_28_), channel_id=1, source_target_pairs={{10,8},{11,9},{26,24},{27,25}} | collective-permute-start | bytes 1179656 | tf_op jit(solution)/shard_map/ppermute | solution.py:313
  5.1 1.3 %collective-permute-start.1 = (bf16[2,128,768]{2,1,0:T(8,128)(2,1)S(1)}, bf16[2,128,768]{2,1,0:T(8,128)(2,1)S(1)}, u32[]{:S(2)}, u32[]{:S(2)}) collective-permute-start(bf16[2,128,768]{2,1,0:T(8,128)(2,1)S(1)} %slice_bitcast_fusion.refs_28_), channel_id=1, source_target_pairs={{10,6},{11,7},{26,22},{27,23}} | collective-permute-start | bytes 1179656 | tf_op jit(solution)/shard_map/ppermute | solution.py:313
  6.4 3.7 %copy-done.2 = bf16[2,2,2,768,768]{4,3,2,1,0:T(8,128)(2,1)S(1)} copy-done((bf16[2,2,2,768,768]{4,3,2,1,0:T(8,128)(2,1)S(1)}, bf16[2,2,2,768,768]{4,3,2,1,0:T(8,128)(2,1)}, u32[]{:S(2)}) %copy-start.2) | copy-done | bytes 9437208
  10.1 2.5 %transpose.9._.maps_ref = bf16[2,2,2,768,768]{4,3,2,1,0:T(8,128)(2,1)S(1)} custom-call(bf16[2,2,2,768,768]{4,3,2,1,0:T(8,128)(2,1)S(1)} %copy-done.2), custom_call_target="tpu_custom_call" | custom-call | tf_op jit(solution)/shard_map/transpose/pallas_call | solution.py:174
  13.3 0.9 copy-done.3
  14.3 1.3 %collective-permute-start.2 = (bf16[2,128,768]{2,1,0:T(8,128)(2,1)S(1)}, bf16[2,128,768]{2,1,0:T(8,128)(2,1)S(1)}, u32[]{:S(2)}, u32[]{:S(2)}) collective-permute-start(bf16[2,128,768]{2,1,0:T(8,128)(2,1)S(1)} %choose.9), channel_id=1, source_target_pairs={{8,4},{10,14},{9,5},{11,15},{24,20},{26,30},{25,21},{27,31}} | collective-permute-start | bytes 1179656 | tf_op jit(solution)/shard_map/ppermute | solution.py:313
  17.1 6.3 %collective-permute-done.2.refs_0_.refs_1_ = bf16[2,128,768]{2,1,0:T(8,128)(2,1)S(1)} collective-permute-done((bf16[2,128,768]{2,1,0:T(8,128)(2,1)S(1)}, bf16[2,128,768]{2,1,0:T(8,128)(2,1)S(1)}, u32[]{:S(2)}, u32[]{:S(2)}) %collective-permute-start.2) | collective-permute-done | bytes 393248 | tf_op jit(solution)/shard_map/ppermute | solution.py:313
  25.5 1.3 %collective-permute-start.8 = (bf16[2,128,768]{2,1,0:T(8,128)(2,1)S(1)}, bf16[2,128,768]{2,1,0:T(8,128)(2,1)S(1)}, u32[]{:S(2)}, u32[]{:S(2)}) collective-permute-start(bf16[2,128,768]{2,1,0:T(8,128)(2,1)S(1)} %slice_bitcast_fusion.1.refs_0_), channel_id=1, source_target_pairs={{10,12},{11,13},{26,28},{27,29}} | collective-permute-start | bytes 1179656 | tf_op jit(solution)/shard_map/ppermute | solution.py:313
  29.0 4.9 %collective-permute-done.8.refs_0_ = bf16[2,128,768]{2,1,0:T(8,128)(2,1)S(1)} collective-permute-done((bf16[2,128,768]{2,1,0:T(8,128)(2,1)S(1)}, bf16[2,128,768]{2,1,0:T(8,128)(2,1)S(1)}, u32[]{:S(2)}, u32[]{:S(2)}) %collective-permute-start.8) | collective-permute-done | bytes 393248 | tf_op jit(solution)/shard_map/ppermute | solution.py:313
  44.2 1.3 %collective-permute-start.28 = (bf16[2,128,768]{2,1,0:T(8,128)(2,1)S(1)}, bf16[2,128,768]{2,1,0:T(8,128)(2,1)S(1)}, u32[]{:S(2)}, u32[]{:S(2)}) collective-permute-start(bf16[2,128,768]{2,1,0:T(8,128)(2,1)S(1)} %front_1_0.25._.refs_0_.refs_15_), channel_id=1, source_target_pairs={{14,10},{15,11},{30,26},{31,27}} | collective-permute-start | bytes 1179656 | tf_op jit(solution)/shard_map/ppermute | solution.py:313
  45.8 1.3 %collective-permute-start.27 = (bf16[2,128,768]{2,1,0:T(8,128)(2,1)S(1)}, bf16[2,128,768]{2,1,0:T(8,128)(2,1)S(1)}, u32[]{:S(2)}, u32[]{:S(2)}) collective-permute-start(bf16[2,128,768]{2,1,0:T(8,128)(2,1)S(1)} %front_1_0.26._.refs_21_), channel_id=1, source_target_pairs={{12,10},{13,11},{28,26},{29,27}} | collective-permute-start | bytes 1179656 | tf_op jit(solution)/shard_map/ppermute | solution.py:313
  47.2 1.6 %collective-permute-start.29 = (bf16[2,128,768]{2,1,0:T(8,128)(2,1)S(1)}, bf16[2,128,768]{2,1,0:T(8,128)(2,1)S(1)}, u32[]{:S(2)}, u32[]{:S(2)}) collective-permute-start(bf16[2,128,768]{2,1,0:T(8,128)(2,1)S(1)} %front_0_0.25._.refs_7_), channel_id=1, source_target_pairs={{8,10},{9,11},{24,26},{25,27}} | collective-permute-start | bytes 1179656 | tf_op jit(solution)/shard_map/ppermute | solution.py:313
  48.8 1.6 %collective-permute-start.30 = (bf16[2,128,768]{2,1,0:T(8,128)(2,1)S(1)}, bf16[2,128,768]{2,1,0:T(8,128)(2,1)S(1)}, u32[]{:S(2)}, u32[]{:S(2)}) collective-permute-start(bf16[2,128,768]{2,1,0:T(8,128)(2,1)S(1)} %front_0_0.26.refs_13_._), channel_id=1, source_target_pairs={{6,10},{7,11},{22,26},{23,27}} | collective-permute-start | bytes 1179656 | tf_op jit(solution)/shard_map/ppermute | solution.py:313
  50.8 6.2 %interior.1 = (bf16[2,2,128,384]{3,2,1,0:T(8,128)(2,1)S(1)}, bf16[2,2,128,768]{3,2,1,0:T(8,128)(2,1)S(1)}, bf16[1,2,2,128,1152]{4,3,2,1,0:T(8,128)(2,1)S(1)}) custom-call(s32[1]{0:T(128)} %bitcast._.place_ref, bf16[2,2,2,768,768]{4,3,2,1,0:T(8,128)(2,1)S(1)} %bitcast.51, bf16[2,128,768]{2,1,0:T(8,128)(2,1)S(1)} %slice_bitcast_fusion.1.refs_0_, ...), custom_call_target="tpu_custom_call" | custom-call | flops 2415919104 | bytes 16777216 | tf_op jit(solution)/shard_map/interior/pallas_call | solution.py:415
  57.0 10.7 %collective-permute-start.26 = (bf16[2,2,128,1152]{3,2,1,0:T(8,128)(2,1)S(1)}, bf16[2,2,128,1152]{3,2,1,0:T(8,128)(2,1)S(1)}, u32[]{:S(2)}, u32[]{:S(2)}) collective-permute-start(bf16[2,2,128,1152]{3,2,1,0:T(8,128)(2,1)S(1)} %bitcast.52), channel_id=1, source_target_pairs={{0,1},{1,0},{2,3},{3,2},{4,5},{5,4},{6,7},{7,6},{8,9},{9,8},{10,11... | collective-permute-start | bytes 3538952 | tf_op jit(solution)/shard_map/ppermute | solution.py:437
  67.7 10.9 %collective-permute-done.27.refs_0_ = bf16[2,128,768]{2,1,0:T(8,128)(2,1)S(1)} collective-permute-done((bf16[2,128,768]{2,1,0:T(8,128)(2,1)S(1)}, bf16[2,128,768]{2,1,0:T(8,128)(2,1)S(1)}, u32[]{:S(2)}, u32[]{:S(2)}) %collective-permute-start.27) | collective-permute-done | bytes 393248 | tf_op jit(solution)/shard_map/ppermute | solution.py:313
  78.8 0.8 front_1_0.27._.refs_1_
  79.6 17.0 %collective-permute-done.30.refs_1_ = bf16[2,128,768]{2,1,0:T(8,128)(2,1)S(1)} collective-permute-done((bf16[2,128,768]{2,1,0:T(8,128)(2,1)S(1)}, bf16[2,128,768]{2,1,0:T(8,128)(2,1)S(1)}, u32[]{:S(2)}, u32[]{:S(2)}) %collective-permute-start.30) | collective-permute-done | bytes 393248 | tf_op jit(solution)/shard_map/ppermute | solution.py:313
  97.4 2.7 %interior_last.1 = (bf16[2,1,128,384]{3,2,1,0:T(8,128)(2,1)S(1)}, bf16[2,1,128,768]{3,2,1,0:T(8,128)(2,1)S(1)}, bf16[1,2,1,128,1152]{4,3,2,1,0:T(8,128)(2,1)S(1)}) custom-call(s32[1]{0:T(128)} %bitcast._.place_ref, bf16[2,2,2,768,768]{4,3,2,1,0:T(8,128)(2,1)S(1)} %bitcast.51, bf16[2,128,768]{2,1,0:T(8,128)(2,1)S(1)} %front_0_0.27.refs_0_, ...), custom_call_target="tpu_custom_call" | custom-call | flops 2415919104 | bytes 16777216 | tf_op jit(solution)/shard_map/interior_last/pallas_call | solution.py:415
  100.1 5.0 %collective-permute-start.31 = (bf16[2,1,128,1152]{3,2,1,0:T(8,128)(2,1)S(1)}, bf16[2,1,128,1152]{3,2,1,0:T(8,128)(2,1)S(1)}, u32[]{:S(2)}, u32[]{:S(2)}) collective-permute-start(bf16[2,1,128,1152]{3,2,1,0:T(8,128)(2,1)S(1)} %bitcast.53), channel_id=1, source_target_pairs={{0,1},{1,0},{2,3},{3,2},{4,5},{5,4},{6,7},{7,6},{8,9},{9,8},{10,11... | collective-permute-start | bytes 1769480 | tf_op jit(solution)/shard_map/ppermute | solution.py:437
  105.1 1.6 %collective-permute-done.31.refs_5_ = bf16[2,1,128,1152]{3,2,1,0:T(8,128)(2,1)S(1)} collective-permute-done((bf16[2,1,128,1152]{3,2,1,0:T(8,128)(2,1)S(1)}, bf16[2,1,128,1152]{3,2,1,0:T(8,128)(2,1)S(1)}, u32[]{:S(2)}, u32[]{:S(2)}) %collective-permute-start.31) | collective-permute-done | bytes 589856 | tf_op jit(solution)/shard_map/ppermute | solution.py:437
  106.7 2.7 %image.1 = f32[2,384,768]{2,1,0:T(8,128)} custom-call(s32[1]{0:T(128)} %bitcast._.place_ref, bf16[2,2,128,384]{3,2,1,0:T(8,128)(2,1)S(1)} %get-tuple-element.15.refs_0_, bf16[2,2,128,768]{3,2,1,0:T(8,128)(2,1)S(1)} %get-tuple-element.16.refs_1_, bf16[2,2,128,1152]{3,2,1,0:T(8,128)(2,1)S(1)} %collective-permute-done.26.refs_2_, ...), custom_call_target="tpu_custom_call" | custom-call | tf_op jit(solution)/shard_map/image/pallas_call | solution.py:482
  (105 shorter events, 18.2 us)
Async XLA Ops:
  2.9 10.4 %collective-permute-start = (bf16[2,128,768]{2,1,0:T(8,128)(2,1)S(1)}, bf16[2,128,768]{2,1,0:T(8,128)(2,1)S(1)}, u32[]{:S(2)}, u32[]{:S(2)}) collective-permute-start(bf16[2,128,768]{2,1,0:T(8,128)(2,1)S(1)} %slice_bitcast_fusion.refs_28_), channel_id=1, source_target_pairs={{10,8},{11,9},{26,24},{27,25}} | collective-permute-start | bytes 1179656 | tf_op jit(solution)/shard_map/ppermute | solution.py:313
  5.1 10.6 %collective-permute-start.1 = (bf16[2,128,768]{2,1,0:T(8,128)(2,1)S(1)}, bf16[2,128,768]{2,1,0:T(8,128)(2,1)S(1)}, u32[]{:S(2)}, u32[]{:S(2)}) collective-permute-start(bf16[2,128,768]{2,1,0:T(8,128)(2,1)S(1)} %slice_bitcast_fusion.refs_28_), channel_id=1, source_target_pairs={{10,6},{11,7},{26,22},{27,23}} | collective-permute-start | bytes 1179656 | tf_op jit(solution)/shard_map/ppermute | solution.py:313
  14.3 9.1 %collective-permute-start.2 = (bf16[2,128,768]{2,1,0:T(8,128)(2,1)S(1)}, bf16[2,128,768]{2,1,0:T(8,128)(2,1)S(1)}, u32[]{:S(2)}, u32[]{:S(2)}) collective-permute-start(bf16[2,128,768]{2,1,0:T(8,128)(2,1)S(1)} %choose.9), channel_id=1, source_target_pairs={{8,4},{10,14},{9,5},{11,15},{24,20},{26,30},{25,21},{27,31}} | collective-permute-start | bytes 1179656 | tf_op jit(solution)/shard_map/ppermute | solution.py:313
  15.7 8.4 %collective-permute-start.3 = (bf16[2,128,768]{2,1,0:T(8,128)(2,1)S(1)}, bf16[2,128,768]{2,1,0:T(8,128)(2,1)S(1)}, u32[]{:S(2)}, u32[]{:S(2)}) collective-permute-start(bf16[2,128,768]{2,1,0:T(8,128)(2,1)S(1)} %front_1_0.16._.refs_26_), channel_id=1, source_target_pairs={{6,2},{7,3},{22,18},{23,19}} | collective-permute-start | bytes 1179656 | tf_op jit(solution)/shard_map/ppermute | solution.py:313
  16.4 7.7 %collective-permute-start.4 = (bf16[2,128,768]{2,1,0:T(8,128)(2,1)S(1)}, bf16[2,128,768]{2,1,0:T(8,128)(2,1)S(1)}, u32[]{:S(2)}, u32[]{:S(2)}) collective-permute-start(bf16[2,128,768]{2,1,0:T(8,128)(2,1)S(1)} %front_1_0.16._.refs_26_), channel_id=1, source_target_pairs={{6,4},{7,5},{22,20},{23,21}} | collective-permute-start | bytes 1179656 | tf_op jit(solution)/shard_map/ppermute | solution.py:313
  23.4 4.2 %collective-permute-start.5 = (bf16[2,128,768]{2,1,0:T(8,128)(2,1)S(1)}, bf16[2,128,768]{2,1,0:T(8,128)(2,1)S(1)}, u32[]{:S(2)}, u32[]{:S(2)}) collective-permute-start(bf16[2,128,768]{2,1,0:T(8,128)(2,1)S(1)} %choose.10), channel_id=1, source_target_pairs={{8,4},{14,2},{9,5},{15,3},{24,20},{30,18},{25,21},{31,19}} | collective-permute-start | bytes 1179656 | tf_op jit(solution)/shard_map/ppermute | solution.py:313
  24.1 4.1 %collective-permute-start.7 = (bf16[2,128,768]{2,1,0:T(8,128)(2,1)S(1)}, bf16[2,128,768]{2,1,0:T(8,128)(2,1)S(1)}, u32[]{:S(2)}, u32[]{:S(2)}) collective-permute-start(bf16[2,128,768]{2,1,0:T(8,128)(2,1)S(1)} %front_1_0.18._.refs_0_.refs_18_), channel_id=1, source_target_pairs={{4,0},{5,1},{20,16},{21,17}} | collective-permute-start | bytes 1179656 | tf_op jit(solution)/shard_map/ppermute | solution.py:313
  25.5 8.4 %collective-permute-start.8 = (bf16[2,128,768]{2,1,0:T(8,128)(2,1)S(1)}, bf16[2,128,768]{2,1,0:T(8,128)(2,1)S(1)}, u32[]{:S(2)}, u32[]{:S(2)}) collective-permute-start(bf16[2,128,768]{2,1,0:T(8,128)(2,1)S(1)} %slice_bitcast_fusion.1.refs_0_), channel_id=1, source_target_pairs={{10,12},{11,13},{26,28},{27,29}} | collective-permute-start | bytes 1179656 | tf_op jit(solution)/shard_map/ppermute | solution.py:313
  26.8 7.8 %collective-permute-start.9 = (bf16[2,128,768]{2,1,0:T(8,128)(2,1)S(1)}, bf16[2,128,768]{2,1,0:T(8,128)(2,1)S(1)}, u32[]{:S(2)}, u32[]{:S(2)}) collective-permute-start(bf16[2,128,768]{2,1,0:T(8,128)(2,1)S(1)} %front_1_0.17._.refs_24_), channel_id=1, source_target_pairs={{2,14},{3,15},{18,30},{19,31}} | collective-permute-start | bytes 1179656 | tf_op jit(solution)/shard_map/ppermute | solution.py:313
  27.5 7.8 %collective-permute-start.10 = (bf16[2,128,768]{2,1,0:T(8,128)(2,1)S(1)}, bf16[2,128,768]{2,1,0:T(8,128)(2,1)S(1)}, u32[]{:S(2)}, u32[]{:S(2)}) collective-permute-start(bf16[2,128,768]{2,1,0:T(8,128)(2,1)S(1)} %front_1_0.19._.refs_25_), channel_id=1, source_target_pairs={{4,0},{5,1},{20,16},{21,17}} | collective-permute-start | bytes 1179656 | tf_op jit(solution)/shard_map/ppermute | solution.py:313
  28.3 8.5 %collective-permute-start.11 = (bf16[2,128,768]{2,1,0:T(8,128)(2,1)S(1)}, bf16[2,128,768]{2,1,0:T(8,128)(2,1)S(1)}, u32[]{:S(2)}, u32[]{:S(2)}) collective-permute-start(bf16[2,128,768]{2,1,0:T(8,128)(2,1)S(1)} %choose.11), channel_id=1, source_target_pairs={{0,12},{2,0},{4,6},{1,13},{3,1},{5,7},{16,28},{18,16},{20,22},{17,... | collective-permute-start | bytes 1179656 | tf_op jit(solution)/shard_map/ppermute | solution.py:313
  33.9 3.7 %collective-permute-start.12 = (bf16[2,128,768]{2,1,0:T(8,128)(2,1)S(1)}, bf16[2,128,768]{2,1,0:T(8,128)(2,1)S(1)}, u32[]{:S(2)}, u32[]{:S(2)}) collective-permute-start(bf16[2,128,768]{2,1,0:T(8,128)(2,1)S(1)} %front_0_0.16._.refs_0_.refs_4_), channel_id=1, source_target_pairs={{2,6},{3,7},{18,22},{19,23}} | collective-permute-start | bytes 1179656 | tf_op jit(solution)/shard_map/ppermute | solution.py:313
  35.4 3.6 %collective-permute-start.14 = (bf16[2,128,768]{2,1,0:T(8,128)(2,1)S(1)}, bf16[2,128,768]{2,1,0:T(8,128)(2,1)S(1)}, u32[]{:S(2)}, u32[]{:S(2)}) collective-permute-start(bf16[2,128,768]{2,1,0:T(8,128)(2,1)S(1)} %choose.13), channel_id=1, source_target_pairs={{0,12},{12,14},{1,13},{13,15},{16,28},{28,30},{17,29},{29,31}} | collective-permute-start | bytes 1179656 | tf_op jit(solution)/shard_map/ppermute | solution.py:313
  36.9 3.7 %collective-permute-start.16 = (bf16[2,128,768]{2,1,0:T(8,128)(2,1)S(1)}, bf16[2,128,768]{2,1,0:T(8,128)(2,1)S(1)}, u32[]{:S(2)}, u32[]{:S(2)}) collective-permute-start(bf16[2,128,768]{2,1,0:T(8,128)(2,1)S(1)} %choose.14), channel_id=1, source_target_pairs={{2,4},{6,2},{3,5},{7,3},{18,20},{22,18},{19,21},{23,19}} | collective-permute-start | bytes 1179656 | tf_op jit(solution)/shard_map/ppermute | solution.py:313
  40.7 3.5 %collective-permute-start.22 = (bf16[2,128,768]{2,1,0:T(8,128)(2,1)S(1)}, bf16[2,128,768]{2,1,0:T(8,128)(2,1)S(1)}, u32[]{:S(2)}, u32[]{:S(2)}) collective-permute-start(bf16[2,128,768]{2,1,0:T(8,128)(2,1)S(1)} %choose.17), channel_id=1, source_target_pairs={{2,14},{4,8},{3,15},{5,9},{18,30},{20,24},{19,31},{21,25}} | collective-permute-start | bytes 1179656 | tf_op jit(solution)/shard_map/ppermute | solution.py:313
  42.1 5.0 %collective-permute-start.23 = (bf16[2,128,768]{2,1,0:T(8,128)(2,1)S(1)}, bf16[2,128,768]{2,1,0:T(8,128)(2,1)S(1)}, u32[]{:S(2)}, u32[]{:S(2)}) collective-permute-start(bf16[2,128,768]{2,1,0:T(8,128)(2,1)S(1)} %front_0_0.22._.refs_5_), channel_id=1, source_target_pairs={{4,8},{5,9},{20,24},{21,25}} | collective-permute-start | bytes 1179656 | tf_op jit(solution)/shard_map/ppermute | solution.py:313
  42.8 5.9 %collective-permute-start.25 = (bf16[2,128,768]{2,1,0:T(8,128)(2,1)S(1)}, bf16[2,128,768]{2,1,0:T(8,128)(2,1)S(1)}, u32[]{:S(2)}, u32[]{:S(2)}) collective-permute-start(bf16[2,128,768]{2,1,0:T(8,128)(2,1)S(1)} %front_0_0.23._.refs_11_), channel_id=1, source_target_pairs={{2,6},{3,7},{18,22},{19,23}} | collective-permute-start | bytes 1179656 | tf_op jit(solution)/shard_map/ppermute | solution.py:313
  43.5 5.3 %collective-permute-start.24 = (bf16[2,128,768]{2,1,0:T(8,128)(2,1)S(1)}, bf16[2,128,768]{2,1,0:T(8,128)(2,1)S(1)}, u32[]{:S(2)}, u32[]{:S(2)}) collective-permute-start(bf16[2,128,768]{2,1,0:T(8,128)(2,1)S(1)} %front_0_0.22._.refs_5_), channel_id=1, source_target_pairs={{4,6},{5,7},{20,22},{21,23}} | collective-permute-start | bytes 1179656 | tf_op jit(solution)/shard_map/ppermute | solution.py:313
  44.2 34.5 %collective-permute-start.28 = (bf16[2,128,768]{2,1,0:T(8,128)(2,1)S(1)}, bf16[2,128,768]{2,1,0:T(8,128)(2,1)S(1)}, u32[]{:S(2)}, u32[]{:S(2)}) collective-permute-start(bf16[2,128,768]{2,1,0:T(8,128)(2,1)S(1)} %front_1_0.25._.refs_0_.refs_15_), channel_id=1, source_target_pairs={{14,10},{15,11},{30,26},{31,27}} | collective-permute-start | bytes 1179656 | tf_op jit(solution)/shard_map/ppermute | solution.py:313
  45.8 32.7 %collective-permute-start.27 = (bf16[2,128,768]{2,1,0:T(8,128)(2,1)S(1)}, bf16[2,128,768]{2,1,0:T(8,128)(2,1)S(1)}, u32[]{:S(2)}, u32[]{:S(2)}) collective-permute-start(bf16[2,128,768]{2,1,0:T(8,128)(2,1)S(1)} %front_1_0.26._.refs_21_), channel_id=1, source_target_pairs={{12,10},{13,11},{28,26},{29,27}} | collective-permute-start | bytes 1179656 | tf_op jit(solution)/shard_map/ppermute | solution.py:313
  47.2 49.4 %collective-permute-start.29 = (bf16[2,128,768]{2,1,0:T(8,128)(2,1)S(1)}, bf16[2,128,768]{2,1,0:T(8,128)(2,1)S(1)}, u32[]{:S(2)}, u32[]{:S(2)}) collective-permute-start(bf16[2,128,768]{2,1,0:T(8,128)(2,1)S(1)} %front_0_0.25._.refs_7_), channel_id=1, source_target_pairs={{8,10},{9,11},{24,26},{25,27}} | collective-permute-start | bytes 1179656 | tf_op jit(solution)/shard_map/ppermute | solution.py:313
  48.8 47.8 %collective-permute-start.30 = (bf16[2,128,768]{2,1,0:T(8,128)(2,1)S(1)}, bf16[2,128,768]{2,1,0:T(8,128)(2,1)S(1)}, u32[]{:S(2)}, u32[]{:S(2)}) collective-permute-start(bf16[2,128,768]{2,1,0:T(8,128)(2,1)S(1)} %front_0_0.26.refs_13_._), channel_id=1, source_target_pairs={{6,10},{7,11},{22,26},{23,27}} | collective-permute-start | bytes 1179656 | tf_op jit(solution)/shard_map/ppermute | solution.py:313
  57.0 49.7 %collective-permute-start.26 = (bf16[2,2,128,1152]{3,2,1,0:T(8,128)(2,1)S(1)}, bf16[2,2,128,1152]{3,2,1,0:T(8,128)(2,1)S(1)}, u32[]{:S(2)}, u32[]{:S(2)}) collective-permute-start(bf16[2,2,128,1152]{3,2,1,0:T(8,128)(2,1)S(1)} %bitcast.52), channel_id=1, source_target_pairs={{0,1},{1,0},{2,3},{3,2},{4,5},{5,4},{6,7},{7,6},{8,9},{9,8},{10,11... | collective-permute-start | bytes 3538952 | tf_op jit(solution)/shard_map/ppermute | solution.py:437
  100.1 6.6 %collective-permute-start.31 = (bf16[2,1,128,1152]{3,2,1,0:T(8,128)(2,1)S(1)}, bf16[2,1,128,1152]{3,2,1,0:T(8,128)(2,1)S(1)}, u32[]{:S(2)}, u32[]{:S(2)}) collective-permute-start(bf16[2,1,128,1152]{3,2,1,0:T(8,128)(2,1)S(1)} %bitcast.53), channel_id=1, source_target_pairs={{0,1},{1,0},{2,3},{3,2},{4,5},{5,4},{6,7},{7,6},{8,9},{9,8},{10,11... | collective-permute-start | bytes 1769480 | tf_op jit(solution)/shard_map/ppermute | solution.py:437
  (17 other events, 57.8 us)
